TPU v7x, 32 devices: a whole 2x2x4 slice. The times are simulated.
32 devices in a mesh: sub: 8 (over z, y), crs: 4 (over x, core).
Axes of the slice: x: 2, y: 2, z: 4, core: 2. Of those that a mesh axis runs over, the one named last changes fastest.
Arguments:
- dual_ops: bfloat16 [96, 1536, 1536], P('sub', 'crs')
- rigid_traces: float32 [96, 6, 1536], P('sub'), may hold values from -0.625 to 0.625
- coarse_factor: float32 [576, 576], P('sub', 'crs')
- partner: int32 [96, 12], P('sub'), may hold values from -1 to 287, as said below
- send_list: int32 [16, 72], P('sub'), may hold values from -1 to 143, as said below
- mode_count: int32 [96], P('sub'), may hold values from 0 to 6
- dual_rhs: float32 [96, 1536], P('sub'), may hold values from -6 to 6
- rigid_load: float32 [576], P('sub'), may hold values from -2400 to 2400
Outputs:
- multipliers: float32 [96, 1536], P('sub')
- projected_residual: float32 [96, 1536], P('sub')
Inputs may be any that keep to these rules, and one draw needn't show every extreme that they name: For each block of a subdomain (subdomains in order, 12 blocks each): -1 for a padding block, else the position of its partner block in the list made of this index of sub's 12 * 12 blocks in order, then the 72 blocks received from the index before along sub, then the 72 from the index after. Partnership is mutual, never a block with itself, never across more than one index of sub. `send_list`: rows 2i and 2i+1 belong to index i of sub: its local blocks sent to the index before and to the index after, -1 in unused slots; the k-th block received from a neighbour is the k-th entry of that neighbour's row toward this index. The first index sends nothing before and the last nothing after; each boundary between neighbouring indices carries 72 // 2 to 72 blocks, one boundary exactly 72.
All inputs are finite; a program needn't handle non-finite values.
Results may differ from a plain program's by a relative error of at most 0.012.
The roundings to bfloat16 on the way count: a program that leaves them out, or rounds other values in their place, can miss the bound.
Values sent between devices are 32-bit elements; how exact they have to be, the bound alone decides.
No kernel may reach another device: no remote copies, remote signals or barrier semaphores. Data moves between devices by JAX's collectives and lax.ppermute only.
A program may use at most 64 MiB of HBM per device.

v0:
```python
import jax
import jax.numpy as jnp
from jax import lax
from jax.sharding import PartitionSpec as P

ITERATIONS = 2


def with_halo(block, sides, width):
    for axis, dim in sides:
        count = lax.axis_size(axis)
        forward = [(i, i + 1) for i in range(count - 1)]
        backward = [(target, source) for source, target in forward]
        low = lax.ppermute(
            lax.slice_in_dim(block, block.shape[dim] - width, None, axis=dim), axis, forward
        )
        high = lax.ppermute(lax.slice_in_dim(block, 0, width, axis=dim), axis, backward)
        block = jnp.concatenate([low, block, high], axis=dim)
    return block


def local(
    dual_ops, rigid_traces, coarse_factor, partner, send_list, mode_count, dual_rhs, rigid_load
):
    sub_count = dual_ops.shape[0]
    block_num = partner.shape[1]
    order_len = dual_ops.shape[2]
    block_len = order_len // block_num
    local_blocks = sub_count * block_num
    mode_num = rigid_traces.shape[1]
    links = partner.reshape(local_blocks)
    linked = (links >= 0)[:, None]
    source = jnp.maximum(links, 0)
    sending = (send_list >= 0)[:, :, None]
    picked = jnp.maximum(send_list, 0)
    mode_mask = (jnp.arange(mode_num, dtype=jnp.int32)[None, :] < mode_count[:, None]).astype(
        jnp.float32
    )

    def jump(vector):
        pieces = vector.reshape(local_blocks, block_len)
        parcels = jnp.where(sending, pieces[picked], 0.0)
        arrived = with_halo(parcels, (("sub", 0),), 1)
        incoming = jnp.concatenate([arrived[0], arrived[3]], axis=0)
        gathered = jnp.concatenate([pieces, incoming], axis=0)
        return jnp.where(linked, pieces - gathered[source], 0.0).reshape(vector.shape)

    def operator(vector):
        lowered = jump(vector).astype(jnp.bfloat16)
        partial_rows = jnp.einsum(
            "srk,sk->sr", dual_ops, lowered, preferred_element_type=jnp.float32
        )
        full_rows = lax.all_gather(partial_rows, "crs", axis=1, tiled=True)
        return jump(full_rows)

    def restrict(vector):
        traced = (
            jnp.einsum("skm,sm->sk", rigid_traces, jump(vector), precision=lax.Precision.HIGHEST)
            * mode_mask
        )
        return traced.reshape(sub_count * mode_num)

    def expand(coarse_vec):
        scaled = coarse_vec.reshape(sub_count, mode_num) * mode_mask
        spread = jnp.einsum("skm,sk->sm", rigid_traces, scaled, precision=lax.Precision.HIGHEST)
        return jump(spread)

    def coarse(restricted, squares):
        column_part = jnp.dot(restricted, coarse_factor, precision=lax.Precision.HIGHEST)
        column_sum, total_sq = lax.psum((column_part, squares), "sub")
        back_part = jnp.dot(coarse_factor, column_sum, precision=lax.Precision.HIGHEST)
        solved, folded = lax.psum((back_part, jnp.sum(column_sum * column_sum)), "crs")
        return (solved, total_sq, folded)

    def project(residual):
        solved, total_sq, folded = coarse(restrict(residual), jnp.sum(residual * residual))
        projected = residual - expand(solved)
        inner_rw = total_sq - folded
        return (projected, inner_rw)

    start_load = rigid_load * mode_mask.reshape(sub_count * mode_num)
    start_solved, unused_sq, unused_fold = coarse(start_load, jnp.zeros((), jnp.float32))
    multipliers = expand(start_solved)
    residual = dual_rhs - operator(multipliers)
    projected, inner_rw = project(residual)
    direction = projected
    for turn_idx in range(ITERATIONS):
        applied = operator(direction)
        curvature = lax.psum(jnp.sum(direction * applied), "sub")
        step_len = inner_rw / curvature
        multipliers = multipliers + step_len * direction
        residual = residual - step_len * applied
        projected, next_rw = project(residual)
        direction = projected + next_rw / inner_rw * direction
        inner_rw = next_rw
    return (multipliers, projected)


def solution(mesh):
    return jax.shard_map(
        local,
        mesh=mesh,
        in_specs=(
            P("sub", "crs", None),
            P("sub", None, None),
            P("sub", "crs"),
            P("sub", None),
            P("sub", None),
            P("sub"),
            P("sub", None),
            P("sub"),
        ),
        out_specs=(P("sub", None), P("sub", None)),
        check_vma=False,
    )
```

profile of v0, /device:TPU:0, one launch (start us, length us, event | category | flops | bytes accessed | tf_op | source)
XLA Modules:
  0.0 336.7 jit_solution(16830118680887080858)
XLA Ops:
  4.1 23.1 %psum.98 = f32[144]{0:T(256)S(1)} all-reduce(f32[144]{0:T(256)S(1)} %bitcast.205), channel_id=1, replica_groups=mesh['sub'=8,'crs'=4] {'sub'}, use_global_device_ids=true, to_apply=%region_0.0 | all-reduce | flops 144 | bytes 1152 | tf_op jit(solution)/shard_map/psum | solution.py:70
  28.4 5.7 %psum.99 = f32[12,6]{1,0:T(8,128)S(1)} all-reduce(f32[12,6]{1,0:T(8,128)S(1)} %reshape.156), channel_id=1, replica_groups=mesh['sub'=8,'crs'=4] {'crs'}, use_global_device_ids=true, to_apply=%region_1.0 | all-reduce | flops 72 | bytes 576 | tf_op jit(solution)/shard_map/psum | solution.py:72
  40.5 2.9 collective-permute-done.1
  45.0 3.6 %collective-permute-start.2 = (f32[1,72,128]{2,1,0:T(8,128)S(1)}, f32[1,72,128]{2,1,0:T(8,128)S(1)}, u32[]{:S(2)}, u32[]{:S(2)}) collective-permute-start(f32[1,72,128]{2,1,0:T(8,128)S(1)} %get-tuple-element.36), channel_id=1, source_target_pairs={{0,4},{4,8},{8,12},{12,16},{16,20},{20,24},{24,28},{1,5},{5,9},{9,... | collective-permute-start | bytes 110600 | tf_op jit(solution)/shard_map/ppermute | solution.py:14
  50.3 4.2 %collective-permute-done.3 = f32[1,72,128]{2,1,0:T(8,128)S(1)} collective-permute-done((f32[1,72,128]{2,1,0:T(8,128)S(1)}, f32[1,72,128]{2,1,0:T(8,128)S(1)}, u32[]{:S(2)}, u32[]{:S(2)}) %collective-permute-start.3) | collective-permute-done | bytes 36896 | tf_op jit(solution)/shard_map/ppermute | solution.py:17
  55.2 8.8 %fusion.10 = f32[12,1,384]{2,1,0:T(1,128)S(1)} fusion(bf16[12,384,1536]{2,1,0:T(8,128)(2,1)} %param.8, bf16[12,1536,1]{1,0,2:T(8,128)(2,1)S(1)} %fusion.12), kind=kOutput, calls=%fused_computation.77 | convolution fusion | flops 14155776 | bytes 14211072 | tf_op jit(solution)/shard_map/srk,sk->sr/dot_general | solution.py:50
  64.0 5.3 %all_gather.9 = f32[12,1536]{1,0:T(8,128)S(1)} all-gather(f32[12,384]{1,0:T(8,128)S(1)} %bitcast.175), channel_id=1, replica_groups=mesh['sub'=8,'crs'=4] {'crs'}, dimensions={1}, use_global_device_ids=true | all-gather | bytes 92160 | tf_op jit(solution)/shard_map/all_gather | solution.py:53
  74.6 4.2 %collective-permute-done.5 = f32[1,72,128]{2,1,0:T(8,128)S(1)} collective-permute-done((f32[1,72,128]{2,1,0:T(8,128)S(1)}, f32[1,72,128]{2,1,0:T(8,128)S(1)}, u32[]{:S(2)}, u32[]{:S(2)}) %collective-permute-start.5) | collective-permute-done | bytes 36896 | tf_op jit(solution)/shard_map/ppermute | solution.py:17
  85.4 4.2 %collective-permute-done.7 = f32[1,72,128]{2,1,0:T(8,128)S(1)} collective-permute-done((f32[1,72,128]{2,1,0:T(8,128)S(1)}, f32[1,72,128]{2,1,0:T(8,128)S(1)}, u32[]{:S(2)}, u32[]{:S(2)}) %collective-permute-start.7) | collective-permute-done | bytes 36896 | tf_op jit(solution)/shard_map/ppermute | solution.py:17
  92.0 18.2 %psum.101 = f32[144]{0:T(256)S(1)} all-reduce(f32[144]{0:T(256)S(1)} %bitcast.207), channel_id=1, replica_groups=mesh['sub'=8,'crs'=4] {'sub'}, use_global_device_ids=true, to_apply=%region_4.5 | all-reduce | flops 144 | bytes 1152 | tf_op jit(solution)/shard_map/psum | solution.py:70
  111.0 6.5 %all-reduce.3 = (f32[12,6]{1,0:T(8,128)S(1)}, f32[]{:T(128)}) all-reduce(f32[12,6]{1,0:T(8,128)S(1)} %reshape.161, f32[]{:T(128)} %multiply_reduce_fusion.5), channel_id=1, replica_groups=mesh['sub'=8,'crs'=4] {'crs'}, use_global_device_ids=true, to_apply=%region_7.8 | all-reduce | flops 73 | bytes 584 | tf_op jit(solution)/shard_map/psum | solution.py:72
  123.5 4.2 %collective-permute-done.9 = f32[1,72,128]{2,1,0:T(8,128)S(1)} collective-permute-done((f32[1,72,128]{2,1,0:T(8,128)S(1)}, f32[1,72,128]{2,1,0:T(8,128)S(1)}, u32[]{:S(2)}, u32[]{:S(2)}) %collective-permute-start.9) | collective-permute-done | bytes 36896 | tf_op jit(solution)/shard_map/ppermute | solution.py:17
  133.7 4.2 %collective-permute-done.11 = f32[1,72,128]{2,1,0:T(8,128)S(1)} collective-permute-done((f32[1,72,128]{2,1,0:T(8,128)S(1)}, f32[1,72,128]{2,1,0:T(8,128)S(1)}, u32[]{:S(2)}, u32[]{:S(2)}) %collective-permute-start.11) | collective-permute-done | bytes 36896 | tf_op jit(solution)/shard_map/ppermute | solution.py:17
  138.7 8.8 %fusion.6 = f32[12,1,384]{2,1,0:T(1,128)S(1)} fusion(bf16[12,384,1536]{2,1,0:T(8,128)(2,1)} %param.8, bf16[12,1536,1]{1,0,2:T(8,128)(2,1)S(1)} %fusion.13), kind=kOutput, calls=%fused_computation.73 | convolution fusion | flops 14155776 | bytes 14211072 | tf_op jit(solution)/shard_map/srk,sk->sr/dot_general | solution.py:50
  147.4 5.3 %all_gather.10 = f32[12,1536]{1,0:T(8,128)S(1)} all-gather(f32[12,384]{1,0:T(8,128)S(1)} %bitcast.176), channel_id=1, replica_groups=mesh['sub'=8,'crs'=4] {'crs'}, dimensions={1}, use_global_device_ids=true | all-gather | bytes 92160 | tf_op jit(solution)/shard_map/all_gather | solution.py:53
  158.0 4.2 %collective-permute-done.13 = f32[1,72,128]{2,1,0:T(8,128)S(1)} collective-permute-done((f32[1,72,128]{2,1,0:T(8,128)S(1)}, f32[1,72,128]{2,1,0:T(8,128)S(1)}, u32[]{:S(2)}, u32[]{:S(2)}) %collective-permute-start.13) | collective-permute-done | bytes 36896 | tf_op jit(solution)/shard_map/ppermute | solution.py:17
  163.6 19.8 %all-reduce.1 = (f32[]{:T(128)}, f32[]{:T(128)}) all-reduce(f32[]{:T(128)} %get-tuple-element.12, f32[]{:T(128)} %multiply_reduce_fusion.2), channel_id=1, replica_groups=mesh['sub'=8,'crs'=4] {'sub'}, use_global_device_ids=true, to_apply=%region_3.4 | all-reduce | flops 2 | bytes 16 | tf_op jit(solution)/shard_map/psum | solution.py:70
  190.4 4.2 %collective-permute-done.15 = f32[1,72,128]{2,1,0:T(8,128)S(1)} collective-permute-done((f32[1,72,128]{2,1,0:T(8,128)S(1)}, f32[1,72,128]{2,1,0:T(8,128)S(1)}, u32[]{:S(2)}, u32[]{:S(2)}) %collective-permute-start.15) | collective-permute-done | bytes 36896 | tf_op jit(solution)/shard_map/ppermute | solution.py:17
  197.0 18.9 %all-reduce = (f32[144]{0:T(256)S(1)}, f32[]{:T(128)}) all-reduce(f32[144]{0:T(256)S(1)} %bitcast.210, f32[]{:T(128)} %get-tuple-element.10), channel_id=1, replica_groups=mesh['sub'=8,'crs'=4] {'sub'}, use_global_device_ids=true, to_apply=%region_12.13 | all-reduce | flops 145 | bytes 1160 | tf_op jit(solution)/shard_map/psum | solution.py:70
  216.7 6.7 %all-reduce.2 = (f32[12,6]{1,0:T(8,128)S(1)}, f32[]{:T(128)}) all-reduce(f32[12,6]{1,0:T(8,128)S(1)} %reshape.167, f32[]{:T(128)} %multiply_reduce_fusion.4), channel_id=1, replica_groups=mesh['sub'=8,'crs'=4] {'crs'}, use_global_device_ids=true, to_apply=%region_15.16 | all-reduce | flops 73 | bytes 584 | tf_op jit(solution)/shard_map/psum | solution.py:72
  230.4 3.2 collective-permute-done.17
  239.5 4.2 %collective-permute-done.19 = f32[1,72,128]{2,1,0:T(8,128)S(1)} collective-permute-done((f32[1,72,128]{2,1,0:T(8,128)S(1)}, f32[1,72,128]{2,1,0:T(8,128)S(1)}, u32[]{:S(2)}, u32[]{:S(2)}) %collective-permute-start.19) | collective-permute-done | bytes 36896 | tf_op jit(solution)/shard_map/ppermute | solution.py:17
  244.5 8.8 %fusion.2 = f32[12,1,384]{2,1,0:T(1,128)S(1)} fusion(bf16[12,384,1536]{2,1,0:T(8,128)(2,1)} %param.8, bf16[12,1536,1]{1,0,2:T(8,128)(2,1)S(1)} %fusion.14), kind=kOutput, calls=%fused_computation.69 | convolution fusion | flops 14155776 | bytes 14211072 | tf_op jit(solution)/shard_map/srk,sk->sr/dot_general | solution.py:50
  253.3 5.3 %all_gather.11 = f32[12,1536]{1,0:T(8,128)S(1)} all-gather(f32[12,384]{1,0:T(8,128)S(1)} %bitcast.177), channel_id=1, replica_groups=mesh['sub'=8,'crs'=4] {'crs'}, dimensions={1}, use_global_device_ids=true | all-gather | bytes 92160 | tf_op jit(solution)/shard_map/all_gather | solution.py:53
  263.8 4.2 %collective-permute-done.21 = f32[1,72,128]{2,1,0:T(8,128)S(1)} collective-permute-done((f32[1,72,128]{2,1,0:T(8,128)S(1)}, f32[1,72,128]{2,1,0:T(8,128)S(1)}, u32[]{:S(2)}, u32[]{:S(2)}) %collective-permute-start.21) | collective-permute-done | bytes 36896 | tf_op jit(solution)/shard_map/ppermute | solution.py:17
  269.4 18.6 %psum.109 = f32[]{:T(128)} all-reduce(f32[]{:T(128)} %multiply_reduce_fusion), channel_id=1, replica_groups=mesh['sub'=8,'crs'=4] {'sub'}, use_global_device_ids=true, to_apply=%region_17.18 | all-reduce | flops 1 | bytes 8 | tf_op jit(solution)/shard_map/psum | solution.py:89
  289.6 3.0 collective-permute-start.22
  294.2 4.3 %collective-permute-done.23 = f32[1,72,128]{2,1,0:T(8,128)S(1)} collective-permute-done((f32[1,72,128]{2,1,0:T(8,128)S(1)}, f32[1,72,128]{2,1,0:T(8,128)S(1)}, u32[]{:S(2)}, u32[]{:S(2)}) %collective-permute-start.23) | collective-permute-done | bytes 36896 | tf_op jit(solution)/shard_map/ppermute | solution.py:17
  300.8 18.0 %psum.110 = f32[144]{0:T(256)S(1)} all-reduce(f32[144]{0:T(256)S(1)} %bitcast.208), channel_id=1, replica_groups=mesh['sub'=8,'crs'=4] {'sub'}, use_global_device_ids=true, to_apply=%region_18.19 | all-reduce | flops 144 | bytes 1152 | tf_op jit(solution)/shard_map/psum | solution.py:70
  319.1 5.8 %psum.111 = f32[12,6]{1,0:T(8,128)S(1)} all-reduce(f32[12,6]{1,0:T(8,128)S(1)} %reshape.173), channel_id=1, replica_groups=mesh['sub'=8,'crs'=4] {'crs'}, use_global_device_ids=true, to_apply=%region_19.20 | all-reduce | flops 72 | bytes 576 | tf_op jit(solution)/shard_map/psum | solution.py:72
  326.4 3.1 collective-permute-start.24
  331.0 4.2 %collective-permute-done.25 = f32[1,72,128]{2,1,0:T(8,128)S(1)} collective-permute-done((f32[1,72,128]{2,1,0:T(8,128)S(1)}, f32[1,72,128]{2,1,0:T(8,128)S(1)}, u32[]{:S(2)}, u32[]{:S(2)}) %collective-permute-start.25) | collective-permute-done | bytes 36896 | tf_op jit(solution)/shard_map/ppermute | solution.py:17
  (201 shorter events, 84.9 us)
Async XLA Ops:
  0.6 34.2 %copy-start = (f32[12,6,1536]{2,1,0:T(8,128)S(1)}, f32[12,6,1536]{2,1,0:T(8,128)}, u32[]{:S(2)}) copy-start(f32[12,6,1536]{2,1,0:T(8,128)} %param.9) | copy-start | bytes 1327108
  0.6 91.0 %copy-start.3 = (s32[12]{0:T(128)S(1)}, s32[12]{0:T(128)}, u32[]{:S(2)}) copy-start(s32[12]{0:T(128)} %param.13) | copy-start | bytes 148
  0.7 91.2 %copy-start.1 = (f32[72,144]{1,0:T(8,128)S(1)}, f32[72,144]{1,0:T(8,128)}, u32[]{:S(2)}) copy-start(f32[72,144]{1,0:T(8,128)} %param.10) | copy-start | bytes 124420
  0.7 78.8 %copy-start.2 = (f32[12,1536]{1,0:T(8,128)S(1)}, f32[12,1536]{1,0:T(8,128)}, u32[]{:S(2)}) copy-start(f32[12,1536]{1,0:T(8,128)} %param.14) | copy-start | bytes 221188
  36.3 4.2 %collective-permute-start = (f32[1,72,128]{2,1,0:T(8,128)S(1)}, f32[1,72,128]{2,1,0:T(8,128)S(1)}, u32[]{:S(2)}, u32[]{:S(2)}) collective-permute-start(f32[1,72,128]{2,1,0:T(8,128)S(1)} %get-tuple-element.38), channel_id=1, source_target_pairs={{0,4},{4,8},{8,12},{12,16},{16,20},{20,24},{24,28},{1,5},{5,9},{9,... | collective-permute-start | bytes 110600 | tf_op jit(solution)/shard_map/ppermute | solution.py:14
  37.6 5.9 %collective-permute-start.1 = (f32[1,72,128]{2,1,0:T(8,128)S(1)}, f32[1,72,128]{2,1,0:T(8,128)S(1)}, u32[]{:S(2)}, u32[]{:S(2)}) collective-permute-start(f32[1,72,128]{2,1,0:T(8,128)S(1)} %get-tuple-element.39), channel_id=1, source_target_pairs={{4,0},{8,4},{12,8},{16,12},{20,16},{24,20},{28,24},{5,1},{9,5},{13... | collective-permute-start | bytes 110600 | tf_op jit(solution)/shard_map/ppermute | solution.py:17
  45.0 5.3 %collective-permute-start.2 = (f32[1,72,128]{2,1,0:T(8,128)S(1)}, f32[1,72,128]{2,1,0:T(8,128)S(1)}, u32[]{:S(2)}, u32[]{:S(2)}) collective-permute-start(f32[1,72,128]{2,1,0:T(8,128)S(1)} %get-tuple-element.36), channel_id=1, source_target_pairs={{0,4},{4,8},{8,12},{12,16},{16,20},{20,24},{24,28},{1,5},{5,9},{9,... | collective-permute-start | bytes 110600 | tf_op jit(solution)/shard_map/ppermute | solution.py:14
  48.6 5.9 %collective-permute-start.3 = (f32[1,72,128]{2,1,0:T(8,128)S(1)}, f32[1,72,128]{2,1,0:T(8,128)S(1)}, u32[]{:S(2)}, u32[]{:S(2)}) collective-permute-start(f32[1,72,128]{2,1,0:T(8,128)S(1)} %get-tuple-element.37), channel_id=1, source_target_pairs={{4,0},{8,4},{12,8},{16,12},{20,16},{24,20},{28,24},{5,1},{9,5},{13... | collective-permute-start | bytes 110600 | tf_op jit(solution)/shard_map/ppermute | solution.py:17
  70.1 4.4 %collective-permute-start.4 = (f32[1,72,128]{2,1,0:T(8,128)S(1)}, f32[1,72,128]{2,1,0:T(8,128)S(1)}, u32[]{:S(2)}, u32[]{:S(2)}) collective-permute-start(f32[1,72,128]{2,1,0:T(8,128)S(1)} %get-tuple-element.34), channel_id=1, source_target_pairs={{0,4},{4,8},{8,12},{12,16},{16,20},{20,24},{24,28},{1,5},{5,9},{9,... | collective-permute-start | bytes 110600 | tf_op jit(solution)/shard_map/ppermute | solution.py:14
  72.9 5.9 %collective-permute-start.5 = (f32[1,72,128]{2,1,0:T(8,128)S(1)}, f32[1,72,128]{2,1,0:T(8,128)S(1)}, u32[]{:S(2)}, u32[]{:S(2)}) collective-permute-start(f32[1,72,128]{2,1,0:T(8,128)S(1)} %get-tuple-element.35), channel_id=1, source_target_pairs={{4,0},{8,4},{12,8},{16,12},{20,16},{24,20},{28,24},{5,1},{9,5},{13... | collective-permute-start | bytes 110600 | tf_op jit(solution)/shard_map/ppermute | solution.py:17
  80.9 4.4 %collective-permute-start.6 = (f32[1,72,128]{2,1,0:T(8,128)S(1)}, f32[1,72,128]{2,1,0:T(8,128)S(1)}, u32[]{:S(2)}, u32[]{:S(2)}) collective-permute-start(f32[1,72,128]{2,1,0:T(8,128)S(1)} %get-tuple-element.32), channel_id=1, source_target_pairs={{0,4},{4,8},{8,12},{12,16},{16,20},{20,24},{24,28},{1,5},{5,9},{9,... | collective-permute-start | bytes 110600 | tf_op jit(solution)/shard_map/ppermute | solution.py:14
  83.7 5.9 %collective-permute-start.7 = (f32[1,72,128]{2,1,0:T(8,128)S(1)}, f32[1,72,128]{2,1,0:T(8,128)S(1)}, u32[]{:S(2)}, u32[]{:S(2)}) collective-permute-start(f32[1,72,128]{2,1,0:T(8,128)S(1)} %get-tuple-element.33), channel_id=1, source_target_pairs={{4,0},{8,4},{12,8},{16,12},{20,16},{24,20},{28,24},{5,1},{9,5},{13... | collective-permute-start | bytes 110600 | tf_op jit(solution)/shard_map/ppermute | solution.py:17
  119.1 4.4 %collective-permute-start.8 = (f32[1,72,128]{2,1,0:T(8,128)S(1)}, f32[1,72,128]{2,1,0:T(8,128)S(1)}, u32[]{:S(2)}, u32[]{:S(2)}) collective-permute-start(f32[1,72,128]{2,1,0:T(8,128)S(1)} %get-tuple-element.30), channel_id=1, source_target_pairs={{0,4},{4,8},{8,12},{12,16},{16,20},{20,24},{24,28},{1,5},{5,9},{9,... | collective-permute-start | bytes 110600 | tf_op jit(solution)/shard_map/ppermute | solution.py:14
  121.9 5.9 %collective-permute-start.9 = (f32[1,72,128]{2,1,0:T(8,128)S(1)}, f32[1,72,128]{2,1,0:T(8,128)S(1)}, u32[]{:S(2)}, u32[]{:S(2)}) collective-permute-start(f32[1,72,128]{2,1,0:T(8,128)S(1)} %get-tuple-element.31), channel_id=1, source_target_pairs={{4,0},{8,4},{12,8},{16,12},{20,16},{24,20},{28,24},{5,1},{9,5},{13... | collective-permute-start | bytes 110600 | tf_op jit(solution)/shard_map/ppermute | solution.py:17
  129.3 4.4 %collective-permute-start.10 = (f32[1,72,128]{2,1,0:T(8,128)S(1)}, f32[1,72,128]{2,1,0:T(8,128)S(1)}, u32[]{:S(2)}, u32[]{:S(2)}) collective-permute-start(f32[1,72,128]{2,1,0:T(8,128)S(1)} %get-tuple-element.28), channel_id=1, source_target_pairs={{0,4},{4,8},{8,12},{12,16},{16,20},{20,24},{24,28},{1,5},{5,9},{9,... | collective-permute-start | bytes 110600 | tf_op jit(solution)/shard_map/ppermute | solution.py:14
  132.1 5.9 %collective-permute-start.11 = (f32[1,72,128]{2,1,0:T(8,128)S(1)}, f32[1,72,128]{2,1,0:T(8,128)S(1)}, u32[]{:S(2)}, u32[]{:S(2)}) collective-permute-start(f32[1,72,128]{2,1,0:T(8,128)S(1)} %get-tuple-element.29), channel_id=1, source_target_pairs={{4,0},{8,4},{12,8},{16,12},{20,16},{24,20},{28,24},{5,1},{9,5},{13... | collective-permute-start | bytes 110600 | tf_op jit(solution)/shard_map/ppermute | solution.py:17
  153.6 4.4 %collective-permute-start.12 = (f32[1,72,128]{2,1,0:T(8,128)S(1)}, f32[1,72,128]{2,1,0:T(8,128)S(1)}, u32[]{:S(2)}, u32[]{:S(2)}) collective-permute-start(f32[1,72,128]{2,1,0:T(8,128)S(1)} %get-tuple-element.26), channel_id=1, source_target_pairs={{0,4},{4,8},{8,12},{12,16},{16,20},{20,24},{24,28},{1,5},{5,9},{9,... | collective-permute-start | bytes 110600 | tf_op jit(solution)/shard_map/ppermute | solution.py:14
  156.4 5.9 %collective-permute-start.13 = (f32[1,72,128]{2,1,0:T(8,128)S(1)}, f32[1,72,128]{2,1,0:T(8,128)S(1)}, u32[]{:S(2)}, u32[]{:S(2)}) collective-permute-start(f32[1,72,128]{2,1,0:T(8,128)S(1)} %get-tuple-element.27), channel_id=1, source_target_pairs={{4,0},{8,4},{12,8},{16,12},{20,16},{24,20},{28,24},{5,1},{9,5},{13... | collective-permute-start | bytes 110600 | tf_op jit(solution)/shard_map/ppermute | solution.py:17
  186.8 3.5 %collective-permute-start.14 = (f32[1,72,128]{2,1,0:T(8,128)S(1)}, f32[1,72,128]{2,1,0:T(8,128)S(1)}, u32[]{:S(2)}, u32[]{:S(2)}) collective-permute-start(f32[1,72,128]{2,1,0:T(8,128)S(1)} %get-tuple-element.24), channel_id=1, source_target_pairs={{0,4},{4,8},{8,12},{12,16},{16,20},{20,24},{24,28},{1,5},{5,9},{9,... | collective-permute-start | bytes 110600 | tf_op jit(solution)/shard_map/ppermute | solution.py:14
  188.8 5.9 %collective-permute-start.15 = (f32[1,72,128]{2,1,0:T(8,128)S(1)}, f32[1,72,128]{2,1,0:T(8,128)S(1)}, u32[]{:S(2)}, u32[]{:S(2)}) collective-permute-start(f32[1,72,128]{2,1,0:T(8,128)S(1)} %get-tuple-element.25), channel_id=1, source_target_pairs={{4,0},{8,4},{12,8},{16,12},{20,16},{24,20},{28,24},{5,1},{9,5},{13... | collective-permute-start | bytes 110600 | tf_op jit(solution)/shard_map/ppermute | solution.py:17
  224.9 5.5 %collective-permute-start.16 = (f32[1,72,128]{2,1,0:T(8,128)S(1)}, f32[1,72,128]{2,1,0:T(8,128)S(1)}, u32[]{:S(2)}, u32[]{:S(2)}) collective-permute-start(f32[1,72,128]{2,1,0:T(8,128)S(1)} %get-tuple-element.22), channel_id=1, source_target_pairs={{0,4},{4,8},{8,12},{12,16},{16,20},{20,24},{24,28},{1,5},{5,9},{9,... | collective-permute-start | bytes 110600 | tf_op jit(solution)/shard_map/ppermute | solution.py:14
  227.7 5.9 %collective-permute-start.17 = (f32[1,72,128]{2,1,0:T(8,128)S(1)}, f32[1,72,128]{2,1,0:T(8,128)S(1)}, u32[]{:S(2)}, u32[]{:S(2)}) collective-permute-start(f32[1,72,128]{2,1,0:T(8,128)S(1)} %get-tuple-element.23), channel_id=1, source_target_pairs={{4,0},{8,4},{12,8},{16,12},{20,16},{24,20},{28,24},{5,1},{9,5},{13... | collective-permute-start | bytes 110600 | tf_op jit(solution)/shard_map/ppermute | solution.py:17
  235.1 4.4 %collective-permute-start.18 = (f32[1,72,128]{2,1,0:T(8,128)S(1)}, f32[1,72,128]{2,1,0:T(8,128)S(1)}, u32[]{:S(2)}, u32[]{:S(2)}) collective-permute-start(f32[1,72,128]{2,1,0:T(8,128)S(1)} %get-tuple-element.20), channel_id=1, source_target_pairs={{0,4},{4,8},{8,12},{12,16},{16,20},{20,24},{24,28},{1,5},{5,9},{9,... | collective-permute-start | bytes 110600 | tf_op jit(solution)/shard_map/ppermute | solution.py:14
  237.9 5.9 %collective-permute-start.19 = (f32[1,72,128]{2,1,0:T(8,128)S(1)}, f32[1,72,128]{2,1,0:T(8,128)S(1)}, u32[]{:S(2)}, u32[]{:S(2)}) collective-permute-start(f32[1,72,128]{2,1,0:T(8,128)S(1)} %get-tuple-element.21), channel_id=1, source_target_pairs={{4,0},{8,4},{12,8},{16,12},{20,16},{24,20},{28,24},{5,1},{9,5},{13... | collective-permute-start | bytes 110600 | tf_op jit(solution)/shard_map/ppermute | solution.py:17
  259.4 4.4 %collective-permute-start.20 = (f32[1,72,128]{2,1,0:T(8,128)S(1)}, f32[1,72,128]{2,1,0:T(8,128)S(1)}, u32[]{:S(2)}, u32[]{:S(2)}) collective-permute-start(f32[1,72,128]{2,1,0:T(8,128)S(1)} %get-tuple-element.18), channel_id=1, source_target_pairs={{0,4},{4,8},{8,12},{12,16},{16,20},{20,24},{24,28},{1,5},{5,9},{9,... | collective-permute-start | bytes 110600 | tf_op jit(solution)/shard_map/ppermute | solution.py:14
  262.2 5.9 %collective-permute-start.21 = (f32[1,72,128]{2,1,0:T(8,128)S(1)}, f32[1,72,128]{2,1,0:T(8,128)S(1)}, u32[]{:S(2)}, u32[]{:S(2)}) collective-permute-start(f32[1,72,128]{2,1,0:T(8,128)S(1)} %get-tuple-element.19), channel_id=1, source_target_pairs={{4,0},{8,4},{12,8},{16,12},{20,16},{24,20},{28,24},{5,1},{9,5},{13... | collective-permute-start | bytes 110600 | tf_op jit(solution)/shard_map/ppermute | solution.py:17
  289.6 4.6 %collective-permute-start.22 = (f32[1,72,128]{2,1,0:T(8,128)S(1)}, f32[1,72,128]{2,1,0:T(8,128)S(1)}, u32[]{:S(2)}, u32[]{:S(2)}) collective-permute-start(f32[1,72,128]{2,1,0:T(8,128)S(1)} %get-tuple-element.16), channel_id=1, source_target_pairs={{0,4},{4,8},{8,12},{12,16},{16,20},{20,24},{24,28},{1,5},{5,9},{9,... | collective-permute-start | bytes 110600 | tf_op jit(solution)/shard_map/ppermute | solution.py:14
  292.6 5.9 %collective-permute-start.23 = (f32[1,72,128]{2,1,0:T(8,128)S(1)}, f32[1,72,128]{2,1,0:T(8,128)S(1)}, u32[]{:S(2)}, u32[]{:S(2)}) collective-permute-start(f32[1,72,128]{2,1,0:T(8,128)S(1)} %get-tuple-element.17), channel_id=1, source_target_pairs={{4,0},{8,4},{12,8},{16,12},{20,16},{24,20},{28,24},{5,1},{9,5},{13... | collective-permute-start | bytes 110600 | tf_op jit(solution)/shard_map/ppermute | solution.py:17
  326.4 4.7 %collective-permute-start.24 = (f32[1,72,128]{2,1,0:T(8,128)S(1)}, f32[1,72,128]{2,1,0:T(8,128)S(1)}, u32[]{:S(2)}, u32[]{:S(2)}) collective-permute-start(f32[1,72,128]{2,1,0:T(8,128)S(1)} %get-tuple-element.14), channel_id=1, source_target_pairs={{0,4},{4,8},{8,12},{12,16},{16,20},{20,24},{24,28},{1,5},{5,9},{9,... | collective-permute-start | bytes 110600 | tf_op jit(solution)/shard_map/ppermute | solution.py:14
  329.4 5.9 %collective-permute-start.25 = (f32[1,72,128]{2,1,0:T(8,128)S(1)}, f32[1,72,128]{2,1,0:T(8,128)S(1)}, u32[]{:S(2)}, u32[]{:S(2)}) collective-permute-start(f32[1,72,128]{2,1,0:T(8,128)S(1)} %get-tuple-element.15), channel_id=1, source_target_pairs={{4,0},{8,4},{12,8},{16,12},{20,16},{24,20},{28,24},{5,1},{9,5},{13... | collective-permute-start | bytes 110600 | tf_op jit(solution)/shard_map/ppermute | solution.py:17
where the time goes:
time: 338 us; the launch traced here: 337 us
  blocking collectives  157 us (46%)
  waiting for transfers between devices  56.1 us (17%)
  starting transfers between devices  52.2 us (15%)
  matrix products  35.6 us (11%)
  local copies, waits for them, and re-layouts  18.9 us (6%)
  other arithmetic  10.8 us (3%)
  between operations  5.57 us (2%)
    psum x5, blocking collectives, coarse(): column_sum, total_sq = lax.psum((column_part, squares), 'sub')  98 us
    ppermute x13, waiting for transfers between devices, with_halo(): lax.ppermute(lax.slice_in_dim(block, 0, width, axis=dim), axis, backward)  52.8 us
    ppermute x13, starting transfers between devices, with_halo(): lax.ppermute(lax.slice_in_dim(block, block.shape[dim] - width, None, axis...  35.5 us
    dot_general x3, matrix products, operator(): jnp.einsum('srk,sk->sr', dual_ops, lowered, preferred_element_type=jnp.fl...  26.3 us
    psum x4, blocking collectives, coarse(): lax.psum((back_part, jnp.sum(column_sum * column_sum)), 'crs')  24.8 us
    psum x1, blocking collectives, local(): curvature = lax.psum(jnp.sum(direction * applied), 'sub')  18.6 us
    ppermute x13, starting transfers between devices, with_halo(): lax.ppermute(lax.slice_in_dim(block, 0, width, axis=dim), axis, backward)  16.8 us
    all_gather x3, blocking collectives, operator(): full_rows = lax.all_gather(partial_rows, 'crs', axis=1, tiled=True)  16 us
  transfers between devices with their start and end apart: 26, of which 24 were waited for; matrix products, arithmetic and copies ran while one was open for 1% of the time, Pallas kernels for 0%

commit v1 on v0

--- a/solution.py
+++ b/solution.py
@@ -1,9 +1,17 @@
+import functools
+
 import jax
 import jax.numpy as jnp
 from jax import lax
+from jax.experimental import pallas as pl
+from jax.experimental.pallas import tpu as pltpu
 from jax.sharding import PartitionSpec as P
 
 ITERATIONS = 2
+AXES = ("sub", "crs")
+LANES = 128
+F32 = jnp.float32
+BF16 = jnp.bfloat16
 
 
 def with_halo(block, sides, width):
@@ -19,7 +27,7 @@
     return block
 
 
-def local(
+def plain(
     dual_ops, rigid_traces, coarse_factor, partner, send_list, mode_count, dual_rhs, rigid_load
 ):
     sub_count = dual_ops.shape[0]
@@ -33,9 +41,7 @@
     source = jnp.maximum(links, 0)
     sending = (send_list >= 0)[:, :, None]
     picked = jnp.maximum(send_list, 0)
-    mode_mask = (jnp.arange(mode_num, dtype=jnp.int32)[None, :] < mode_count[:, None]).astype(
-        jnp.float32
-    )
+    mode_mask = (jnp.arange(mode_num, dtype=jnp.int32)[None, :] < mode_count[:, None]).astype(F32)
 
     def jump(vector):
         pieces = vector.reshape(local_blocks, block_len)
@@ -46,19 +52,16 @@
         return jnp.where(linked, pieces - gathered[source], 0.0).reshape(vector.shape)
 
     def operator(vector):
-        lowered = jump(vector).astype(jnp.bfloat16)
-        partial_rows = jnp.einsum(
-            "srk,sk->sr", dual_ops, lowered, preferred_element_type=jnp.float32
-        )
+        lowered = jump(vector).astype(BF16)
+        partial_rows = jnp.einsum("srk,sk->sr", dual_ops, lowered, preferred_element_type=F32)
         full_rows = lax.all_gather(partial_rows, "crs", axis=1, tiled=True)
         return jump(full_rows)
 
     def restrict(vector):
-        traced = (
-            jnp.einsum("skm,sm->sk", rigid_traces, jump(vector), precision=lax.Precision.HIGHEST)
-            * mode_mask
+        traced = jnp.einsum(
+            "skm,sm->sk", rigid_traces, jump(vector), precision=lax.Precision.HIGHEST
         )
-        return traced.reshape(sub_count * mode_num)
+        return (traced * mode_mask).reshape(sub_count * mode_num)
 
     def expand(coarse_vec):
         scaled = coarse_vec.reshape(sub_count, mode_num) * mode_mask
@@ -74,17 +77,15 @@
 
     def project(residual):
         solved, total_sq, folded = coarse(restrict(residual), jnp.sum(residual * residual))
-        projected = residual - expand(solved)
-        inner_rw = total_sq - folded
-        return (projected, inner_rw)
+        return (residual - expand(solved), total_sq - folded)
 
     start_load = rigid_load * mode_mask.reshape(sub_count * mode_num)
-    start_solved, unused_sq, unused_fold = coarse(start_load, jnp.zeros((), jnp.float32))
+    start_solved, _, _ = coarse(start_load, jnp.zeros((), F32))
     multipliers = expand(start_solved)
     residual = dual_rhs - operator(multipliers)
     projected, inner_rw = project(residual)
     direction = projected
-    for turn_idx in range(ITERATIONS):
+    for _ in range(ITERATIONS):
         applied = operator(direction)
         curvature = lax.psum(jnp.sum(direction * applied), "sub")
         step_len = inner_rw / curvature
@@ -96,9 +97,531 @@
     return (multipliers, projected)
 
 
+def split3(value):
+    high = value.astype(BF16)
+    rest = value - high.astype(F32)
+    mid = rest.astype(BF16)
+    low = (rest - mid.astype(F32)).astype(BF16)
+    return high, mid, low
+
+
+def select_dot(chooser, value):
+    width = value.shape[1]
+    wide = jnp.dot(
+        chooser, jnp.concatenate(split3(value), axis=1), preferred_element_type=F32
+    )
+    return (wide[:, 2 * width :] + wide[:, width : 2 * width]) + wide[:, :width]
+
+
+def one_hot(column, width):
+    rows = column.shape[0]
+    return (lax.broadcasted_iota(jnp.int32, (rows, width), 1) == column).astype(F32)
+
+
+def total(value):
+    return jnp.sum(jnp.sum(value, axis=0, keepdims=True), axis=1, keepdims=True)
+
+
+class Shape:
+    def __init__(self, dual_ops, rigid_traces, coarse_factor, partner, send_list):
+        self.subs, self.rows, self.order = dual_ops.shape
+        self.blocks = partner.shape[1]
+        self.modes = rigid_traces.shape[1]
+        self.slots = send_list.shape[1]
+        self.crs = lax.axis_size("crs")
+        self.ndev = lax.axis_size("sub") * self.crs
+        self.pad = -(-self.subs // 16) * 16
+        self.all_rows = self.blocks * self.pad
+        self.piece_blocks = self.rows // LANES
+        self.piece = self.piece_blocks * self.pad
+        self.cols = coarse_factor.shape[1]
+        self.halves = -(-(self.cols + 8) // LANES)
+        self.wide = self.halves * LANES
+        self.t_rows = self.crs * self.halves
+        self.spot = self.cols - (self.halves - 1) * LANES
+
+    def scalar_at(self, index):
+        rows = lax.broadcasted_iota(jnp.int32, (self.t_rows, LANES), 0)
+        lanes = lax.broadcasted_iota(jnp.int32, (self.t_rows, LANES), 1)
+        return (rows == self.halves - 1) & (lanes == self.spot + index)
+
+    def t_mask(self):
+        rows = lax.broadcasted_iota(jnp.int32, (self.t_rows, LANES), 0)
+        lanes = lax.broadcasted_iota(jnp.int32, (self.t_rows, LANES), 1)
+        return (rows % self.halves < self.halves - 1) | (lanes < self.spot)
+
+    def slot_of(self, rel):
+        return (rel % 2) * (self.crs // 2) + rel // 2
+
+
+def rows_of(value, sh):
+    return jnp.concatenate(
+        [value[:, b * LANES : (b + 1) * LANES] for b in range(value.shape[1] // LANES)], axis=0
+    )
+
+
+def lanes_of(value, sh):
+    return jnp.concatenate(
+        [value[b * sh.pad : (b + 1) * sh.pad] for b in range(value.shape[0] // sh.pad)], axis=1
+    )
+
+
+def factor_tile(w_refs, sh, rel, where, mode):
+    slot = sh.slot_of(rel)
+    half = sh.crs // 2
+    ref = w_refs[slot // half]
+    base = ((slot % half) * 3 + where) * sh.modes * sh.pad + mode * sh.pad
+    return ref[base : base + sh.pad, :]
+
+
+def coarse_back(w_refs, t_ref, me, sh):
+    t_row = []
+    for rel in range(sh.crs):
+        at = jnp.bitwise_xor(me, rel) * sh.halves
+        t_row.append(
+            jnp.concatenate([t_ref[pl.ds(at + h, 1), :] for h in range(sh.halves)], axis=1)
+        )
+    columns = []
+    for mode in range(sh.modes):
+        parts = []
+        for where in range(3):
+            acc = jnp.zeros((sh.pad, sh.wide), F32)
+            for rel in range(sh.crs):
+                acc += factor_tile(w_refs, sh, rel, where, mode) * t_row[rel]
+            parts.append(
+                jnp.broadcast_to(jnp.sum(acc, axis=1, keepdims=True), (sh.pad, LANES))
+            )
+        columns.append(jnp.concatenate(parts, axis=0))
+    return jnp.concatenate(columns, axis=1)
+
+
+def lift(tr_ref, pt_ref, ep_ref, w_refs, t_ref, me, sh):
+    spread = coarse_back(w_refs, t_ref, me, sh)
+    far = select_dot(ep_ref[...], spread)
+    out = jnp.zeros((sh.all_rows, LANES), F32)
+    for mode in range(sh.modes):
+        own = spread[: sh.pad, mode * LANES : (mode + 1) * LANES]
+        own = jnp.concatenate([own] * sh.blocks, axis=0)
+        out += tr_ref[mode] * own - pt_ref[mode] * far[:, mode * LANES : (mode + 1) * LANES]
+    return out
+
+
+def coarse_part(value, tr_ref, pt_ref, ept_ref, w_refs, me, sh, t_out):
+    at = pl.multiple_of(me * sh.piece, 16)
+    own, far = [], []
+    for mode in range(sh.modes):
+        mine = tr_ref[mode, pl.ds(at, sh.piece), :] * value
+        acc = mine[: sh.pad]
+        for b in range(1, sh.piece_blocks):
+            acc = acc + mine[b * sh.pad : (b + 1) * sh.pad]
+        own.append(acc)
+        far.append(pt_ref[mode, pl.ds(at, sh.piece), :] * value)
+    moved = select_dot(ept_ref[...], jnp.concatenate(far, axis=1))
+    sums = [jnp.zeros((sh.pad, sh.wide), F32) for _ in range(sh.crs)]
+    for mode in range(sh.modes):
+        moved_k = moved[:, mode * LANES : (mode + 1) * LANES]
+        for where in range(3):
+            part = -moved_k[where * sh.pad : (where + 1) * sh.pad]
+            if where == 0:
+                part = part + own[mode]
+            weight = jnp.sum(part, axis=1, keepdims=True)
+            for rel in range(sh.crs):
+                sums[rel] = sums[rel] + factor_tile(w_refs, sh, rel, where, mode) * weight
+    for rel in range(sh.crs):
+        row = jnp.sum(sums[rel], axis=0, keepdims=True)
+        at_t = jnp.bitwise_xor(me, rel) * sh.halves
+        for h in range(sh.halves):
+            t_out[pl.ds(at_t + h, 1), :] = row[:, h * LANES : (h + 1) * LANES]
+
+
+def start_ops(ops_hbm, ops_vmem, sems, sh):
+    for s in range(sh.subs):
+        pltpu.make_async_copy(ops_hbm.at[s], ops_vmem.at[s], sems.at[s]).start()
+
+
+def product(lowered, ops_hbm, ops_vmem, sems, sh):
+    row = lax.broadcasted_iota(jnp.int32, (sh.pad, sh.rows), 0)
+    acc = jnp.zeros((sh.pad, sh.rows), F32)
+    for s in range(sh.subs):
+        pltpu.make_async_copy(ops_hbm.at[s], ops_vmem.at[s], sems.at[s]).wait()
+        part = lax.dot_general(
+            lowered, ops_vmem[s], (((1,), (1,)), ((), ())), preferred_element_type=F32
+        )
+        acc = jnp.where(row == s, part, acc)
+    return rows_of(acc, sh)
+
+
+def sum_parcels(t_in_ref, sh):
+    acc = t_in_ref[0]
+    for i in range(1, sh.ndev):
+        acc = acc + t_in_ref[i]
+    return acc
+
+
+def pick(t_sum, sh, index):
+    return total(jnp.where(sh.scalar_at(index), t_sum, 0.0))
+
+
+def norm2(t_vec, sh):
+    return total(jnp.where(sh.t_mask(), t_vec * t_vec, 0.0))
+
+
+def send_t(t_scr, scalars, sh, t_out):
+    payload = jnp.where(sh.t_mask(), t_scr[...], 0.0)
+    for index, value in scalars.items():
+        payload = jnp.where(sh.scalar_at(index), value, payload)
+    if len(t_out.shape) == 2:
+        t_out[...] = payload
+    else:
+        for i in range(sh.ndev):
+            t_out[i] = payload
+
+
+def pack_kernel(sh, me_ref, tr_ref, send_ref, load_ref, factor_ref, parcel_a, parcel_b, t_out):
+    for which, out in ((0, parcel_a), (1, parcel_b)):
+        chooser = one_hot(send_ref[:, which : which + 1], sh.all_rows).astype(BF16)
+        for k in range(sh.modes + 1):
+            out[k] = select_dot(chooser, tr_ref[k])
+    part = jnp.dot(
+        load_ref[...], factor_ref[...], preferred_element_type=F32, precision=lax.Precision.HIGHEST
+    )
+    part = jnp.concatenate(
+        [part, jnp.zeros((part.shape[0], sh.wide - sh.cols), F32)], axis=1
+    )[:1]
+    rows = lax.broadcasted_iota(jnp.int32, (sh.t_rows, LANES), 0)
+    payload = jnp.zeros((sh.t_rows, LANES), F32)
+    for h in range(sh.halves):
+        payload = jnp.where(
+            rows == me_ref[0] * sh.halves + h, part[:, h * LANES : (h + 1) * LANES], payload
+        )
+    for i in range(sh.ndev):
+        t_out[i] = payload
+
+
+def first_kernel(
+    sh, me_ref, tr_in, halo_a, halo_b, index_ref, psub_ref, t_in, w0, w1, ops_hbm,
+    tr_out, pt_out, jump_out, ep_out, ept_out, lam_out, q_out, t_out,
+    t_scr, ops_vmem, sems,
+):
+    start_ops(ops_hbm, ops_vmem, sems, sh)
+    me = me_ref[0]
+    w_refs = (w0, w1)
+    index = index_ref[...]
+    live = (index[:, 2:3] >= 0).astype(F32)
+    col_num = 3 * sh.crs * sh.piece
+    jump_out[...] = (one_hot(index[:, 0:1], col_num) - one_hot(index[:, 1:2], col_num)).astype(BF16)
+    ep_out[...] = one_hot(index[:, 3:4], 3 * sh.pad).astype(BF16)
+    ept_out[...] = (
+        lax.broadcasted_iota(jnp.int32, (3 * sh.pad, sh.piece), 0) == psub_ref[...]
+    ).astype(BF16)
+    source = one_hot(index[:, 2:3], sh.all_rows + 2 * sh.slots).astype(BF16)
+    for k in range(sh.modes + 1):
+        whole = jnp.concatenate([tr_in[k], halo_a[k], halo_b[k]], axis=0)
+        far = select_dot(source, whole)
+        if k < sh.modes:
+            tr_out[k] = tr_in[k] * live
+            pt_out[k] = far
+        else:
+            tr_out[k] = tr_in[k]
+            pt_out[k] = tr_in[k] * live - far
+    t_scr[...] = sum_parcels(t_in, sh)
+    lam = lift(tr_out, pt_out, ep_out, w_refs, t_scr, me, sh)
+    lam_out[...] = lam
+    lowered = lanes_of(2.0 * lam, sh).astype(BF16)
+    q = product(lowered, ops_hbm, ops_vmem, sems, sh)
+    q_out[...] = q
+    at = pl.multiple_of(me * sh.piece, 16)
+    value = tr_out[sh.modes, pl.ds(at, sh.piece), :] - 2.0 * q
+    coarse_part(value, tr_out, pt_out, ept_out, w_refs, me, sh, t_scr)
+    send_t(t_scr, {}, sh, t_out)
+
+
+def second_kernel(
+    sh, me_ref, tr_ref, pt_ref, jump_ref, ep_ref, ept_ref, q0, q1, t_in, w0, w1, ops_hbm,
+    r_out, jr_out, d_out, jd_out, tr0_out, q_out, t_out,
+    t_scr, ops_vmem, sems,
+):
+    start_ops(ops_hbm, ops_vmem, sems, sh)
+    me = me_ref[0]
+    w_refs = (w0, w1)
+    tr0_out[...] = sum_parcels(t_in, sh)
+    applied = select_dot(jump_ref[...], jnp.concatenate([q0[...], q1[...]], axis=0))
+    back = lift(tr_ref, pt_ref, ep_ref, w_refs, tr0_out, me, sh)
+    residual = tr_ref[sh.modes] - applied
+    r_out[...] = residual
+    jump_r = pt_ref[sh.modes] - 2.0 * applied
+    jr_out[...] = jump_r
+    d_out[...] = residual - back
+    jump_d = jump_r - 2.0 * back
+    jd_out[...] = jump_d
+    q = product(lanes_of(jump_d, sh).astype(BF16), ops_hbm, ops_vmem, sems, sh)
+    q_out[...] = q
+    coarse_part(2.0 * q, tr_ref, pt_ref, ept_ref, w_refs, me, sh, t_scr)
+    at = pl.multiple_of(me * sh.piece, 16)
+    mine = pl.ds(at, sh.piece)
+    send_t(
+        t_scr,
+        {
+            0: total(jd_out[mine, :] * q),
+            1: total(jr_out[mine, :] * q),
+            2: total(r_out[mine, :] * r_out[mine, :]),
+        },
+        sh,
+        t_out,
+    )
+
+
+def square_kernel(sh, me_ref, jump_ref, q0, q1, t_in, applied_out, t_out):
+    me = me_ref[0]
+    applied_out[...] = select_dot(jump_ref[...], jnp.concatenate([q0[...], q1[...]], axis=0))
+    at = pl.multiple_of(me * sh.piece, 16)
+    mine = applied_out[pl.ds(at, sh.piece), :]
+    payload = jnp.where(sh.scalar_at(3), total(mine * mine), t_in[...])
+    for i in range(sh.ndev):
+        t_out[i] = payload
+
+
+def third_kernel(
+    sh, me_ref, tr_ref, pt_ref, ep_ref, ept_ref, applied_ref, t_in, w0, w1, r_ref, jr_ref, d_ref,
+    jd_ref, tr0_ref, lam_ref, ops_hbm,
+    r_out, d_out, lam_out, tr1_out, q_out, t_out,
+    t_scr, jd_scr, ops_vmem, sems,
+):
+    start_ops(ops_hbm, ops_vmem, sems, sh)
+    me = me_ref[0]
+    w_refs = (w0, w1)
+    sums = sum_parcels(t_in, sh)
+    tr0 = tr0_ref[...]
+    d_a, r_a, r_r, a_a = (pick(sums, sh, i) for i in range(4))
+    rw0 = r_r - norm2(tr0, sh)
+    alpha = rw0 / d_a
+    tr1 = tr0 - alpha * sums
+    rw1 = (r_r - 2.0 * alpha * r_a + alpha * alpha * a_a) - norm2(tr1, sh)
+    beta = rw1 / rw0
+    tr1_out[...] = jnp.where(sh.scalar_at(0), rw1, tr1)
+    back = lift(tr_ref, pt_ref, ep_ref, w_refs, tr1_out, me, sh)
+    applied = applied_ref[...]
+    residual = r_ref[...] - alpha * applied
+    r_out[...] = residual
+    lam_out[...] = lam_ref[...] + alpha * d_ref[...]
+    d_out[...] = (residual - back) + beta * d_ref[...]
+    jump_d = (jr_ref[...] - 2.0 * alpha * applied - 2.0 * back) + beta * jd_ref[...]
+    jd_scr[...] = jump_d
+    q = product(lanes_of(jump_d, sh).astype(BF16), ops_hbm, ops_vmem, sems, sh)
+    q_out[...] = q
+    coarse_part(2.0 * q, tr_ref, pt_ref, ept_ref, w_refs, me, sh, t_scr)
+    at = pl.multiple_of(me * sh.piece, 16)
+    send_t(t_scr, {0: total(jd_scr[pl.ds(at, sh.piece), :] * q)}, sh, t_out)
+
+
+def last_kernel(
+    sh, me_ref, tr_ref, pt_ref, jump_ref, ep_ref, q0, q1, t_in, w0, w1, r_ref, d_ref, lam_ref,
+    tr1_ref, lam_out, p_out, t_scr,
+):
+    me = me_ref[0]
+    sums = sum_parcels(t_in, sh)
+    tr1 = tr1_ref[...]
+    alpha = pick(tr1, sh, 0) / pick(sums, sh, 0)
+    t_scr[...] = tr1 - alpha * sums
+    applied = select_dot(jump_ref[...], jnp.concatenate([q0[...], q1[...]], axis=0))
+    back = lift(tr_ref, pt_ref, ep_ref, (w0, w1), t_scr, me, sh)
+    lam = lam_ref[...] + alpha * d_ref[...]
+    projected = (r_ref[...] - alpha * applied) - back
+    lam_out[...] = lanes_of(lam, sh)[: sh.subs]
+    p_out[...] = lanes_of(projected, sh)[: sh.subs]
+
+
+def permute(value, move):
+    sub_num, crs_num = lax.axis_size("sub"), lax.axis_size("crs")
+    pairs = []
+    for i in range(sub_num):
+        for j in range(crs_num):
+            to_i, to_j = move(i, j)
+            if 0 <= to_i < sub_num:
+                pairs.append((i * crs_num + j, to_i * crs_num + to_j))
+    return lax.ppermute(value, AXES, pairs)
+
+
+def swap_a(value):
+    return permute(value, lambda i, j: (i ^ 1, j))
+
+
+def swap_b(value):
+    return permute(value, lambda i, j: (((i + 1) ^ 1) - 1, j))
+
+
+def spread_pieces(value):
+    crs_num = lax.axis_size("crs")
+    near = jnp.concatenate([value, swap_a(value), swap_b(value)], axis=0)
+    group = [near]
+    for shift in range(1, crs_num // 2):
+        group.append(permute(near, lambda i, j: (i, j ^ (2 * shift))))
+    first = jnp.concatenate(group, axis=0)
+    return first, permute(first, lambda i, j: (i, j ^ 1))
+
+
+def local(
+    dual_ops, rigid_traces, coarse_factor, partner, send_list, mode_count, dual_rhs, rigid_load
+):
+    sh = Shape(dual_ops, rigid_traces, coarse_factor, partner, send_list)
+    me = lax.axis_index("crs")
+    odd = lax.axis_index("sub") % 2
+    blocks, pad, subs, modes = sh.blocks, sh.pad, sh.subs, sh.modes
+    local_blocks = subs * blocks
+    extra = pad - subs
+
+    mode_mask = (jnp.arange(modes, dtype=jnp.int32)[None, :] < mode_count[:, None]).astype(F32)
+    fields = jnp.concatenate([rigid_traces * mode_mask[:, :, None], dual_rhs[:, None, :]], axis=1)
+    fields = fields.reshape(subs, modes + 1, blocks, LANES).transpose(1, 2, 0, 3)
+    fields = jnp.pad(fields, ((0, 0), (0, 0), (0, extra), (0, 0)))
+    fields = fields.reshape(modes + 1, sh.all_rows, LANES)
+    load = jnp.broadcast_to((rigid_load * mode_mask.reshape(-1))[None, :], (8, subs * modes))
+
+    factor = coarse_factor.reshape(subs, modes, sh.cols).transpose(1, 0, 2)
+    factor = jnp.pad(factor, ((0, 0), (0, extra), (0, sh.wide - sh.cols)))
+    factor = factor.reshape(modes * pad, sh.wide)
+
+    to_a = jnp.where(odd == 1, send_list[0], send_list[1])
+    to_b = jnp.where(odd == 1, send_list[1], send_list[0])
+    from_a, from_b = swap_a(to_a), swap_b(to_b)
+    outgoing = jnp.stack([to_a, to_b], axis=1)
+    outgoing = jnp.where(outgoing >= 0, (outgoing % blocks) * pad + outgoing // blocks, -1)
+
+    code = jnp.pad(partner.T, ((0, 0), (0, extra)), constant_values=-1).reshape(sh.all_rows)
+    own_row = jnp.arange(sh.all_rows, dtype=jnp.int32)
+    is_own = (code >= 0) & (code < local_blocks)
+    before = (code >= local_blocks) & (code < local_blocks + sh.slots)
+    slot = jnp.where(before, code - local_blocks, code - local_blocks - sh.slots)
+    is_a = (code >= local_blocks) & (before == (odd == 1))
+    is_b = (code >= local_blocks) & (before != (odd == 1))
+    hit = slot[:, None] == jnp.arange(sh.slots, dtype=jnp.int32)[None, :]
+    theirs = jnp.where(is_a[:, None], from_a[None, :], from_b[None, :])
+    theirs = jnp.sum(jnp.where(hit, theirs, 0), axis=1)
+    there = jnp.where(is_own, code, theirs)
+    there_s, there_b = there // blocks, there % blocks
+    where_d = jnp.where(is_own, 0, jnp.where(is_a, 1, 2))
+
+    def piece_row(block, sub, where):
+        place = sh.slot_of(jnp.bitwise_xor(block // sh.piece_blocks, me)) * 3 + where
+        return place * sh.piece + (block % sh.piece_blocks) * pad + sub
+
+    linked = code >= 0
+    own_col = jnp.where(linked, piece_row(own_row // pad, own_row % pad, 0), -1)
+    far_col = jnp.where(linked, piece_row(there_b, there_s, where_d), -1)
+    trace_col = jnp.where(
+        is_own,
+        there_b * pad + there_s,
+        jnp.where(is_a, sh.all_rows + slot, sh.all_rows + sh.slots + slot),
+    )
+    trace_col = jnp.where(linked, trace_col, -1)
+    far_sub = jnp.where(linked, where_d * pad + there_s, -1)
+    index = jnp.stack([own_col, far_col, trace_col, far_sub], axis=1)
+    piece_sub = lax.dynamic_slice_in_dim(far_sub, me * sh.piece, sh.piece)[None, :]
+    me_arr = me.reshape(1)
+
+    vmem = pl.BlockSpec(memory_space=pltpu.VMEM)
+    smem = pl.BlockSpec(memory_space=pltpu.SMEM)
+    hbm = pl.BlockSpec(memory_space=pl.ANY)
+    params = pltpu.CompilerParams(vmem_limit_bytes=48 * 1024 * 1024)
+
+    def call(kernel, outs, scratch, *operands, name):
+        ops = any(x is dual_ops for x in operands)
+        if ops:
+            scratch = scratch + [
+                pltpu.VMEM(dual_ops.shape, BF16),
+                pltpu.SemaphoreType.DMA((subs,)),
+            ]
+        return pl.pallas_call(
+            functools.partial(kernel, sh),
+            out_shape=[jax.ShapeDtypeStruct(s, t) for s, t in outs],
+            in_specs=[smem] + [hbm if x is dual_ops else vmem for x in operands],
+            out_specs=[vmem] * len(outs),
+            scratch_shapes=scratch,
+            compiler_params=params,
+            name=name,
+        )(me_arr, *operands)
+
+    state = ((sh.all_rows, LANES), F32)
+    t_shape = ((sh.t_rows, LANES), F32)
+    parcels = ((sh.ndev, sh.t_rows, LANES), F32)
+    q_shape = ((sh.piece, LANES), F32)
+    field_shape = (fields.shape, F32)
+    t_scratch = [pltpu.VMEM((sh.t_rows, LANES), F32)]
+
+    def exchange(parcel):
+        return lax.all_to_all(parcel, AXES, 0, 0)
+
+    parcel_shape = ((modes + 1, sh.slots, LANES), F32)
+    parcel_a, parcel_b, t_part = call(
+        pack_kernel, [parcel_shape, parcel_shape, parcels], [],
+        fields, outgoing, load, coarse_factor, name="pack",
+    )
+    halo_a, halo_b = swap_a(parcel_a), swap_b(parcel_b)
+    w0, w1 = spread_pieces(factor)
+    t_in = exchange(t_part)
+
+    traces, far_traces, jumper, far_pick, far_put, lam0, q, t_part = call(
+        first_kernel,
+        [
+            field_shape, field_shape,
+            ((sh.all_rows, 3 * sh.crs * sh.piece), BF16),
+            ((sh.all_rows, 3 * pad), BF16),
+            ((3 * pad, sh.piece), BF16),
+            state, q_shape, parcels,
+        ],
+        t_scratch,
+        fields, halo_a, halo_b, index, piece_sub, t_in, w0, w1, dual_ops, name="first",
+    )
+    q0, q1 = spread_pieces(q)
+    t_in = exchange(t_part)
+
+    r0, jr0, d0, jd0, tr0, q, t_part = call(
+        second_kernel,
+        [state, state, state, state, t_shape, q_shape, t_shape],
+        t_scratch,
+        traces, far_traces, jumper, far_pick, far_put, q0, q1, t_in, w0, w1, dual_ops,
+        name="second",
+    )
+    q0, q1 = spread_pieces(q)
+    applied, t_part = call(
+        square_kernel, [state, parcels], [], jumper, q0, q1, t_part, name="square"
+    )
+    t_in = exchange(t_part)
+
+    r1, d1, lam1, tr1, q, t_part = call(
+        third_kernel,
+        [state, state, state, t_shape, q_shape, parcels],
+        t_scratch + [pltpu.VMEM((sh.all_rows, LANES), F32)],
+        traces, far_traces, far_pick, far_put, applied, t_in, w0, w1, r0, jr0, d0, jd0, tr0, lam0,
+        dual_ops, name="third",
+    )
+    q0, q1 = spread_pieces(q)
+    t_in = exchange(t_part)
+
+    multipliers, projected = call(
+        last_kernel,
+        [((subs, sh.order), F32), ((subs, sh.order), F32)],
+        t_scratch,
+        traces, far_traces, jumper, far_pick, q0, q1, t_in, w0, w1, r1, d1, lam1, tr1,
+        name="last",
+    )
+    return multipliers, projected
+
+
+def body(*args):
+    dual_ops, _, _, partner = args[:4]
+    crs_num, sub_num = lax.axis_size("crs"), lax.axis_size("sub")
+    whole_blocks = (
+        dual_ops.shape[2] // partner.shape[1] == LANES and dual_ops.shape[1] % LANES == 0
+    )
+    if whole_blocks and crs_num % 2 == 0 and crs_num & (crs_num - 1) == 0 and sub_num % 2 == 0:
+        return local(*args)
+    return plain(*args)
+
+
 def solution(mesh):
     return jax.shard_map(
-        local,
+        body,
         mesh=mesh,
         in_specs=(
             P("sub", "crs", None),

time: 338 us -> 137 us (0.41)
  blocking collectives: 157 us -> 12.8 us
  matrix products: 35.6 us -> 0 us
  waiting for transfers between devices: 56.1 us -> 26 us
  Pallas kernels: 0 us -> 29.2 us
  other arithmetic: 10.8 us -> 4.49 us
  starting transfers between devices: 52.2 us -> 46.4 us
  between operations: 5.57 us -> 1 us
    psum x10 -> x0, blocking collectives: 141 us -> none  [the longest x5 98 us: coarse(): column_sum, total_sq = lax.psum((column_part, squares), 'sub')]
    dot_general x18 -> x0, matrix products: 35.6 us -> none  [the longest x3 26.3 us: operator(): jnp.einsum('srk,sk->sr', dual_ops, lowered, preferred_element_type=jnp.fl...]
    ppermute x26 -> x20, waiting for transfers between devices: 56.1 us -> 23.2 us  [permute(): return lax.ppermute(value, AXES, pairs)]
    pallas_call x0 -> x6, Pallas kernels: none -> 29.2 us  [call(): pl.pallas_call(functools.partial(kernel, sh), out_shape=[jax.ShapeDtypeSt...]
    ppermute x26 -> x20, starting transfers between devices: 52.2 us -> 34.6 us  [permute(): return lax.ppermute(value, AXES, pairs)]
    gather x39 -> x0, local copies, waits for them, and re-layouts: 17.4 us -> none  [the longest x26 8.81 us: jump(): gathered[source]]
    all_gather x3 -> x0, blocking collectives: 16 us -> none  [operator(): full_rows = lax.all_gather(partial_rows, 'crs', axis=1, tiled=True)]
    all_to_all x0 -> x1, blocking collectives: none -> 12.8 us  [exchange(): return lax.all_to_all(parcel, AXES, 0, 0)]
  transfers between devices with their start and end apart: 26 -> 23, of which waited for: 24 -> 10; matrix products, arithmetic and copies ran while one was open for 1% -> 6% of each run, Pallas kernels for 0% -> 1%
where the time goes in v1:
time: 137 us; the launch traced here: 136 us
  starting transfers between devices  46.4 us (34%)
  Pallas kernels  29.2 us (21%)
  waiting for transfers between devices  26 us (19%)
  local copies, waits for them, and re-layouts  16.3 us (12%)
  blocking collectives  12.8 us (9%)
  other arithmetic  4.49 us (3%)
    ppermute x20, starting transfers between devices, permute(): return lax.ppermute(value, AXES, pairs)  34.6 us
    pallas_call x6, Pallas kernels, call(): pl.pallas_call(functools.partial(kernel, sh), out_shape=[jax.ShapeDtypeSt...  29.2 us
    ppermute x20, waiting for transfers between devices, permute(): return lax.ppermute(value, AXES, pairs)  23.2 us
    all_to_all x1, blocking collectives, exchange(): return lax.all_to_all(parcel, AXES, 0, 0)  12.8 us
    unnamed x40, local copies, waits for them, and re-layouts  12.6 us
    all_to_all x3, starting transfers between devices, exchange(): return lax.all_to_all(parcel, AXES, 0, 0)  11.8 us
    all_to_all x3, waiting for transfers between devices, exchange(): return lax.all_to_all(parcel, AXES, 0, 0)  2.75 us
  transfers between devices with their start and end apart: 23, of which 10 were waited for; matrix products, arithmetic and copies ran while one was open for 6% of the time, Pallas kernels for 1%

profile of v1, /device:TPU:0, one launch (start us, length us, event | category | flops | bytes accessed | tf_op | source)
XLA Modules:
  0.0 136.2 jit_solution(7483607683836461977)
XLA Ops:
  2.3 5.8 %collective-permute-start.4 = (f32[96,256]{1,0:T(8,128)S(1)}, f32[96,256]{1,0:T(8,128)S(1)}, u32[]{:S(2)}, u32[]{:S(2)}) collective-permute-start(f32[96,256]{1,0:T(8,128)S(1)} %bitcast.19), channel_id=1, source_target_pairs={{0,4},{1,5},{2,6},{3,7},{4,0},{5,1},{6,2},{7,3},{8,12},{9,13},{10,... | collective-permute-start | bytes 294920 | tf_op jit(solution)/shard_map/ppermute | solution.py:442
  9.5 4.4 %collective-permute-start.2 = (s32[72]{0:T(128)S(1)}, s32[72]{0:T(128)S(1)}, u32[]{:S(2)}, u32[]{:S(2)}) collective-permute-start(s32[72]{0:T(128)S(1)} %bitcast.26), channel_id=1, source_target_pairs={{0,4},{1,5},{2,6},{3,7},{4,0},{5,1},{6,2},{7,3},{8,12},{9,13},{10,... | collective-permute-start | bytes 872 | tf_op jit(solution)/shard_map/ppermute | solution.py:442
  15.8 1.2 broadcast_multiply_fusion
  19.2 1.3 pack.1
  20.5 3.6 %all-to-all-start = ((f32[32,8,128]{2,1,0:T(8,128)}), f32[32,8,128]{2,1,0:T(8,128)S(1)}, u32[]{:S(2)}, u32[]{:S(2)}) async-start(f32[32,8,128]{2,1,0:T(8,128)} %get-tuple-element.30), calls=%async_computation | async-start | bytes 262144 | tf_op jit(solution)/shard_map/all_to_all | solution.py:552
  24.1 1.8 %collective-permute-start = (f32[7,72,128]{2,1,0:T(8,128)S(1)}, f32[7,72,128]{2,1,0:T(8,128)S(1)}, u32[]{:S(2)}, u32[]{:S(2)}) collective-permute-start(f32[7,72,128]{2,1,0:T(8,128)S(1)} %get-tuple-element.28), channel_id=1, source_target_pairs={{0,4},{1,5},{2,6},{3,7},{4,0},{5,1},{6,2},{7,3},{8,12},{9,13},{10,... | collective-permute-start | bytes 774152 | tf_op jit(solution)/shard_map/ppermute | solution.py:442
  27.6 1.5 %collective-permute-start.6 = (f32[288,256]{1,0:T(8,128)S(1)}, f32[288,256]{1,0:T(8,128)S(1)}, u32[]{:S(2)}, u32[]{:S(2)}) collective-permute-start(f32[288,256]{1,0:T(8,128)S(1)} %pad_maximum_fusion.1), channel_id=1, source_target_pairs={{0,2},{1,3},{2,0},{3,1},{4,6},{5,7},{6,4},{7,5},{8,10},{9,11},{10,... | collective-permute-start | bytes 884744 | tf_op jit(solution)/shard_map/ppermute | solution.py:442
  29.3 7.5 %collective-permute-done.6 = f32[288,256]{1,0:T(8,128)S(1)} collective-permute-done((f32[288,256]{1,0:T(8,128)S(1)}, f32[288,256]{1,0:T(8,128)S(1)}, u32[]{:S(2)}, u32[]{:S(2)}) %collective-permute-start.6) | collective-permute-done | bytes 294944 | tf_op jit(solution)/shard_map/ppermute | solution.py:442
  41.8 0.9 copy-done.5
  42.7 0.9 copy-done.7
  43.7 9.1 %first.1 = (f32[7,192,128]{2,1,0:T(8,128)S(1)}, f32[7,192,128]{2,1,0:T(8,128)S(1)}, bf16[192,576]{1,0:T(8,128)(2,1)S(1)}, bf16[192,48]{1,0:T(8,128)(2,1)S(1)}, b...) custom-call(s32[1]{0:T(128)} %bitcast.me_ref, ...), custom_call_target="tpu_custom_call" | custom-call | tf_op jit(solution)/shard_map/first/pallas_call | solution.py:534
  54.9 5.3 %collective-permute-start.8 = (f32[48,128]{1,0:T(8,128)}, f32[48,128]{1,0:T(8,128)S(1)}, u32[]{:S(2)}, u32[]{:S(2)}) collective-permute-start(f32[48,128]{1,0:T(8,128)} %get-tuple-element.36), channel_id=1, source_target_pairs={{0,4},{1,5},{2,6},{3,7},{4,0},{5,1},{6,2},{7,3},{8,12},{9,13},{10,... | collective-permute-start | bytes 73736 | tf_op jit(solution)/shard_map/ppermute | solution.py:442
  61.0 5.6 %all-to-all-start.1 = ((f32[32,8,128]{2,1,0:T(8,128)}), f32[32,8,128]{2,1,0:T(8,128)S(1)}, u32[]{:S(2)}, u32[]{:S(2)}) async-start(f32[32,8,128]{2,1,0:T(8,128)} %copy-done.8), calls=%async_computation.1 | async-start | bytes 262144 | tf_op jit(solution)/shard_map/all_to_all | solution.py:552
  67.3 1.8 %collective-permute-start.10 = (f32[144,128]{1,0:T(8,128)S(1)}, f32[144,128]{1,0:T(8,128)S(1)}, u32[]{:S(2)}, u32[]{:S(2)}) collective-permute-start(f32[144,128]{1,0:T(8,128)S(1)} %pad_maximum_fusion.2), channel_id=1, source_target_pairs={{0,2},{1,3},{2,0},{3,1},{4,6},{5,7},{6,4},{7,5},{8,10},{9,11},{10,... | collective-permute-start | bytes 221192 | tf_op jit(solution)/shard_map/ppermute | solution.py:442
  69.1 3.3 %collective-permute-done.10 = f32[144,128]{1,0:T(8,128)S(1)} collective-permute-done((f32[144,128]{1,0:T(8,128)S(1)}, f32[144,128]{1,0:T(8,128)S(1)}, u32[]{:S(2)}, u32[]{:S(2)}) %collective-permute-start.10) | collective-permute-done | bytes 73760 | tf_op jit(solution)/shard_map/ppermute | solution.py:442
  72.4 1.4 %collective-permute-done.11.q1 = f32[288,128]{1,0:T(8,128)S(1)} collective-permute-done((f32[288,128]{1,0:T(8,128)S(1)}, f32[288,128]{1,0:T(8,128)S(1)}, u32[]{:S(2)}, u32[]{:S(2)}) %collective-permute-start.11) | collective-permute-done | bytes 147488 | tf_op jit(solution)/shard_map/ppermute | solution.py:442
  73.8 1.0 all-to-all-done.1.t_in
  74.8 8.1 %second.1 = (f32[192,128]{1,0:T(8,128)S(1)}, f32[192,128]{1,0:T(8,128)S(1)}, f32[192,128]{1,0:T(8,128)S(1)}, f32[192,128]{1,0:T(8,128)S(1)}, f32[8,128]{1,0:T(8,...) custom-call(s32[1]{0:T(128)} %bitcast.me_ref, f32[7,192,128]{2,1,0:T(8,128)S(1)} %get-tuple-element.31.tr_ref, ...), custom_call_target="tpu_custom_call" | custom-call | tf_op jit(solution)/shard_map/second/pallas_call | solution.py:534
  83.6 3.5 %collective-permute-start.12 = (f32[48,128]{1,0:T(8,128)S(1)}, f32[48,128]{1,0:T(8,128)S(1)}, u32[]{:S(2)}, u32[]{:S(2)}) collective-permute-start(f32[48,128]{1,0:T(8,128)S(1)} %get-tuple-element.38), channel_id=1, source_target_pairs={{0,4},{1,5},{2,6},{3,7},{4,0},{5,1},{6,2},{7,3},{8,12},{9,13},{10,... | collective-permute-start | bytes 73736 | tf_op jit(solution)/shard_map/ppermute | solution.py:442
  87.2 1.8 %collective-permute-done.12 = f32[48,128]{1,0:T(8,128)S(1)} collective-permute-done((f32[48,128]{1,0:T(8,128)S(1)}, f32[48,128]{1,0:T(8,128)S(1)}, u32[]{:S(2)}, u32[]{:S(2)}) %collective-permute-start.12) | collective-permute-done | bytes 24608 | tf_op jit(solution)/shard_map/ppermute | solution.py:442
  89.0 1.2 collective-permute-start.14
  90.2 3.1 %collective-permute-done.14 = f32[144,128]{1,0:T(8,128)S(1)} collective-permute-done((f32[144,128]{1,0:T(8,128)S(1)}, f32[144,128]{1,0:T(8,128)S(1)}, u32[]{:S(2)}, u32[]{:S(2)}) %collective-permute-start.14) | collective-permute-done | bytes 73760 | tf_op jit(solution)/shard_map/ppermute | solution.py:442
  93.3 1.4 %collective-permute-done.15.q1 = f32[288,128]{1,0:T(8,128)S(1)} collective-permute-done((f32[288,128]{1,0:T(8,128)S(1)}, f32[288,128]{1,0:T(8,128)S(1)}, u32[]{:S(2)}, u32[]{:S(2)}) %collective-permute-start.15) | collective-permute-done | bytes 147488 | tf_op jit(solution)/shard_map/ppermute | solution.py:442
  95.1 12.8 %all_to_all.20.t_in = f32[32,8,128]{2,1,0:T(8,128)S(1)} all-to-all(f32[32,8,128]{2,1,0:T(8,128)S(1)} %get-tuple-element.41), channel_id=1, replica_groups=mesh['sub'=8,'crs'=4] {'sub','crs'}, dimensions={0} | all-to-all | bytes 262144 | tf_op jit(solution)/shard_map/all_to_all | solution.py:552
  107.9 8.9 %third.1 = (f32[192,128]{1,0:T(8,128)S(1)}, f32[192,128]{1,0:T(8,128)S(1)}, f32[192,128]{1,0:T(8,128)S(1)}, f32[8,128]{1,0:T(8,128)S(1)}, f32[48,128]{1,0:T(8,128)S(1)}, /*index=5*/f32[32,8,128]{2,1,0:T(8,128)}) custom-call(s32[1]{0:T(128)} %bitcast.me_ref, f32[7,192,128]{2,1,0:T(8,128)S(1)} %get-tuple-element.31.tr_ref, ...), custom_call_target="tpu_custom_call" | custom-call | tf_op jit(solution)/shard_map/third/pallas_call | solution.py:534
  118.8 3.4 %collective-permute-start.16 = (f32[48,128]{1,0:T(8,128)S(1)}, f32[48,128]{1,0:T(8,128)S(1)}, u32[]{:S(2)}, u32[]{:S(2)}) collective-permute-start(f32[48,128]{1,0:T(8,128)S(1)} %get-tuple-element.48), channel_id=1, source_target_pairs={{0,4},{1,5},{2,6},{3,7},{4,0},{5,1},{6,2},{7,3},{8,12},{9,13},{10,... | collective-permute-start | bytes 73736 | tf_op jit(solution)/shard_map/ppermute | solution.py:442
  122.2 2.6 %all-to-all-start.3 = ((f32[32,8,128]{2,1,0:T(8,128)}), f32[32,8,128]{2,1,0:T(8,128)S(1)}, u32[]{:S(2)}, u32[]{:S(2)}) async-start(f32[32,8,128]{2,1,0:T(8,128)} %get-tuple-element.49), calls=%async_computation.3 | async-start | bytes 262144 | tf_op jit(solution)/shard_map/all_to_all | solution.py:552
  124.8 1.7 %collective-permute-start.18 = (f32[144,128]{1,0:T(8,128)S(1)}, f32[144,128]{1,0:T(8,128)S(1)}, u32[]{:S(2)}, u32[]{:S(2)}) collective-permute-start(f32[144,128]{1,0:T(8,128)S(1)} %pad_maximum_fusion.4), channel_id=1, source_target_pairs={{0,2},{1,3},{2,0},{3,1},{4,6},{5,7},{6,4},{7,5},{8,10},{9,11},{10,... | collective-permute-start | bytes 221192 | tf_op jit(solution)/shard_map/ppermute | solution.py:442
  126.6 3.4 %collective-permute-done.18 = f32[144,128]{1,0:T(8,128)S(1)} collective-permute-done((f32[144,128]{1,0:T(8,128)S(1)}, f32[144,128]{1,0:T(8,128)S(1)}, u32[]{:S(2)}, u32[]{:S(2)}) %collective-permute-start.18) | collective-permute-done | bytes 73760 | tf_op jit(solution)/shard_map/ppermute | solution.py:442
  129.9 1.4 %collective-permute-done.19.q1 = f32[288,128]{1,0:T(8,128)S(1)} collective-permute-done((f32[288,128]{1,0:T(8,128)S(1)}, f32[288,128]{1,0:T(8,128)S(1)}, u32[]{:S(2)}, u32[]{:S(2)}) %collective-permute-start.19) | collective-permute-done | bytes 147488 | tf_op jit(solution)/shard_map/ppermute | solution.py:442
  131.3 1.8 %all-to-all-done.3.t_in = f32[32,8,128]{2,1,0:T(8,128)S(1)} async-done(((f32[32,8,128]{2,1,0:T(8,128)}), f32[32,8,128]{2,1,0:T(8,128)S(1)}, u32[]{:S(2)}, u32[]{:S(2)}) %all-to-all-start.3) | async-done | bytes 131104 | tf_op jit(solution)/shard_map/all_to_all | solution.py:552
  134.8 1.3 last.1
  (101 shorter events, 22.3 us)
Async XLA Ops:
  1.6 25.3 %collective-permute-start.5 = (f32[96,256]{1,0:T(8,128)S(1)}, f32[96,256]{1,0:T(8,128)S(1)}, u32[]{:S(2)}, u32[]{:S(2)}) collective-permute-start(f32[96,256]{1,0:T(8,128)S(1)} %bitcast.18), channel_id=1, source_target_pairs={{4,8},{5,9},{6,10},{7,11},{8,4},{9,5},{10,6},{11,7},{12,16},{13,17... | collective-permute-start | bytes 294920 | tf_op jit(solution)/shard_map/ppermute | solution.py:442
  2.3 25.3 %collective-permute-start.4 = (f32[96,256]{1,0:T(8,128)S(1)}, f32[96,256]{1,0:T(8,128)S(1)}, u32[]{:S(2)}, u32[]{:S(2)}) collective-permute-start(f32[96,256]{1,0:T(8,128)S(1)} %bitcast.19), channel_id=1, source_target_pairs={{0,4},{1,5},{2,6},{3,7},{4,0},{5,1},{6,2},{7,3},{8,12},{9,13},{10,... | collective-permute-start | bytes 294920 | tf_op jit(solution)/shard_map/ppermute | solution.py:442
  8.8 20.4 %collective-permute-start.3 = (s32[72]{0:T(128)S(1)}, s32[72]{0:T(128)S(1)}, u32[]{:S(2)}, u32[]{:S(2)}) collective-permute-start(s32[72]{0:T(128)S(1)} %bitcast.29), channel_id=1, source_target_pairs={{4,8},{5,9},{6,10},{7,11},{8,4},{9,5},{10,6},{11,7},{12,16},{13,17... | collective-permute-start | bytes 872 | tf_op jit(solution)/shard_map/ppermute | solution.py:442
  9.5 19.7 %collective-permute-start.2 = (s32[72]{0:T(128)S(1)}, s32[72]{0:T(128)S(1)}, u32[]{:S(2)}, u32[]{:S(2)}) collective-permute-start(s32[72]{0:T(128)S(1)} %bitcast.26), channel_id=1, source_target_pairs={{0,4},{1,5},{2,6},{3,7},{4,0},{5,1},{6,2},{7,3},{8,12},{9,13},{10,... | collective-permute-start | bytes 872 | tf_op jit(solution)/shard_map/ppermute | solution.py:442
  18.3 0.9 copy-start.3
  20.5 17.4 %all-to-all-start = ((f32[32,8,128]{2,1,0:T(8,128)}), f32[32,8,128]{2,1,0:T(8,128)S(1)}, u32[]{:S(2)}, u32[]{:S(2)}) async-start(f32[32,8,128]{2,1,0:T(8,128)} %get-tuple-element.30), calls=%async_computation | async-start | bytes 262144 | tf_op jit(solution)/shard_map/all_to_all | solution.py:552
  24.1 14.4 %collective-permute-start = (f32[7,72,128]{2,1,0:T(8,128)S(1)}, f32[7,72,128]{2,1,0:T(8,128)S(1)}, u32[]{:S(2)}, u32[]{:S(2)}) collective-permute-start(f32[7,72,128]{2,1,0:T(8,128)S(1)} %get-tuple-element.28), channel_id=1, source_target_pairs={{0,4},{1,5},{2,6},{3,7},{4,0},{5,1},{6,2},{7,3},{8,12},{9,13},{10,... | collective-permute-start | bytes 774152 | tf_op jit(solution)/shard_map/ppermute | solution.py:442
  26.9 12.3 %collective-permute-start.1 = (f32[7,72,128]{2,1,0:T(8,128)S(1)}, f32[7,72,128]{2,1,0:T(8,128)S(1)}, u32[]{:S(2)}, u32[]{:S(2)}) collective-permute-start(f32[7,72,128]{2,1,0:T(8,128)S(1)} %get-tuple-element.29), channel_id=1, source_target_pairs={{4,8},{5,9},{6,10},{7,11},{8,4},{9,5},{10,6},{11,7},{12,16},{13,17... | collective-permute-start | bytes 774152 | tf_op jit(solution)/shard_map/ppermute | solution.py:442
  27.6 9.2 %collective-permute-start.6 = (f32[288,256]{1,0:T(8,128)S(1)}, f32[288,256]{1,0:T(8,128)S(1)}, u32[]{:S(2)}, u32[]{:S(2)}) collective-permute-start(f32[288,256]{1,0:T(8,128)S(1)} %pad_maximum_fusion.1), channel_id=1, source_target_pairs={{0,2},{1,3},{2,0},{3,1},{4,6},{5,7},{6,4},{7,5},{8,10},{9,11},{10,... | collective-permute-start | bytes 884744 | tf_op jit(solution)/shard_map/ppermute | solution.py:442
  36.9 3.1 %collective-permute-start.7 = (f32[576,256]{1,0:T(8,128)S(1)}, f32[576,256]{1,0:T(8,128)S(1)}, u32[]{:S(2)}, u32[]{:S(2)}) collective-permute-start(f32[576,256]{1,0:T(8,128)S(1)} %pad_maximum_fusion.w0), channel_id=1, source_target_pairs={{0,1},{1,0},{2,3},{3,2},{4,5},{5,4},{6,7},{7,6},{8,9},{9,8},{10,11... | collective-permute-start | bytes 1769480 | tf_op jit(solution)/shard_map/ppermute | solution.py:442
  39.3 0.7 copy-start.6
  40.0 0.9 copy-start.1
  40.9 0.9 copy-start.2
  41.8 0.9 copy-start.5
  42.7 0.9 copy-start.7
  54.1 53.9 %copy-start.10 = (f32[192,128]{1,0:T(8,128)S(1)}, f32[192,128]{1,0:T(8,128)}, u32[]{:S(2)}) copy-start(f32[192,128]{1,0:T(8,128)} %copy-done.9) | copy-start | bytes 294916
  54.1 12.5 %collective-permute-start.9 = (f32[48,128]{1,0:T(8,128)}, f32[48,128]{1,0:T(8,128)S(1)}, u32[]{:S(2)}, u32[]{:S(2)}) collective-permute-start(f32[48,128]{1,0:T(8,128)} %get-tuple-element.36), channel_id=1, source_target_pairs={{4,8},{5,9},{6,10},{7,11},{8,4},{9,5},{10,6},{11,7},{12,16},{13,17... | collective-permute-start | bytes 73736 | tf_op jit(solution)/shard_map/ppermute | solution.py:442
  54.9 11.7 %collective-permute-start.8 = (f32[48,128]{1,0:T(8,128)}, f32[48,128]{1,0:T(8,128)S(1)}, u32[]{:S(2)}, u32[]{:S(2)}) collective-permute-start(f32[48,128]{1,0:T(8,128)} %get-tuple-element.36), channel_id=1, source_target_pairs={{0,4},{1,5},{2,6},{3,7},{4,0},{5,1},{6,2},{7,3},{8,12},{9,13},{10,... | collective-permute-start | bytes 73736 | tf_op jit(solution)/shard_map/ppermute | solution.py:442
  61.0 13.8 %all-to-all-start.1 = ((f32[32,8,128]{2,1,0:T(8,128)}), f32[32,8,128]{2,1,0:T(8,128)S(1)}, u32[]{:S(2)}, u32[]{:S(2)}) async-start(f32[32,8,128]{2,1,0:T(8,128)} %copy-done.8), calls=%async_computation.1 | async-start | bytes 262144 | tf_op jit(solution)/shard_map/all_to_all | solution.py:552
  67.3 5.1 %collective-permute-start.10 = (f32[144,128]{1,0:T(8,128)S(1)}, f32[144,128]{1,0:T(8,128)S(1)}, u32[]{:S(2)}, u32[]{:S(2)}) collective-permute-start(f32[144,128]{1,0:T(8,128)S(1)} %pad_maximum_fusion.2), channel_id=1, source_target_pairs={{0,2},{1,3},{2,0},{3,1},{4,6},{5,7},{6,4},{7,5},{8,10},{9,11},{10,... | collective-permute-start | bytes 221192 | tf_op jit(solution)/shard_map/ppermute | solution.py:442
  72.4 1.4 %collective-permute-start.11 = (f32[288,128]{1,0:T(8,128)S(1)}, f32[288,128]{1,0:T(8,128)S(1)}, u32[]{:S(2)}, u32[]{:S(2)}) collective-permute-start(f32[288,128]{1,0:T(8,128)S(1)} %constant_dynamic-update-slice_fusion.q0), channel_id=1, source_target_pairs={{0,1},{1,0},{2,3},{3,2},{4,5},{5,4},{6,7},{7,6},{8,9},{9,8},{10,11... | collective-permute-start | bytes 442376 | tf_op jit(solution)/shard_map/ppermute | solution.py:442
  82.9 4.2 %collective-permute-start.13 = (f32[48,128]{1,0:T(8,128)S(1)}, f32[48,128]{1,0:T(8,128)S(1)}, u32[]{:S(2)}, u32[]{:S(2)}) collective-permute-start(f32[48,128]{1,0:T(8,128)S(1)} %get-tuple-element.38), channel_id=1, source_target_pairs={{4,8},{5,9},{6,10},{7,11},{8,4},{9,5},{10,6},{11,7},{12,16},{13,17... | collective-permute-start | bytes 73736 | tf_op jit(solution)/shard_map/ppermute | solution.py:442
  83.6 5.3 %collective-permute-start.12 = (f32[48,128]{1,0:T(8,128)S(1)}, f32[48,128]{1,0:T(8,128)S(1)}, u32[]{:S(2)}, u32[]{:S(2)}) collective-permute-start(f32[48,128]{1,0:T(8,128)S(1)} %get-tuple-element.38), channel_id=1, source_target_pairs={{0,4},{1,5},{2,6},{3,7},{4,0},{5,1},{6,2},{7,3},{8,12},{9,13},{10,... | collective-permute-start | bytes 73736 | tf_op jit(solution)/shard_map/ppermute | solution.py:442
  89.0 4.4 %collective-permute-start.14 = (f32[144,128]{1,0:T(8,128)S(1)}, f32[144,128]{1,0:T(8,128)S(1)}, u32[]{:S(2)}, u32[]{:S(2)}) collective-permute-start(f32[144,128]{1,0:T(8,128)S(1)} %pad_maximum_fusion.3), channel_id=1, source_target_pairs={{0,2},{1,3},{2,0},{3,1},{4,6},{5,7},{6,4},{7,5},{8,10},{9,11},{10,... | collective-permute-start | bytes 221192 | tf_op jit(solution)/shard_map/ppermute | solution.py:442
  93.3 1.4 %collective-permute-start.15 = (f32[288,128]{1,0:T(8,128)S(1)}, f32[288,128]{1,0:T(8,128)S(1)}, u32[]{:S(2)}, u32[]{:S(2)}) collective-permute-start(f32[288,128]{1,0:T(8,128)S(1)} %constant_dynamic-update-slice_fusion.4.q0), channel_id=1, source_target_pairs={{0,1},{1,0},{2,3},{3,2},{4,5},{5,4},{6,7},{7,6},{8,9},{9,8},{10,11... | collective-permute-start | bytes 442376 | tf_op jit(solution)/shard_map/ppermute | solution.py:442
  118.2 6.7 %collective-permute-start.17 = (f32[48,128]{1,0:T(8,128)S(1)}, f32[48,128]{1,0:T(8,128)S(1)}, u32[]{:S(2)}, u32[]{:S(2)}) collective-permute-start(f32[48,128]{1,0:T(8,128)S(1)} %get-tuple-element.48), channel_id=1, source_target_pairs={{4,8},{5,9},{6,10},{7,11},{8,4},{9,5},{10,6},{11,7},{12,16},{13,17... | collective-permute-start | bytes 73736 | tf_op jit(solution)/shard_map/ppermute | solution.py:442
  118.8 6.0 %collective-permute-start.16 = (f32[48,128]{1,0:T(8,128)S(1)}, f32[48,128]{1,0:T(8,128)S(1)}, u32[]{:S(2)}, u32[]{:S(2)}) collective-permute-start(f32[48,128]{1,0:T(8,128)S(1)} %get-tuple-element.48), channel_id=1, source_target_pairs={{0,4},{1,5},{2,6},{3,7},{4,0},{5,1},{6,2},{7,3},{8,12},{9,13},{10,... | collective-permute-start | bytes 73736 | tf_op jit(solution)/shard_map/ppermute | solution.py:442
  122.2 10.8 %all-to-all-start.3 = ((f32[32,8,128]{2,1,0:T(8,128)}), f32[32,8,128]{2,1,0:T(8,128)S(1)}, u32[]{:S(2)}, u32[]{:S(2)}) async-start(f32[32,8,128]{2,1,0:T(8,128)} %get-tuple-element.49), calls=%async_computation.3 | async-start | bytes 262144 | tf_op jit(solution)/shard_map/all_to_all | solution.py:552
  124.8 5.1 %collective-permute-start.18 = (f32[144,128]{1,0:T(8,128)S(1)}, f32[144,128]{1,0:T(8,128)S(1)}, u32[]{:S(2)}, u32[]{:S(2)}) collective-permute-start(f32[144,128]{1,0:T(8,128)S(1)} %pad_maximum_fusion.4), channel_id=1, source_target_pairs={{0,2},{1,3},{2,0},{3,1},{4,6},{5,7},{6,4},{7,5},{8,10},{9,11},{10,... | collective-permute-start | bytes 221192 | tf_op jit(solution)/shard_map/ppermute | solution.py:442
  129.9 1.4 %collective-permute-start.19 = (f32[288,128]{1,0:T(8,128)S(1)}, f32[288,128]{1,0:T(8,128)S(1)}, u32[]{:S(2)}, u32[]{:S(2)}) collective-permute-start(f32[288,128]{1,0:T(8,128)S(1)} %constant_dynamic-update-slice_fusion.8.q0), channel_id=1, source_target_pairs={{0,1},{1,0},{2,3},{3,2},{4,5},{5,4},{6,7},{7,6},{8,9},{9,8},{10,11... | collective-permute-start | bytes 442376 | tf_op jit(solution)/shard_map/ppermute | solution.py:442
  133.0 0.9 copy-start.12
  133.9 0.9 copy-start.14
  (6 other events, 3.9 us)

commit v2 on v1

v2 whole, which is shorter than its diff:
```python
import functools

import jax
import jax.numpy as jnp
from jax import lax
from jax.experimental import pallas as pl
from jax.experimental.pallas import tpu as pltpu
from jax.sharding import PartitionSpec as P

ITERATIONS = 2
AXES = ("sub", "crs")
LANES = 128
F32 = jnp.float32
BF16 = jnp.bfloat16


def with_halo(block, sides, width):
    for axis, dim in sides:
        count = lax.axis_size(axis)
        forward = [(i, i + 1) for i in range(count - 1)]
        backward = [(target, source) for source, target in forward]
        low = lax.ppermute(
            lax.slice_in_dim(block, block.shape[dim] - width, None, axis=dim), axis, forward
        )
        high = lax.ppermute(lax.slice_in_dim(block, 0, width, axis=dim), axis, backward)
        block = jnp.concatenate([low, block, high], axis=dim)
    return block


def plain(
    dual_ops, rigid_traces, coarse_factor, partner, send_list, mode_count, dual_rhs, rigid_load
):
    sub_count = dual_ops.shape[0]
    block_num = partner.shape[1]
    order_len = dual_ops.shape[2]
    block_len = order_len // block_num
    local_blocks = sub_count * block_num
    mode_num = rigid_traces.shape[1]
    links = partner.reshape(local_blocks)
    linked = (links >= 0)[:, None]
    source = jnp.maximum(links, 0)
    sending = (send_list >= 0)[:, :, None]
    picked = jnp.maximum(send_list, 0)
    mode_mask = (jnp.arange(mode_num, dtype=jnp.int32)[None, :] < mode_count[:, None]).astype(F32)

    def jump(vector):
        pieces = vector.reshape(local_blocks, block_len)
        parcels = jnp.where(sending, pieces[picked], 0.0)
        arrived = with_halo(parcels, (("sub", 0),), 1)
        incoming = jnp.concatenate([arrived[0], arrived[3]], axis=0)
        gathered = jnp.concatenate([pieces, incoming], axis=0)
        return jnp.where(linked, pieces - gathered[source], 0.0).reshape(vector.shape)

    def operator(vector):
        lowered = jump(vector).astype(BF16)
        partial_rows = jnp.einsum("srk,sk->sr", dual_ops, lowered, preferred_element_type=F32)
        full_rows = lax.all_gather(partial_rows, "crs", axis=1, tiled=True)
        return jump(full_rows)

    def restrict(vector):
        traced = jnp.einsum(
            "skm,sm->sk", rigid_traces, jump(vector), precision=lax.Precision.HIGHEST
        )
        return (traced * mode_mask).reshape(sub_count * mode_num)

    def expand(coarse_vec):
        scaled = coarse_vec.reshape(sub_count, mode_num) * mode_mask
        spread = jnp.einsum("skm,sk->sm", rigid_traces, scaled, precision=lax.Precision.HIGHEST)
        return jump(spread)

    def coarse(restricted, squares):
        column_part = jnp.dot(restricted, coarse_factor, precision=lax.Precision.HIGHEST)
        column_sum, total_sq = lax.psum((column_part, squares), "sub")
        back_part = jnp.dot(coarse_factor, column_sum, precision=lax.Precision.HIGHEST)
        solved, folded = lax.psum((back_part, jnp.sum(column_sum * column_sum)), "crs")
        return (solved, total_sq, folded)

    def project(residual):
        solved, total_sq, folded = coarse(restrict(residual), jnp.sum(residual * residual))
        return (residual - expand(solved), total_sq - folded)

    start_load = rigid_load * mode_mask.reshape(sub_count * mode_num)
    start_solved, _, _ = coarse(start_load, jnp.zeros((), F32))
    multipliers = expand(start_solved)
    residual = dual_rhs - operator(multipliers)
    projected, inner_rw = project(residual)
    direction = projected
    for _ in range(ITERATIONS):
        applied = operator(direction)
        curvature = lax.psum(jnp.sum(direction * applied), "sub")
        step_len = inner_rw / curvature
        multipliers = multipliers + step_len * direction
        residual = residual - step_len * applied
        projected, next_rw = project(residual)
        direction = projected + next_rw / inner_rw * direction
        inner_rw = next_rw
    return (multipliers, projected)


def split3(value):
    high = value.astype(BF16)
    rest = value - high.astype(F32)
    mid = rest.astype(BF16)
    low = (rest - mid.astype(F32)).astype(BF16)
    return high, mid, low


def select_dot(chooser, value):
    width = value.shape[1]
    wide = jnp.dot(
        chooser, jnp.concatenate(split3(value), axis=1), preferred_element_type=F32
    )
    return (wide[:, 2 * width :] + wide[:, width : 2 * width]) + wide[:, :width]


def one_hot(column, width):
    rows = column.shape[0]
    return (lax.broadcasted_iota(jnp.int32, (rows, width), 1) == column).astype(F32)


def repeated_one_hot(code, width):
    lane = lax.broadcasted_iota(jnp.int32, code.shape, 1)
    tiles = [(lane + at == code).astype(F32) for at in range(0, width, LANES)]
    return jnp.concatenate(tiles, axis=1)[:, :width].astype(BF16)


def floor_div(value, by, most):
    out = jnp.zeros(value.shape, jnp.int32)
    for i in range(1, most):
        out = out + (value >= i * by).astype(jnp.int32)
    return out


def total(value):
    return jnp.sum(jnp.sum(value, axis=0, keepdims=True), axis=1, keepdims=True)


class Shape:
    def __init__(self, dual_ops, rigid_traces, coarse_factor, partner, send_list):
        self.subs, self.rows, self.order = dual_ops.shape
        self.blocks = partner.shape[1]
        self.modes = rigid_traces.shape[1]
        self.slots = send_list.shape[1]
        self.crs = lax.axis_size("crs")
        self.ndev = lax.axis_size("sub") * self.crs
        self.pad = -(-self.subs // 16) * 16
        self.all_rows = self.blocks * self.pad
        self.piece_blocks = self.rows // LANES
        self.piece = self.piece_blocks * self.pad
        self.half_slots = -(-self.slots // 16) * 8
        self.planes = self.modes + 1
        self.group = 2 if self.subs % 2 == 0 else 1
        self.names_at = self.planes * self.half_slots
        self.slot_lanes = -(-2 * self.half_slots // LANES) * LANES
        self.parcel = self.names_at + 8 * (self.slot_lanes // LANES)
        self.cols = coarse_factor.shape[1]
        self.full = self.cols // LANES
        self.spot = self.cols % LANES
        self.halves = self.full + 1
        self.wide = self.halves * LANES
        self.t_rows = self.crs * self.halves
        self.tile_rows = self.modes * self.pad
        self.beside = LANES // max(self.spot, 1)
        self.rest_tiles = -(-self.modes // self.beside) if self.spot else 0
        self.factor_rows = self.full * self.tile_rows + self.rest_tiles * self.pad

    def scalar_at(self, index):
        rows = lax.broadcasted_iota(jnp.int32, (self.t_rows, LANES), 0)
        lanes = lax.broadcasted_iota(jnp.int32, (self.t_rows, LANES), 1)
        return (rows == self.halves - 1) & (lanes == self.spot + index)

    def t_mask(self):
        rows = lax.broadcasted_iota(jnp.int32, (self.t_rows, LANES), 0)
        lanes = lax.broadcasted_iota(jnp.int32, (self.t_rows, LANES), 1)
        return (rows % self.halves < self.halves - 1) | (lanes < self.spot)

    def slot_of(self, rel):
        return (rel % 2) * (self.crs // 2) + rel // 2


def rows_of(value, sh):
    return jnp.concatenate(
        [value[:, b * LANES : (b + 1) * LANES] for b in range(value.shape[1] // LANES)], axis=0
    )


def rows_of_lanes(value):
    return jnp.concatenate(
        [value[:, at : at + LANES] for at in range(0, value.shape[1], LANES)], axis=0
    )


def lanes_of(value, sh):
    return jnp.concatenate(
        [value[b * sh.pad : (b + 1) * sh.pad] for b in range(value.shape[0] // sh.pad)], axis=1
    )


def factor_tile(w_refs, sh, rel, where, at):
    slot = sh.slot_of(rel)
    xs = sh.crs // 2
    base = ((slot % xs) * 3 + where) * sh.factor_rows + at
    return w_refs[slot // xs][base : base + sh.pad, :]


def full_tile(w_refs, sh, rel, where, mode, h):
    return factor_tile(w_refs, sh, rel, where, h * sh.tile_rows + mode * sh.pad)


def rest_tile(w_refs, sh, rel, where, tile):
    return factor_tile(w_refs, sh, rel, where, sh.full * sh.tile_rows + tile * sh.pad)


def lane_group(sh, shape):
    lane = lax.broadcasted_iota(jnp.int32, shape, 1)
    return floor_div(lane, sh.spot, sh.beside + 1)


def coarse_back(w_refs, t_ref, me, sh):
    t_row, t_rest = {}, []
    lane = lax.broadcasted_iota(jnp.int32, (8, LANES), 1)
    for rel in range(sh.crs):
        at = jnp.bitwise_xor(me, rel) * sh.halves
        for h in range(sh.full):
            t_row[rel, h] = t_ref[pl.ds(at + h, 1), :]
        if sh.spot:
            rest = jnp.broadcast_to(t_ref[pl.ds(at + sh.full, 1), :], (8, LANES))
            rest = jnp.where(lane < sh.spot, rest, 0.0)
            spread = rest
            for i in range(1, sh.beside):
                spread = spread + pltpu.roll(rest, i * sh.spot, 1)
            t_rest.append(spread[:1])
    rests = {}
    for where in range(3):
        for tile in range(sh.rest_tiles):
            acc = jnp.zeros((sh.pad, LANES), F32)
            for rel in range(sh.crs):
                acc += rest_tile(w_refs, sh, rel, where, tile) * t_rest[rel]
            rests[where, tile] = acc
    group = lane_group(sh, (sh.pad, LANES)) if sh.spot else None
    columns = []
    for mode in range(sh.modes):
        parts = []
        for where in range(3):
            acc = jnp.zeros((sh.pad, LANES), F32)
            if sh.spot:
                mine = group == mode % sh.beside
                acc = jnp.where(mine, rests[where, mode // sh.beside], 0.0)
            for rel in range(sh.crs):
                for h in range(sh.full):
                    acc += full_tile(w_refs, sh, rel, where, mode, h) * t_row[rel, h]
            parts.append(
                jnp.broadcast_to(jnp.sum(acc, axis=1, keepdims=True), (sh.pad, LANES))
            )
        columns.append(jnp.concatenate(parts, axis=0))
    return jnp.concatenate(columns, axis=1)


def lift(tr_ref, pt_ref, ep_ref, w_refs, t_ref, me, sh):
    spread = coarse_back(w_refs, t_ref, me, sh)
    far = select_dot(ep_ref[...], spread)
    out = jnp.zeros((sh.all_rows, LANES), F32)
    for mode in range(sh.modes):
        own = spread[: sh.pad, mode * LANES : (mode + 1) * LANES]
        own = jnp.concatenate([own] * sh.blocks, axis=0)
        out += tr_ref[mode] * own - pt_ref[mode] * far[:, mode * LANES : (mode + 1) * LANES]
    return out


def coarse_part(value, tr_ref, pt_ref, ept_ref, w_refs, me, sh, t_out):
    at = pl.multiple_of(me * sh.piece, 16)
    own, far = [], []
    for mode in range(sh.modes):
        mine = tr_ref[mode, pl.ds(at, sh.piece), :] * value
        acc = mine[: sh.pad]
        for b in range(1, sh.piece_blocks):
            acc = acc + mine[b * sh.pad : (b + 1) * sh.pad]
        own.append(acc)
        far.append(pt_ref[mode, pl.ds(at, sh.piece), :] * value)
    moved = select_dot(ept_ref[...], jnp.concatenate(far, axis=1))
    sums, rests = {}, {}
    group = lane_group(sh, (sh.pad, LANES)) if sh.spot else None
    side = {}

    def add(table, key, term):
        table[key] = table[key] + term if key in table else term

    for mode in range(sh.modes):
        moved_k = moved[:, mode * LANES : (mode + 1) * LANES]
        for where in range(3):
            part = -moved_k[where * sh.pad : (where + 1) * sh.pad]
            if where == 0:
                part = part + own[mode]
            weight = jnp.broadcast_to(jnp.sum(part, axis=1, keepdims=True), (sh.pad, LANES))
            for rel in range(sh.crs):
                for h in range(sh.full):
                    add(sums, (rel, h), full_tile(w_refs, sh, rel, where, mode, h) * weight)
            if sh.spot:
                mine = group == mode % sh.beside
                add(side, (where, mode // sh.beside), jnp.where(mine, weight, 0.0))
    for (where, tile), weight in side.items():
        for rel in range(sh.crs):
            add(rests, rel, rest_tile(w_refs, sh, rel, where, tile) * weight)
    for rel in range(sh.crs):
        at_t = jnp.bitwise_xor(me, rel) * sh.halves
        for h in range(sh.full):
            t_out[pl.ds(at_t + h, 1), :] = jnp.sum(sums[rel, h], axis=0, keepdims=True)
        last = jnp.zeros((1, LANES), F32)
        if sh.spot:
            row = jnp.broadcast_to(jnp.sum(rests[rel], axis=0, keepdims=True), (8, LANES))
            folded = row
            for i in range(1, min(sh.beside, sh.modes)):
                folded = folded + pltpu.roll(row, LANES - i * sh.spot, 1)
            last = folded[:1]
        t_out[pl.ds(at_t + sh.full, 1), :] = last


def ops_copies(ops_hbm, ops_vmem, sems, sh):
    span = sh.group * sh.rows
    return [
        pltpu.make_async_copy(
            ops_hbm.at[pl.ds(i * span, span)], ops_vmem.at[pl.ds(i * span, span)], sems.at[i]
        )
        for i in range(sh.subs // sh.group)
    ]


def product(lowered, ops_vmem, sh, copies=None):
    row = lax.broadcasted_iota(jnp.int32, (sh.pad, sh.rows), 0)
    acc = jnp.zeros((sh.pad, sh.rows), F32)
    span = sh.group * sh.rows
    for i in range(sh.subs // sh.group):
        if copies is not None:
            copies[i].wait()
        part = lax.dot_general(
            lowered,
            ops_vmem[i * span : (i + 1) * span],
            (((1,), (1,)), ((), ())),
            preferred_element_type=F32,
        )
        for j in range(sh.group):
            acc = jnp.where(
                row == i * sh.group + j, part[:, j * sh.rows : (j + 1) * sh.rows], acc
            )
    return rows_of(acc, sh)


def sum_parcels(t_in_ref, sh):
    acc = t_in_ref[0]
    for i in range(1, sh.ndev):
        acc = acc + t_in_ref[i]
    return acc


def pick(t_sum, sh, index):
    return total(jnp.where(sh.scalar_at(index), t_sum, 0.0))


def norm2(t_vec, sh):
    return total(jnp.where(sh.t_mask(), t_vec * t_vec, 0.0))


def send_t(t_scr, scalars, sh, t_out):
    payload = jnp.where(sh.t_mask(), t_scr[...], 0.0)
    for index, value in scalars.items():
        payload = jnp.where(sh.scalar_at(index), value, payload)
    if len(t_out.shape) == 2:
        t_out[...] = payload
    else:
        for i in range(sh.ndev):
            t_out[i] = payload


def pack_kernel(
    sh, place_ref, count_ref, traces_hbm, rhs_hbm, send_hbm, load_hbm, factor_hbm,
    fields_out, parcel_a, parcel_b, factor_out, t_out,
    slot_scr, traces_ref, rhs_ref, send_ref, load_ref, factor_ref, sems,
):
    copies = [
        pltpu.make_async_copy(source, target, sems.at[i])
        for i, (source, target) in enumerate(
            (
                (factor_hbm, factor_ref),
                (load_hbm, load_ref),
                (send_hbm, send_ref),
                (rhs_hbm, rhs_ref),
                (traces_hbm, traces_ref),
            )
        )
    ]
    for copy in copies:
        copy.start()
    for copy in copies:
        copy.wait()
    me, odd = place_ref[0], place_ref[1]
    group = -(-(sh.modes + 1) // 8) * 8
    filler = jnp.zeros((group - sh.modes - 1, sh.order), F32)
    row = lax.broadcasted_iota(jnp.int32, (group, sh.order), 0)
    tiles = []
    for s in range(sh.subs):
        tile = jnp.concatenate([traces_ref[s], rhs_ref[s : s + 1, :], filler], axis=0)
        tiles.append(jnp.where((row < count_ref[s]) | (row >= sh.modes), tile, 0.0))
    by_sub = jnp.concatenate(tiles, axis=0)
    shape = ((sh.modes + 1) * sh.pad, sh.subs * group)
    out_row = lax.broadcasted_iota(jnp.int32, shape, 0)
    mode = floor_div(out_row, sh.pad, sh.modes + 1)
    sub = out_row - mode * sh.pad
    hit = lax.broadcasted_iota(jnp.int32, shape, 1) == sub * group + mode
    order = jnp.where(hit & (sub < sh.subs), 1.0, 0.0).astype(BF16)
    by_mode = select_dot(order, by_sub)
    fields = []
    for k in range(sh.modes + 1):
        fields.append(rows_of(by_mode[k * sh.pad : (k + 1) * sh.pad], sh))
        fields_out[k] = fields[k]
    fields = jnp.concatenate(fields, axis=1)

    shape = (sh.tile_rows, sh.subs * sh.modes)
    out_row = lax.broadcasted_iota(jnp.int32, shape, 0)
    mode = floor_div(out_row, sh.pad, sh.modes)
    sub = out_row - mode * sh.pad
    hit = lax.broadcasted_iota(jnp.int32, shape, 1) == sub * sh.modes + mode
    order = jnp.where(hit & (sub < sh.subs), 1.0, 0.0).astype(BF16)
    factor = select_dot(order, factor_ref[...])
    factor = jnp.concatenate(
        [factor, jnp.zeros((sh.tile_rows, sh.wide - sh.cols), F32)], axis=1
    )
    tiles = [factor[:, h * LANES : (h + 1) * LANES] for h in range(sh.full)]
    rest = factor[:, sh.full * LANES :]
    for tile in range(sh.rest_tiles):
        side = jnp.zeros((sh.pad, LANES), F32)
        for i in range(min(sh.beside, sh.modes - tile * sh.beside)):
            mode = tile * sh.beside + i
            part = rest[mode * sh.pad : (mode + 1) * sh.pad]
            side = side + (pltpu.roll(part, i * sh.spot, 1) if i else part)
        tiles.append(side)
    factor = jnp.concatenate(tiles, axis=0)
    factor_out[...] = factor

    width = sh.slot_lanes
    lists = send_ref[...].astype(F32)
    lists = jnp.concatenate([lists, jnp.full((2, width - sh.slots), -1.0, F32)], axis=1)
    lists = jnp.concatenate([lists, jnp.full((6, width), -1.0, F32)], axis=0).astype(jnp.int32)
    sub = floor_div(lists, sh.blocks, sh.subs)
    lists = jnp.where(lists >= 0, (lists - sub * sh.blocks) * sh.pad + sub, -1).astype(F32)
    turned = jnp.transpose(lists)
    at = pl.multiple_of((me % 2) * sh.half_slots, 8)
    for out, row in ((parcel_a, 1 - odd), (parcel_b, odd)):
        names = jnp.where(row == 0, lists[0:1], lists[1:2])
        column = jnp.where(row == 0, turned[:, 0:1], turned[:, 1:2])
        slot_scr[...] = jnp.broadcast_to(column, (width, LANES))
        line = slot_scr[pl.ds(at, sh.half_slots), :].astype(jnp.int32)
        picked = select_dot(repeated_one_hot(line, sh.all_rows), fields)
        for k in range(sh.planes):
            out[k * sh.half_slots : (k + 1) * sh.half_slots, :] = picked[
                :, k * LANES : (k + 1) * LANES
            ]
        for i in range(width // LANES):
            out[sh.names_at + 8 * i : sh.names_at + 8 * (i + 1), :] = jnp.broadcast_to(
                names[:, i * LANES : (i + 1) * LANES], (8, LANES)
            )
        out[sh.parcel :, :] = factor

    lane = lax.broadcasted_iota(jnp.int32, (8, sh.subs * sh.modes), 1)
    kept = lane < 0
    for s in range(sh.subs):
        kept = kept | ((lane >= s * sh.modes) & (lane < s * sh.modes + count_ref[s]))
    load = jnp.where(kept, jnp.broadcast_to(load_ref[...], kept.shape), 0.0)
    part = jnp.dot(
        load, factor_ref[...], preferred_element_type=F32, precision=lax.Precision.HIGHEST
    )
    part = jnp.concatenate([part, jnp.zeros((8, sh.wide - sh.cols), F32)], axis=1)[:1]
    payload = rows_of_lanes(part)
    for i in range(sh.ndev):
        t_out[i] = payload


def setup_kernel(
    sh, place_ref, partner_ref, fields_ref, near_a, near_b, core_ref,
    tr_out, pt_out, jump_out, ep_out, ept_out, sub_scr,
):
    me, odd = place_ref[0], place_ref[1]
    codes = partner_ref[...]
    codes = jnp.concatenate(
        [codes, jnp.full((sh.pad - sh.subs, sh.blocks), -1, jnp.int32)], axis=0
    )
    code = jnp.concatenate(
        [jnp.broadcast_to(codes[:, b : b + 1], (sh.pad, LANES)) for b in range(sh.blocks)], axis=0
    )
    local_blocks = sh.subs * sh.blocks
    linked = code >= 0
    is_own = linked & (code < local_blocks)
    before = (code >= local_blocks) & (code < local_blocks + sh.slots)
    after = code >= local_blocks + sh.slots
    is_a = (before & (odd == 1)) | (after & (odd == 0))
    slot = jnp.where(before, code - local_blocks, code - local_blocks - sh.slots)
    upper = (slot >= sh.half_slots).astype(jnp.int32)
    other = jnp.where(upper == me % 2, 0, 1)
    own_sub = floor_div(code, sh.blocks, sh.subs)
    line = (code - own_sub * sh.blocks) * sh.pad + own_sub
    source = jnp.where(
        is_own,
        line,
        sh.all_rows
        + other * 2 * sh.half_slots
        + jnp.where(is_a, 0, sh.half_slots)
        + (slot - upper * sh.half_slots),
    )
    source = jnp.where(linked, source, -1)
    chooser = repeated_one_hot(source, sh.all_rows + 4 * sh.half_slots)
    columns = []
    for k in range(sh.planes):
        rows = slice(k * sh.half_slots, (k + 1) * sh.half_slots)
        rows_b = slice(sh.names_at + k * sh.half_slots, sh.names_at + (k + 1) * sh.half_slots)
        columns.append(
            jnp.concatenate(
                [
                    fields_ref[k], near_a[rows, :], near_b[rows, :],
                    core_ref[rows, :], core_ref[rows_b, :],
                ],
                axis=0,
            )
        )
    far = select_dot(chooser, jnp.concatenate(columns, axis=1))
    live = linked.astype(F32)
    for k in range(sh.modes + 1):
        far_k = far[:, k * LANES : (k + 1) * LANES]
        if k < sh.modes:
            tr_out[k] = fields_ref[k] * live
            pt_out[k] = far_k
        else:
            tr_out[k] = fields_ref[k]
            pt_out[k] = fields_ref[k] * live - far_k

    names = []
    for ref in (near_a, near_b):
        parts = []
        for i in range(sh.slot_lanes // LANES):
            tile = ref[sh.names_at + 8 * i : sh.names_at + 8 * (i + 1), :]
            parts.append(jnp.broadcast_to(jnp.transpose(tile)[:, 0:1], (LANES, LANES)))
        names.append(jnp.concatenate(parts, axis=0))
    named = select_dot(
        repeated_one_hot(slot, sh.slot_lanes), jnp.concatenate(names, axis=1)
    ).astype(jnp.int32)
    far_line = jnp.where(is_own, line, jnp.where(is_a, named[:, :LANES], named[:, LANES:]))
    wide = (sh.all_rows, LANES)
    own_line = lax.broadcasted_iota(jnp.int32, wide, 0)

    def piece_row(block, sub, where):
        member = floor_div(block, sh.piece_blocks, sh.crs)
        place = sh.slot_of(jnp.bitwise_xor(member, me)) * 3 + where
        return place * sh.piece + (block - member * sh.piece_blocks) * sh.pad + sub

    def split(value):
        block = floor_div(value, sh.pad, sh.blocks)
        return block, value - block * sh.pad

    far_block, far_sub = split(far_line)
    own_block, own_sub = split(own_line)
    where = jnp.where(is_own, 0, jnp.where(is_a, 1, 2))
    own_col = jnp.where(linked, piece_row(own_block, own_sub, 0), -1)
    far_col = jnp.where(linked, piece_row(far_block, far_sub, where), -1)
    columns = 3 * sh.crs * sh.piece
    jump_out[...] = repeated_one_hot(own_col, columns) - repeated_one_hot(far_col, columns)
    far_sub = jnp.where(linked, where * sh.pad + far_sub, -1)
    pick_far = repeated_one_hot(far_sub, 3 * sh.pad)
    ep_out[...] = pick_far
    sub_scr[...] = far_sub.astype(F32)
    mine = sub_scr[pl.ds(pl.multiple_of(me * sh.piece, 16), sh.piece), :]
    mine = jnp.transpose(mine)[: 3 * sh.pad] if 3 * sh.pad <= LANES else jnp.transpose(mine)
    row = lax.broadcasted_iota(jnp.int32, (3 * sh.pad, sh.piece), 0).astype(F32)
    ept_out[...] = jnp.where(mine[:1] == row, 1.0, 0.0).astype(BF16)


def first_kernel(
    sh, place_ref, tr_ref, pt_ref, ep_ref, ept_ref, t_in, w0, w1, ops_hbm,
    lam_out, q_out, t_out, t_scr, ops_vmem, sems,
):
    copies = ops_copies(ops_hbm, ops_vmem, sems, sh)
    for copy in copies:
        copy.start()
    me = place_ref[0]
    w_refs = (w0, w1)
    for j in range(sh.crs):
        acc = t_in[j]
        for i in range(j + sh.crs, sh.ndev, sh.crs):
            acc = acc + t_in[i]
        t_scr[j * sh.halves : (j + 1) * sh.halves, :] = acc
    lam = lift(tr_ref, pt_ref, ep_ref, w_refs, t_scr, me, sh)
    lam_out[...] = lam
    q = product(lanes_of(2.0 * lam, sh).astype(BF16), ops_vmem, sh, copies)
    q_out[...] = q
    at = pl.multiple_of(me * sh.piece, 16)
    value = tr_ref[sh.modes, pl.ds(at, sh.piece), :] - 2.0 * q
    coarse_part(value, tr_ref, pt_ref, ept_ref, w_refs, me, sh, t_scr)
    send_t(t_scr, {}, sh, t_out)


def second_kernel(
    sh, place_ref, tr_ref, pt_ref, jump_ref, ep_ref, ept_ref, q0, q1, t_in, w0, w1, ops_hbm,
    state_ref, tr0_out, q_out, t_out, ops_out, t_scr, sems,
):
    copies = ops_copies(ops_hbm, ops_out, sems, sh)
    for copy in copies:
        copy.start()
    me = place_ref[0]
    w_refs = (w0, w1)
    applied = select_dot(jump_ref[...], jnp.concatenate([q0[...], q1[...]], axis=0))
    tr0_out[...] = sum_parcels(t_in, sh)
    back = lift(tr_ref, pt_ref, ep_ref, w_refs, tr0_out, me, sh)
    residual = tr_ref[sh.modes] - applied
    jump_r = pt_ref[sh.modes] - 2.0 * applied
    jump_d = jump_r - 2.0 * back
    state_ref[0] = residual
    state_ref[1] = jump_r
    state_ref[2] = residual - back
    state_ref[3] = jump_d
    q = product(lanes_of(jump_d, sh).astype(BF16), ops_out, sh, copies)
    q_out[...] = q
    coarse_part(2.0 * q, tr_ref, pt_ref, ept_ref, w_refs, me, sh, t_scr)
    mine = pl.ds(pl.multiple_of(me * sh.piece, 16), sh.piece)
    own_r = state_ref[0, mine, :]
    send_t(
        t_scr,
        {
            0: total(state_ref[3, mine, :] * q),
            1: total(state_ref[1, mine, :] * q),
            2: total(own_r * own_r),
        },
        sh,
        t_out,
    )


def square_kernel(sh, place_ref, jump_ref, q0, q1, t_in, applied_out, t_out):
    me = place_ref[0]
    applied_out[...] = select_dot(jump_ref[...], jnp.concatenate([q0[...], q1[...]], axis=0))
    at = pl.multiple_of(me * sh.piece, 16)
    mine = applied_out[pl.ds(at, sh.piece), :]
    payload = jnp.where(sh.scalar_at(3), total(mine * mine), t_in[...])
    for i in range(sh.ndev):
        t_out[i] = payload


def third_kernel(
    sh, place_ref, tr_ref, pt_ref, ep_ref, ept_ref, applied_ref, t_in, w0, w1, tr0_ref,
    state_ref, lam_ref, ops_ref,
    next_out, tr1_out, q_out, t_out, t_scr, jd_scr,
):
    me = place_ref[0]
    w_refs = (w0, w1)
    sums = sum_parcels(t_in, sh)
    tr0 = tr0_ref[...]
    d_a, r_a, r_r, a_a = (pick(sums, sh, i) for i in range(4))
    rw0 = r_r - norm2(tr0, sh)
    alpha = rw0 / d_a
    tr1 = tr0 - alpha * sums
    rw1 = (r_r - 2.0 * alpha * r_a + alpha * alpha * a_a) - norm2(tr1, sh)
    beta = rw1 / rw0
    tr1_out[...] = jnp.where(sh.scalar_at(0), rw1, tr1)
    back = lift(tr_ref, pt_ref, ep_ref, w_refs, tr1_out, me, sh)
    applied = applied_ref[...]
    direction = state_ref[2]
    jump_d = (state_ref[1] - 2.0 * alpha * applied - 2.0 * back) + beta * state_ref[3]
    jd_scr[...] = jump_d
    residual = state_ref[0] - alpha * applied
    next_out[0] = residual
    next_out[1] = (residual - back) + beta * direction
    next_out[2] = lam_ref[...] + alpha * direction
    q = product(lanes_of(jump_d, sh).astype(BF16), ops_ref, sh)
    q_out[...] = q
    coarse_part(2.0 * q, tr_ref, pt_ref, ept_ref, w_refs, me, sh, t_scr)
    at = pl.multiple_of(me * sh.piece, 16)
    send_t(t_scr, {0: total(jd_scr[pl.ds(at, sh.piece), :] * q)}, sh, t_out)


def last_kernel(
    sh, place_ref, tr_ref, pt_ref, jump_ref, ep_ref, q0, q1, t_in, w0, w1, tr1_ref, state_ref,
    lam_out, p_out, t_scr,
):
    me = place_ref[0]
    sums = sum_parcels(t_in, sh)
    tr1 = tr1_ref[...]
    alpha = pick(tr1, sh, 0) / pick(sums, sh, 0)
    t_scr[...] = tr1 - alpha * sums
    applied = select_dot(jump_ref[...], jnp.concatenate([q0[...], q1[...]], axis=0))
    back = lift(tr_ref, pt_ref, ep_ref, (w0, w1), t_scr, me, sh)
    lam = state_ref[2] + alpha * state_ref[1]
    projected = (state_ref[0] - alpha * applied) - back
    lam_out[...] = lanes_of(lam, sh)[: sh.subs]
    p_out[...] = lanes_of(projected, sh)[: sh.subs]


def permute(value, move):
    sub_num, crs_num = lax.axis_size("sub"), lax.axis_size("crs")
    pairs = []
    for i in range(sub_num):
        for j in range(crs_num):
            to_i, to_j = move(i, j)
            if 0 <= to_i < sub_num:
                pairs.append((i * crs_num + j, to_i * crs_num + to_j))
    return lax.ppermute(value, AXES, pairs)


def swap_a(value):
    return permute(value, lambda i, j: (i ^ 1, j))


def swap_b(value):
    return permute(value, lambda i, j: (((i + 1) ^ 1) - 1, j))


def core_swap(value):
    return permute(value, lambda i, j: (i, j ^ 1))


def x_swaps(value):
    return [
        permute(value, lambda i, j: (i, j ^ (2 * shift)))
        for shift in range(1, lax.axis_size("crs") // 2)
    ]


def spread_pieces(value):
    near = jnp.concatenate([value, swap_a(value), swap_b(value)], axis=0)
    first = jnp.concatenate([near] + x_swaps(near), axis=0)
    return first, core_swap(first)


def local(
    dual_ops, rigid_traces, coarse_factor, partner, send_list, mode_count, dual_rhs, rigid_load
):
    sh = Shape(dual_ops, rigid_traces, coarse_factor, partner, send_list)
    modes, subs = sh.modes, sh.subs
    place = jnp.stack([lax.axis_index("crs"), lax.axis_index("sub") % 2]).astype(jnp.int32)

    vmem = pl.BlockSpec(memory_space=pltpu.VMEM)
    smem = pl.BlockSpec(memory_space=pltpu.SMEM)
    hbm = pl.BlockSpec(memory_space=pltpu.HBM)

    tags = {"v": vmem, "k": vmem, "s": smem, "h": hbm}

    def call(kernel, ins, outs, scratch, *operands, name, cost):
        operands = [
            pltpu.with_memory_space_constraint(x, pltpu.HBM) if tag == "h" else x
            for tag, x in zip(ins, operands)
        ]
        return pl.pallas_call(
            functools.partial(kernel, sh),
            out_shape=[
                pltpu.VMEM(s, t) if tag == "k" else jax.ShapeDtypeStruct(s, t)
                for tag, s, t in outs
            ],
            in_specs=[smem] + [tags[tag] for tag in ins],
            out_specs=[tags[tag] for tag, _, _ in outs],
            scratch_shapes=scratch,
            compiler_params=pltpu.CompilerParams(vmem_limit_bytes=24 * 1024 * 1024),
            cost_estimate=pl.CostEstimate(flops=0, bytes_accessed=cost, transcendentals=0),
            name=name,
        )(place, *operands)

    rows = (sh.all_rows, LANES)
    t_shape = ("v", (sh.t_rows, LANES), F32)
    parcels = ("v", (sh.ndev, sh.t_rows, LANES), F32)
    columns = ("v", (sh.ndev, sh.halves, LANES), F32)
    q_shape = ("v", (sh.piece, LANES), F32)
    field_shape = ("v", (modes + 1,) + rows, F32)
    t_scratch = pltpu.VMEM((sh.t_rows, LANES), F32)
    ops = dual_ops.reshape(subs * sh.rows, sh.order)
    ops_kept = ("k", ops.shape, BF16)
    ops_sems = subs // sh.group
    long = dual_ops.size * 2

    def exchange(parcel):
        return lax.all_to_all(parcel, AXES, 0, 0)

    def stack(count):
        return (count,) + rows

    parcel_shape = ("v", (sh.parcel + sh.factor_rows, LANES), F32)
    raw = (rigid_traces, dual_rhs, send_list, rigid_load[None, :], coarse_factor)
    fields, parcel_a, parcel_b, factor, t_part = call(
        pack_kernel, "shhhhh",
        [field_shape, parcel_shape, parcel_shape, ("v", (sh.factor_rows, LANES), F32), columns],
        [pltpu.VMEM((sh.slot_lanes, LANES), F32)]
        + [pltpu.VMEM(x.shape, x.dtype) for x in raw]
        + [pltpu.SemaphoreType.DMA((len(raw),))],
        mode_count, *raw, name="pack", cost=8_000_000,
    )
    near_a, near_b = swap_a(parcel_a), swap_b(parcel_b)
    factor_x = x_swaps(factor)
    t_part, near_b = lax.optimization_barrier((t_part, near_b))
    t_in = exchange(t_part)
    halves = core_swap(jnp.concatenate([near_a[: sh.names_at], near_b[: sh.names_at]], axis=0))
    factor_ab = jnp.concatenate([near_a[sh.parcel :], near_b[sh.parcel :]], axis=0)
    w0 = [factor, factor_ab]
    for own, pair in zip(factor_x, x_swaps(factor_ab)):
        w0 += [own, pair]
    traces, far_traces, jumper, far_pick, far_put = call(
        setup_kernel, "vvvvv",
        [
            field_shape, field_shape,
            ("v", (sh.all_rows, 3 * sh.crs * sh.piece), BF16),
            ("v", (sh.all_rows, 3 * sh.pad), BF16),
            ("v", (3 * sh.pad, sh.piece), BF16),
        ],
        [pltpu.VMEM(rows, F32)],
        partner, fields, near_a, near_b, halves, name="setup", cost=6_000_000,
    )
    rider = jnp.concatenate([t_in[0, :1], far_traces[0, :7]], axis=0)
    w0 = jnp.concatenate(w0 + [rider], axis=0)
    w1 = core_swap(w0)
    lam0, q, t_part = call(
        first_kernel, "vvvvvvvh",
        [("v", rows, F32), q_shape, parcels],
        [t_scratch, pltpu.VMEM(ops.shape, BF16), pltpu.SemaphoreType.DMA((ops_sems,))],
        traces, far_traces, far_pick, far_put, t_in, w0, w1, ops, name="first", cost=long,
    )
    q0, q1 = spread_pieces(q)
    t_in = exchange(t_part)

    state0, tr0, q, t_part, ops_vmem = call(
        second_kernel, "vvvvvvvvvvh",
        [("v", stack(4), F32), t_shape, q_shape, t_shape, ops_kept],
        [t_scratch, pltpu.SemaphoreType.DMA((ops_sems,))],
        traces, far_traces, jumper, far_pick, far_put, q0, q1, t_in, w0, w1, ops,
        name="second", cost=long,
    )
    q0, q1 = spread_pieces(q)
    applied, t_part = call(
        square_kernel, "vvvv", [("v", rows, F32), parcels], [],
        jumper, q0, q1, t_part, name="square", cost=2_000_000,
    )
    t_in = exchange(t_part)

    state1, tr1, q, t_part = call(
        third_kernel, "vvvvvvvvvvvv",
        [("v", stack(3), F32), t_shape, q_shape, parcels],
        [t_scratch, pltpu.VMEM(rows, F32)],
        traces, far_traces, far_pick, far_put, applied, t_in, w0, w1, tr0, state0, lam0, ops_vmem,
        name="third", cost=long,
    )
    q0, q1 = spread_pieces(q)
    t_in = exchange(t_part)

    return tuple(
        call(
            last_kernel, "vvvvvvvvvvv",
            [("v", (subs, sh.order), F32)] * 2,
            [t_scratch],
            traces, far_traces, jumper, far_pick, q0, q1, t_in, w0, w1, tr1, state1,
            name="last", cost=4_000_000,
        )
    )


def body(*args):
    dual_ops, _, _, partner = args[:4]
    crs_num, sub_num = lax.axis_size("crs"), lax.axis_size("sub")
    whole_blocks = (
        dual_ops.shape[2] // partner.shape[1] == LANES and dual_ops.shape[1] % LANES == 0
    )
    fits = whole_blocks and args[2].shape[1] % LANES + 8 <= LANES
    if fits and crs_num % 2 == 0 and crs_num & (crs_num - 1) == 0 and sub_num % 2 == 0:
        return local(*args)
    return plain(*args)


def solution(mesh):
    return jax.shard_map(
        body,
        mesh=mesh,
        in_specs=(
            P("sub", "crs", None),
            P("sub", None, None),
            P("sub", "crs"),
            P("sub", None),
            P("sub", None),
            P("sub"),
            P("sub", None),
            P("sub"),
        ),
        out_specs=(P("sub", None), P("sub", None)),
        check_vma=False,
    )
```

time: 137 us -> 115 us (0.84)
  local copies, waits for them, and re-layouts: 16.3 us -> 2.3 us
  starting transfers between devices: 46.4 us -> 39.7 us
  other arithmetic: 4.49 us -> 0.13 us
  Pallas kernels: 29.2 us -> 32.5 us
    unnamed x40 -> x13, local copies, waits for them, and re-layouts: 12.6 us -> 1.38 us
    ppermute x20 -> x18, starting transfers between devices: 34.6 us -> 26.5 us  [permute(): return lax.ppermute(value, AXES, pairs)]
    all_to_all x3, waiting for transfers between devices: 2.75 us -> 8.61 us  [exchange(): return lax.all_to_all(parcel, AXES, 0, 0)]
    ppermute x20 -> x18, waiting for transfers between devices: 23.2 us -> 17.8 us  [permute(): return lax.ppermute(value, AXES, pairs)]
    pallas_call x6 -> x7, Pallas kernels: 29.2 us -> 32.5 us  [call(): pl.pallas_call(functools.partial(kernel, sh), out_shape=[pltpu.VMEM(s, t)...]
    mul x2 -> x0, other arithmetic: 1.83 us -> none  [the longest x1 1.17 us: local(): rigid_traces * mode_mask[:, :, None]]
    all_to_all x3, starting transfers between devices: 11.8 us -> 13.2 us  [exchange(): return lax.all_to_all(parcel, AXES, 0, 0)]
  transfers between devices with their start and end apart: 23 -> 21, of which waited for: 10 -> 11; matrix products, arithmetic and copies ran while one was open for 6% -> 0% of each run, Pallas kernels for 1% -> 2%
where the time goes in v2:
time: 115 us; the launch traced here: 114 us
  starting transfers between devices  39.7 us (35%)
  Pallas kernels  32.5 us (28%)
  waiting for transfers between devices  26.4 us (23%)
  blocking collectives  12.5 us (11%)
  local copies, waits for them, and re-layouts  2.3 us (2%)
    pallas_call x7, Pallas kernels, call(): pl.pallas_call(functools.partial(kernel, sh), out_shape=[pltpu.VMEM(s, t)...  32.5 us
    ppermute x18, starting transfers between devices, permute(): return lax.ppermute(value, AXES, pairs)  26.5 us
    ppermute x18, waiting for transfers between devices, permute(): return lax.ppermute(value, AXES, pairs)  17.8 us
    all_to_all x3, starting transfers between devices, exchange(): return lax.all_to_all(parcel, AXES, 0, 0)  13.2 us
    all_to_all x1, blocking collectives, exchange(): return lax.all_to_all(parcel, AXES, 0, 0)  12.5 us
    all_to_all x3, waiting for transfers between devices, exchange(): return lax.all_to_all(parcel, AXES, 0, 0)  8.61 us
  transfers between devices with their start and end apart: 21, of which 11 were waited for; matrix products, arithmetic and copies ran while one was open for 0% of the time, Pallas kernels for 2%

profile of v2, /device:TPU:0, one launch (start us, length us, event | category | flops | bytes accessed | tf_op | source)
XLA Modules:
  0.0 114.4 jit_solution(7775331325590536057)
XLA Ops:
  1.4 3.4 %pack.1 = (f32[7,192,128]{2,1,0:T(8,128)S(1)}, f32[400,128]{1,0:T(8,128)S(1)}, f32[400,128]{1,0:T(8,128)S(1)}, f32[112,128]{1,0:T(8,128)S(1)}, f32[32,2,128]{2,1,0:T(2,128)}) custom-call(s32[2]{0:T(128)S(1)} %pad_add_fusion.place_ref, s32[12]{0:T(128)S(1)} %copy-done.1, f32[12,6,1536]{2,1,0:T(8,128)} %traces_hbm.1, f32[12,1536]{1,0:T(8,128)} %rhs_hbm.1, ...), custom_call_target="tpu_custom_call" | custom-call | bytes 8000000 | tf_op jit(solution)/shard_map/pack/pallas_call | solution.py:747
  5.5 5.8 %collective-permute-start = (f32[400,128]{1,0:T(8,128)S(1)}, f32[400,128]{1,0:T(8,128)S(1)}, u32[]{:S(2)}, u32[]{:S(2)}) collective-permute-start(f32[400,128]{1,0:T(8,128)S(1)} %get-tuple-element.29), channel_id=1, source_target_pairs={{0,4},{1,5},{2,6},{3,7},{4,0},{5,1},{6,2},{7,3},{8,12},{9,13},{10,... | collective-permute-start | bytes 614408 | tf_op jit(solution)/shard_map/ppermute | solution.py:701
  11.2 1.5 %collective-permute-start.3 = (f32[112,128]{1,0:T(8,128)S(1)}, f32[112,128]{1,0:T(8,128)}, u32[]{:S(2)}, u32[]{:S(2)}) collective-permute-start(f32[112,128]{1,0:T(8,128)S(1)} %get-tuple-element.39), channel_id=1, source_target_pairs={{0,2},{1,3},{2,0},{3,1},{4,6},{5,7},{6,4},{7,5},{8,10},{9,11},{10,... | collective-permute-start | bytes 172040 | tf_op jit(solution)/shard_map/ppermute | solution.py:701
  12.8 8.1 %all-to-all-start = ((f32[32,2,128]{2,1,0:T(2,128)}), f32[32,2,128]{2,1,0:T(2,128)S(1)}, u32[]{:S(2)}, u32[]{:S(2)}) async-start(f32[32,2,128]{2,1,0:T(2,128)} %get-tuple-element.38), calls=%async_computation | async-start | bytes 65536 | tf_op jit(solution)/shard_map/all_to_all | solution.py:774
  21.2 1.7 %collective-permute-start.4 = (f32[224,128]{1,0:T(8,128)S(1)}, f32[224,128]{1,0:T(8,128)S(1)}, u32[]{:S(2)}, u32[]{:S(2)}) collective-permute-start(f32[224,128]{1,0:T(8,128)S(1)} %pad_maximum_fusion.1), channel_id=1, source_target_pairs={{0,2},{1,3},{2,0},{3,1},{4,6},{5,7},{6,4},{7,5},{8,10},{9,11},{10,... | collective-permute-start | bytes 344072 | tf_op jit(solution)/shard_map/ppermute | solution.py:701
  23.0 5.1 %all-to-all-done.t_in = f32[32,2,128]{2,1,0:T(2,128)S(1)} async-done(((f32[32,2,128]{2,1,0:T(2,128)}), f32[32,2,128]{2,1,0:T(2,128)S(1)}, u32[]{:S(2)}, u32[]{:S(2)}) %all-to-all-start) | async-done | bytes 32800 | tf_op jit(solution)/shard_map/all_to_all | solution.py:774
  28.8 2.2 %setup.1 = (f32[7,192,128]{2,1,0:T(8,128)S(1)}, f32[7,192,128]{2,1,0:T(8,128)S(1)}, bf16[192,576]{1,0:T(8,128)(2,1)S(1)}, bf16[192,48]{1,0:T(8,128)(2,1)S(1)}, bf16[48,48]{1,0:T(8,128)(2,1)S(1)}) custom-call(s32[2]{0:T(128)S(1)} %pad_add_fusion.place_ref, s32[12,12]{1,0:T(8,128)S(1)} %copy-done, f32[7,192,128]{2,1,0:T(8,128)S(1)} %get-tuple-element.28.fields_ref, ...), custom_call_target="tpu_custom_call" | custom-call | bytes 6000000 | tf_op jit(solution)/shard_map/setup/pallas_call | solution.py:747
  31.0 0.9 concatenate.33.w0
  32.1 1.5 %collective-permute-done.5.w1 = f32[680,128]{1,0:T(8,128)S(1)} collective-permute-done((f32[680,128]{1,0:T(8,128)S(1)}, f32[680,128]{1,0:T(8,128)S(1)}, u32[]{:S(2)}, u32[]{:S(2)}) %collective-permute-start.5) | collective-permute-done | bytes 348192 | tf_op jit(solution)/shard_map/ppermute | solution.py:701
  33.6 9.4 %first.1 = (f32[192,128]{1,0:T(8,128)S(1)}, f32[48,128]{1,0:T(8,128)S(1)}, f32[32,8,128]{2,1,0:T(8,128)}) custom-call(s32[2]{0:T(128)S(1)} %pad_add_fusion.place_ref, f32[7,192,128]{2,1,0:T(8,128)S(1)} %get-tuple-element.33.tr_ref, f32[7,192,128]{2,1,0:T(8,128)S(1)} %get-tuple-element.34.pt_ref, bf16[192,48]{1,0:T(8,128)(2,1)S(1)} %get-tuple-element.36.ep_ref, ...), custom_call_target="tpu_custom_call" | custom-call | bytes 14155776 | tf_op jit(solution)/shard_map/first/pallas_call | solution.py:747
  43.7 3.4 %collective-permute-start.6 = (f32[48,128]{1,0:T(8,128)S(1)}, f32[48,128]{1,0:T(8,128)S(1)}, u32[]{:S(2)}, u32[]{:S(2)}) collective-permute-start(f32[48,128]{1,0:T(8,128)S(1)} %get-tuple-element.40), channel_id=1, source_target_pairs={{0,4},{1,5},{2,6},{3,7},{4,0},{5,1},{6,2},{7,3},{8,12},{9,13},{10,... | collective-permute-start | bytes 73736 | tf_op jit(solution)/shard_map/ppermute | solution.py:701
  47.1 2.6 %all-to-all-start.1 = ((f32[32,8,128]{2,1,0:T(8,128)}), f32[32,8,128]{2,1,0:T(8,128)S(1)}, u32[]{:S(2)}, u32[]{:S(2)}) async-start(f32[32,8,128]{2,1,0:T(8,128)} %get-tuple-element.41), calls=%async_computation.1 | async-start | bytes 262144 | tf_op jit(solution)/shard_map/all_to_all | solution.py:774
  49.7 1.7 %collective-permute-start.8 = (f32[144,128]{1,0:T(8,128)S(1)}, f32[144,128]{1,0:T(8,128)S(1)}, u32[]{:S(2)}, u32[]{:S(2)}) collective-permute-start(f32[144,128]{1,0:T(8,128)S(1)} %pad_maximum_fusion.2), channel_id=1, source_target_pairs={{0,2},{1,3},{2,0},{3,1},{4,6},{5,7},{6,4},{7,5},{8,10},{9,11},{10,... | collective-permute-start | bytes 221192 | tf_op jit(solution)/shard_map/ppermute | solution.py:701
  51.4 3.4 %collective-permute-done.8 = f32[144,128]{1,0:T(8,128)S(1)} collective-permute-done((f32[144,128]{1,0:T(8,128)S(1)}, f32[144,128]{1,0:T(8,128)S(1)}, u32[]{:S(2)}, u32[]{:S(2)}) %collective-permute-start.8) | collective-permute-done | bytes 73760 | tf_op jit(solution)/shard_map/ppermute | solution.py:701
  54.8 1.4 %collective-permute-done.9.q1 = f32[288,128]{1,0:T(8,128)S(1)} collective-permute-done((f32[288,128]{1,0:T(8,128)S(1)}, f32[288,128]{1,0:T(8,128)S(1)}, u32[]{:S(2)}, u32[]{:S(2)}) %collective-permute-start.9) | collective-permute-done | bytes 147488 | tf_op jit(solution)/shard_map/ppermute | solution.py:701
  56.2 1.8 %all-to-all-done.1.t_in = f32[32,8,128]{2,1,0:T(8,128)S(1)} async-done(((f32[32,8,128]{2,1,0:T(8,128)}), f32[32,8,128]{2,1,0:T(8,128)S(1)}, u32[]{:S(2)}, u32[]{:S(2)}) %all-to-all-start.1) | async-done | bytes 131104 | tf_op jit(solution)/shard_map/all_to_all | solution.py:774
  57.9 8.4 %second.1 = (f32[4,192,128]{2,1,0:T(8,128)S(1)}, f32[8,128]{1,0:T(8,128)S(1)}, f32[48,128]{1,0:T(8,128)S(1)}, f32[8,128]{1,0:T(8,128)S(1)}, bf16[4608,1536]{1,0:T(8,128)(2,1)S(1)}) custom-call(s32[2]{0:T(128)S(1)} %pad_add_fusion.place_ref, f32[7,192,128]{2,1,0:T(8,128)S(1)} %get-tuple-element.33.tr_ref, f32[7,192,128]{2,1,0:T(8,128)S(1)} %get-tuple-element.34.pt_ref, ...), custom_call_target="tpu_custom_call" | custom-call | bytes 14155776 | tf_op jit(solution)/shard_map/second/pallas_call | solution.py:747
  67.0 3.4 %collective-permute-start.10 = (f32[48,128]{1,0:T(8,128)S(1)}, f32[48,128]{1,0:T(8,128)S(1)}, u32[]{:S(2)}, u32[]{:S(2)}) collective-permute-start(f32[48,128]{1,0:T(8,128)S(1)} %get-tuple-element.42), channel_id=1, source_target_pairs={{0,4},{1,5},{2,6},{3,7},{4,0},{5,1},{6,2},{7,3},{8,12},{9,13},{10,... | collective-permute-start | bytes 73736 | tf_op jit(solution)/shard_map/ppermute | solution.py:701
  70.4 1.8 %collective-permute-done.10 = f32[48,128]{1,0:T(8,128)S(1)} collective-permute-done((f32[48,128]{1,0:T(8,128)S(1)}, f32[48,128]{1,0:T(8,128)S(1)}, u32[]{:S(2)}, u32[]{:S(2)}) %collective-permute-start.10) | collective-permute-done | bytes 24608 | tf_op jit(solution)/shard_map/ppermute | solution.py:701
  72.2 0.7 collective-permute-start.12
  72.9 3.6 %collective-permute-done.12 = f32[144,128]{1,0:T(8,128)S(1)} collective-permute-done((f32[144,128]{1,0:T(8,128)S(1)}, f32[144,128]{1,0:T(8,128)S(1)}, u32[]{:S(2)}, u32[]{:S(2)}) %collective-permute-start.12) | collective-permute-done | bytes 73760 | tf_op jit(solution)/shard_map/ppermute | solution.py:701
  76.6 1.4 %collective-permute-done.13.q1 = f32[288,128]{1,0:T(8,128)S(1)} collective-permute-done((f32[288,128]{1,0:T(8,128)S(1)}, f32[288,128]{1,0:T(8,128)S(1)}, u32[]{:S(2)}, u32[]{:S(2)}) %collective-permute-start.13) | collective-permute-done | bytes 147488 | tf_op jit(solution)/shard_map/ppermute | solution.py:701
  77.9 0.9 square.1
  78.9 12.5 %all_to_all.20.t_in = f32[32,8,128]{2,1,0:T(8,128)S(1)} all-to-all(f32[32,8,128]{2,1,0:T(8,128)S(1)} %get-tuple-element.45), channel_id=1, replica_groups=mesh['sub'=8,'crs'=4] {'sub','crs'}, dimensions={0} | all-to-all | bytes 262144 | tf_op jit(solution)/shard_map/all_to_all | solution.py:774
  91.3 6.2 %third.1 = (f32[3,192,128]{2,1,0:T(8,128)S(1)}, f32[8,128]{1,0:T(8,128)S(1)}, f32[48,128]{1,0:T(8,128)S(1)}, f32[32,8,128]{2,1,0:T(8,128)}) custom-call(s32[2]{0:T(128)S(1)} %pad_add_fusion.place_ref, f32[7,192,128]{2,1,0:T(8,128)S(1)} %get-tuple-element.33.tr_ref, f32[7,192,128]{2,1,0:T(8,128)S(1)} %get-tuple-element.34.pt_ref, ...), custom_call_target="tpu_custom_call" | custom-call | bytes 14155776 | tf_op jit(solution)/shard_map/third/pallas_call | solution.py:747
  98.2 3.4 %collective-permute-start.14 = (f32[48,128]{1,0:T(8,128)S(1)}, f32[48,128]{1,0:T(8,128)S(1)}, u32[]{:S(2)}, u32[]{:S(2)}) collective-permute-start(f32[48,128]{1,0:T(8,128)S(1)} %get-tuple-element.50), channel_id=1, source_target_pairs={{0,4},{1,5},{2,6},{3,7},{4,0},{5,1},{6,2},{7,3},{8,12},{9,13},{10,... | collective-permute-start | bytes 73736 | tf_op jit(solution)/shard_map/ppermute | solution.py:701
  101.6 2.6 %all-to-all-start.3 = ((f32[32,8,128]{2,1,0:T(8,128)}), f32[32,8,128]{2,1,0:T(8,128)S(1)}, u32[]{:S(2)}, u32[]{:S(2)}) async-start(f32[32,8,128]{2,1,0:T(8,128)} %get-tuple-element.51), calls=%async_computation.3 | async-start | bytes 262144 | tf_op jit(solution)/shard_map/all_to_all | solution.py:774
  104.2 1.7 %collective-permute-start.16 = (f32[144,128]{1,0:T(8,128)S(1)}, f32[144,128]{1,0:T(8,128)S(1)}, u32[]{:S(2)}, u32[]{:S(2)}) collective-permute-start(f32[144,128]{1,0:T(8,128)S(1)} %pad_maximum_fusion.4), channel_id=1, source_target_pairs={{0,2},{1,3},{2,0},{3,1},{4,6},{5,7},{6,4},{7,5},{8,10},{9,11},{10,... | collective-permute-start | bytes 221192 | tf_op jit(solution)/shard_map/ppermute | solution.py:701
  105.9 3.4 %collective-permute-done.16 = f32[144,128]{1,0:T(8,128)S(1)} collective-permute-done((f32[144,128]{1,0:T(8,128)S(1)}, f32[144,128]{1,0:T(8,128)S(1)}, u32[]{:S(2)}, u32[]{:S(2)}) %collective-permute-start.16) | collective-permute-done | bytes 73760 | tf_op jit(solution)/shard_map/ppermute | solution.py:701
  109.3 1.4 %collective-permute-done.17.q1 = f32[288,128]{1,0:T(8,128)S(1)} collective-permute-done((f32[288,128]{1,0:T(8,128)S(1)}, f32[288,128]{1,0:T(8,128)S(1)}, u32[]{:S(2)}, u32[]{:S(2)}) %collective-permute-start.17) | collective-permute-done | bytes 147488 | tf_op jit(solution)/shard_map/ppermute | solution.py:701
  110.7 1.8 %all-to-all-done.3.t_in = f32[32,8,128]{2,1,0:T(8,128)S(1)} async-done(((f32[32,8,128]{2,1,0:T(8,128)}), f32[32,8,128]{2,1,0:T(8,128)S(1)}, u32[]{:S(2)}, u32[]{:S(2)}) %all-to-all-start.3) | async-done | bytes 131104 | tf_op jit(solution)/shard_map/all_to_all | solution.py:774
  112.4 2.0 %last.1 = (f32[12,1536]{1,0:T(8,128)}, f32[12,1536]{1,0:T(8,128)}) custom-call(s32[2]{0:T(128)S(1)} %pad_add_fusion.place_ref, f32[7,192,128]{2,1,0:T(8,128)S(1)} %get-tuple-element.33.tr_ref, f32[7,192,128]{2,1,0:T(8,128)S(1)} %get-tuple-element.34.pt_ref, bf16[192,576]{1,0:T(8,128)(2,1)S(1)} %get-tuple-element.35.jump_ref, ...), custom_call_target="tpu_custom_call" | custom-call | bytes 4000000 | tf_op jit(solution)/shard_map/last/pallas_call | solution.py:747
  (47 shorter events, 4.7 us)
Async XLA Ops:
  0.7 0.7 copy-start.1
  4.8 8.0 %collective-permute-start.1 = (f32[400,128]{1,0:T(8,128)S(1)}, f32[400,128]{1,0:T(8,128)S(1)}, u32[]{:S(2)}, u32[]{:S(2)}) collective-permute-start(f32[400,128]{1,0:T(8,128)S(1)} %get-tuple-element.31), channel_id=1, source_target_pairs={{4,8},{5,9},{6,10},{7,11},{8,4},{9,5},{10,6},{11,7},{12,16},{13,17... | collective-permute-start | bytes 614408 | tf_op jit(solution)/shard_map/ppermute | solution.py:701
  5.5 15.4 %collective-permute-start = (f32[400,128]{1,0:T(8,128)S(1)}, f32[400,128]{1,0:T(8,128)S(1)}, u32[]{:S(2)}, u32[]{:S(2)}) collective-permute-start(f32[400,128]{1,0:T(8,128)S(1)} %get-tuple-element.29), channel_id=1, source_target_pairs={{0,4},{1,5},{2,6},{3,7},{4,0},{5,1},{6,2},{7,3},{8,12},{9,13},{10,... | collective-permute-start | bytes 614408 | tf_op jit(solution)/shard_map/ppermute | solution.py:701
  11.2 19.8 %collective-permute-start.3 = (f32[112,128]{1,0:T(8,128)S(1)}, f32[112,128]{1,0:T(8,128)}, u32[]{:S(2)}, u32[]{:S(2)}) collective-permute-start(f32[112,128]{1,0:T(8,128)S(1)} %get-tuple-element.39), channel_id=1, source_target_pairs={{0,2},{1,3},{2,0},{3,1},{4,6},{5,7},{6,4},{7,5},{8,10},{9,11},{10,... | collective-permute-start | bytes 172040 | tf_op jit(solution)/shard_map/ppermute | solution.py:701
  12.8 15.3 %all-to-all-start = ((f32[32,2,128]{2,1,0:T(2,128)}), f32[32,2,128]{2,1,0:T(2,128)S(1)}, u32[]{:S(2)}, u32[]{:S(2)}) async-start(f32[32,2,128]{2,1,0:T(2,128)} %get-tuple-element.38), calls=%async_computation | async-start | bytes 65536 | tf_op jit(solution)/shard_map/all_to_all | solution.py:774
  20.9 7.2 %collective-permute-start.2 = (f32[560,128]{1,0:T(8,128)S(1)}, f32[560,128]{1,0:T(8,128)S(1)}, u32[]{:S(2)}, u32[]{:S(2)}) collective-permute-start(f32[560,128]{1,0:T(8,128)S(1)} %pad_maximum_fusion), channel_id=1, source_target_pairs={{0,1},{1,0},{2,3},{3,2},{4,5},{5,4},{6,7},{7,6},{8,9},{9,8},{10,11... | collective-permute-start | bytes 860168 | tf_op jit(solution)/shard_map/ppermute | solution.py:701
  21.2 9.8 %collective-permute-start.4 = (f32[224,128]{1,0:T(8,128)S(1)}, f32[224,128]{1,0:T(8,128)S(1)}, u32[]{:S(2)}, u32[]{:S(2)}) collective-permute-start(f32[224,128]{1,0:T(8,128)S(1)} %pad_maximum_fusion.1), channel_id=1, source_target_pairs={{0,2},{1,3},{2,0},{3,1},{4,6},{5,7},{6,4},{7,5},{8,10},{9,11},{10,... | collective-permute-start | bytes 344072 | tf_op jit(solution)/shard_map/ppermute | solution.py:701
  28.1 0.7 copy-start
  31.9 1.7 %collective-permute-start.5 = (f32[680,128]{1,0:T(8,128)S(1)}, f32[680,128]{1,0:T(8,128)S(1)}, u32[]{:S(2)}, u32[]{:S(2)}) collective-permute-start(f32[680,128]{1,0:T(8,128)S(1)} %concatenate.33.w0), channel_id=1, source_target_pairs={{0,1},{1,0},{2,3},{3,2},{4,5},{5,4},{6,7},{7,6},{8,9},{9,8},{10,11... | collective-permute-start | bytes 1044488 | tf_op jit(solution)/shard_map/ppermute | solution.py:701
  43.1 6.6 %collective-permute-start.7 = (f32[48,128]{1,0:T(8,128)S(1)}, f32[48,128]{1,0:T(8,128)S(1)}, u32[]{:S(2)}, u32[]{:S(2)}) collective-permute-start(f32[48,128]{1,0:T(8,128)S(1)} %get-tuple-element.40), channel_id=1, source_target_pairs={{4,8},{5,9},{6,10},{7,11},{8,4},{9,5},{10,6},{11,7},{12,16},{13,17... | collective-permute-start | bytes 73736 | tf_op jit(solution)/shard_map/ppermute | solution.py:701
  43.7 6.0 %collective-permute-start.6 = (f32[48,128]{1,0:T(8,128)S(1)}, f32[48,128]{1,0:T(8,128)S(1)}, u32[]{:S(2)}, u32[]{:S(2)}) collective-permute-start(f32[48,128]{1,0:T(8,128)S(1)} %get-tuple-element.40), channel_id=1, source_target_pairs={{0,4},{1,5},{2,6},{3,7},{4,0},{5,1},{6,2},{7,3},{8,12},{9,13},{10,... | collective-permute-start | bytes 73736 | tf_op jit(solution)/shard_map/ppermute | solution.py:701
  47.1 10.8 %all-to-all-start.1 = ((f32[32,8,128]{2,1,0:T(8,128)}), f32[32,8,128]{2,1,0:T(8,128)S(1)}, u32[]{:S(2)}, u32[]{:S(2)}) async-start(f32[32,8,128]{2,1,0:T(8,128)} %get-tuple-element.41), calls=%async_computation.1 | async-start | bytes 262144 | tf_op jit(solution)/shard_map/all_to_all | solution.py:774
  49.7 5.1 %collective-permute-start.8 = (f32[144,128]{1,0:T(8,128)S(1)}, f32[144,128]{1,0:T(8,128)S(1)}, u32[]{:S(2)}, u32[]{:S(2)}) collective-permute-start(f32[144,128]{1,0:T(8,128)S(1)} %pad_maximum_fusion.2), channel_id=1, source_target_pairs={{0,2},{1,3},{2,0},{3,1},{4,6},{5,7},{6,4},{7,5},{8,10},{9,11},{10,... | collective-permute-start | bytes 221192 | tf_op jit(solution)/shard_map/ppermute | solution.py:701
  54.8 1.4 %collective-permute-start.9 = (f32[288,128]{1,0:T(8,128)S(1)}, f32[288,128]{1,0:T(8,128)S(1)}, u32[]{:S(2)}, u32[]{:S(2)}) collective-permute-start(f32[288,128]{1,0:T(8,128)S(1)} %constant_dynamic-update-slice_fusion.q0), channel_id=1, source_target_pairs={{0,1},{1,0},{2,3},{3,2},{4,5},{5,4},{6,7},{7,6},{8,9},{9,8},{10,11... | collective-permute-start | bytes 442376 | tf_op jit(solution)/shard_map/ppermute | solution.py:701
  66.3 4.1 %collective-permute-start.11 = (f32[48,128]{1,0:T(8,128)S(1)}, f32[48,128]{1,0:T(8,128)S(1)}, u32[]{:S(2)}, u32[]{:S(2)}) collective-permute-start(f32[48,128]{1,0:T(8,128)S(1)} %get-tuple-element.42), channel_id=1, source_target_pairs={{4,8},{5,9},{6,10},{7,11},{8,4},{9,5},{10,6},{11,7},{12,16},{13,17... | collective-permute-start | bytes 73736 | tf_op jit(solution)/shard_map/ppermute | solution.py:701
  67.0 5.2 %collective-permute-start.10 = (f32[48,128]{1,0:T(8,128)S(1)}, f32[48,128]{1,0:T(8,128)S(1)}, u32[]{:S(2)}, u32[]{:S(2)}) collective-permute-start(f32[48,128]{1,0:T(8,128)S(1)} %get-tuple-element.42), channel_id=1, source_target_pairs={{0,4},{1,5},{2,6},{3,7},{4,0},{5,1},{6,2},{7,3},{8,12},{9,13},{10,... | collective-permute-start | bytes 73736 | tf_op jit(solution)/shard_map/ppermute | solution.py:701
  72.2 4.4 %collective-permute-start.12 = (f32[144,128]{1,0:T(8,128)S(1)}, f32[144,128]{1,0:T(8,128)S(1)}, u32[]{:S(2)}, u32[]{:S(2)}) collective-permute-start(f32[144,128]{1,0:T(8,128)S(1)} %pad_maximum_fusion.3), channel_id=1, source_target_pairs={{0,2},{1,3},{2,0},{3,1},{4,6},{5,7},{6,4},{7,5},{8,10},{9,11},{10,... | collective-permute-start | bytes 221192 | tf_op jit(solution)/shard_map/ppermute | solution.py:701
  76.6 1.4 %collective-permute-start.13 = (f32[288,128]{1,0:T(8,128)S(1)}, f32[288,128]{1,0:T(8,128)S(1)}, u32[]{:S(2)}, u32[]{:S(2)}) collective-permute-start(f32[288,128]{1,0:T(8,128)S(1)} %constant_dynamic-update-slice_fusion.4.q0), channel_id=1, source_target_pairs={{0,1},{1,0},{2,3},{3,2},{4,5},{5,4},{6,7},{7,6},{8,9},{9,8},{10,11... | collective-permute-start | bytes 442376 | tf_op jit(solution)/shard_map/ppermute | solution.py:701
  97.5 6.7 %collective-permute-start.15 = (f32[48,128]{1,0:T(8,128)S(1)}, f32[48,128]{1,0:T(8,128)S(1)}, u32[]{:S(2)}, u32[]{:S(2)}) collective-permute-start(f32[48,128]{1,0:T(8,128)S(1)} %get-tuple-element.50), channel_id=1, source_target_pairs={{4,8},{5,9},{6,10},{7,11},{8,4},{9,5},{10,6},{11,7},{12,16},{13,17... | collective-permute-start | bytes 73736 | tf_op jit(solution)/shard_map/ppermute | solution.py:701
  98.2 6.0 %collective-permute-start.14 = (f32[48,128]{1,0:T(8,128)S(1)}, f32[48,128]{1,0:T(8,128)S(1)}, u32[]{:S(2)}, u32[]{:S(2)}) collective-permute-start(f32[48,128]{1,0:T(8,128)S(1)} %get-tuple-element.50), channel_id=1, source_target_pairs={{0,4},{1,5},{2,6},{3,7},{4,0},{5,1},{6,2},{7,3},{8,12},{9,13},{10,... | collective-permute-start | bytes 73736 | tf_op jit(solution)/shard_map/ppermute | solution.py:701
  101.6 10.8 %all-to-all-start.3 = ((f32[32,8,128]{2,1,0:T(8,128)}), f32[32,8,128]{2,1,0:T(8,128)S(1)}, u32[]{:S(2)}, u32[]{:S(2)}) async-start(f32[32,8,128]{2,1,0:T(8,128)} %get-tuple-element.51), calls=%async_computation.3 | async-start | bytes 262144 | tf_op jit(solution)/shard_map/all_to_all | solution.py:774
  104.2 5.1 %collective-permute-start.16 = (f32[144,128]{1,0:T(8,128)S(1)}, f32[144,128]{1,0:T(8,128)S(1)}, u32[]{:S(2)}, u32[]{:S(2)}) collective-permute-start(f32[144,128]{1,0:T(8,128)S(1)} %pad_maximum_fusion.4), channel_id=1, source_target_pairs={{0,2},{1,3},{2,0},{3,1},{4,6},{5,7},{6,4},{7,5},{8,10},{9,11},{10,... | collective-permute-start | bytes 221192 | tf_op jit(solution)/shard_map/ppermute | solution.py:701
  109.3 1.4 %collective-permute-start.17 = (f32[288,128]{1,0:T(8,128)S(1)}, f32[288,128]{1,0:T(8,128)S(1)}, u32[]{:S(2)}, u32[]{:S(2)}) collective-permute-start(f32[288,128]{1,0:T(8,128)S(1)} %constant_dynamic-update-slice_fusion.8.q0), channel_id=1, source_target_pairs={{0,1},{1,0},{2,3},{3,2},{4,5},{5,4},{6,7},{7,6},{8,9},{9,8},{10,11... | collective-permute-start | bytes 442376 | tf_op jit(solution)/shard_map/ppermute | solution.py:701

commit v3 on v2

--- a/solution.py
+++ b/solution.py
@@ -159,6 +159,7 @@
         self.halves = self.full + 1
         self.wide = self.halves * LANES
         self.t_rows = self.crs * self.halves
+        self.sum_rows = -(-self.halves // 8) * 8
         self.tile_rows = self.modes * self.pad
         self.beside = LANES // max(self.spot, 1)
         self.rest_tiles = -(-self.modes // self.beside) if self.spot else 0
@@ -328,20 +329,28 @@
 def product(lowered, ops_vmem, sh, copies=None):
     row = lax.broadcasted_iota(jnp.int32, (sh.pad, sh.rows), 0)
     acc = jnp.zeros((sh.pad, sh.rows), F32)
-    span = sh.group * sh.rows
-    for i in range(sh.subs // sh.group):
-        if copies is not None:
-            copies[i].wait()
-        part = lax.dot_general(
-            lowered,
-            ops_vmem[i * span : (i + 1) * span],
-            (((1,), (1,)), ((), ())),
-            preferred_element_type=F32,
-        )
-        for j in range(sh.group):
-            acc = jnp.where(
-                row == i * sh.group + j, part[:, j * sh.rows : (j + 1) * sh.rows], acc
+    wide = lowered.astype(F32)
+    for s in range(sh.subs):
+        if copies is not None and s % sh.group == 0:
+            copies[s // sh.group].wait()
+        base = s * sh.rows
+        if s % 2 == 0:
+            part = lax.dot_general(
+                lowered,
+                ops_vmem[base : base + sh.rows],
+                (((1,), (1,)), ((), ())),
+                preferred_element_type=F32,
             )
+        else:
+            sums = []
+            for at in range(base, base + sh.rows, LANES):
+                tile = jnp.zeros((LANES, LANES), F32)
+                for k in range(0, sh.order, LANES):
+                    block = ops_vmem[at : at + LANES, k : k + LANES].astype(F32)
+                    tile = tile + block * wide[s : s + 1, k : k + LANES]
+                sums.append(jnp.sum(jnp.transpose(tile), axis=0, keepdims=True))
+            part = jnp.concatenate(sums, axis=1)
+        acc = jnp.where(row == s, part, acc)
     return rows_of(acc, sh)
 
 
@@ -371,17 +380,48 @@
             t_out[i] = payload
 
 
+def start_kernel(sh, place_ref, count_ref, load_hbm, factor_hbm, t_out, load_ref, factor_ref, sems):
+    copies = [
+        pltpu.make_async_copy(load_hbm, load_ref, sems.at[0]),
+        pltpu.make_async_copy(factor_hbm, factor_ref, sems.at[1]),
+    ]
+    for copy in copies:
+        copy.start()
+    for copy in copies:
+        copy.wait()
+    lane = lax.broadcasted_iota(jnp.int32, (8, sh.subs * sh.modes), 1)
+    kept = lane < 0
+    for s in range(sh.subs):
+        kept = kept | ((lane >= s * sh.modes) & (lane < s * sh.modes + count_ref[s]))
+    load = jnp.where(kept, jnp.broadcast_to(load_ref[...], kept.shape), 0.0)
+    part = jnp.dot(
+        load, factor_ref[...], preferred_element_type=F32, precision=lax.Precision.HIGHEST
+    )
+    part = jnp.concatenate([part, jnp.zeros((8, sh.wide - sh.cols), F32)], axis=1)[:1]
+    part = rows_of_lanes(part)
+    empty = jnp.zeros((sh.sum_rows - sh.halves, LANES), F32)
+    t_out[...] = jnp.concatenate([part, empty], axis=0)
+
+
+def load_kernel(sh, place_ref, ops_hbm, sum_ref, ops_out, sum_out, sems):
+    copies = ops_copies(ops_hbm, ops_out, sems, sh)
+    for copy in copies:
+        copy.start()
+    sum_out[...] = sum_ref[...]
+    for copy in copies:
+        copy.wait()
+
+
 def pack_kernel(
-    sh, place_ref, count_ref, traces_hbm, rhs_hbm, send_hbm, load_hbm, factor_hbm,
-    fields_out, parcel_a, parcel_b, factor_out, t_out,
-    slot_scr, traces_ref, rhs_ref, send_ref, load_ref, factor_ref, sems,
+    sh, place_ref, count_ref, traces_hbm, rhs_hbm, send_hbm, factor_hbm, after_ref,
+    fields_out, parcel_a, parcel_b, factor_out,
+    slot_scr, traces_ref, rhs_ref, send_ref, factor_ref, sems,
 ):
     copies = [
         pltpu.make_async_copy(source, target, sems.at[i])
         for i, (source, target) in enumerate(
             (
                 (factor_hbm, factor_ref),
-                (load_hbm, load_ref),
                 (send_hbm, send_ref),
                 (rhs_hbm, rhs_ref),
                 (traces_hbm, traces_ref),
@@ -460,19 +500,6 @@
             )
         out[sh.parcel :, :] = factor
 
-    lane = lax.broadcasted_iota(jnp.int32, (8, sh.subs * sh.modes), 1)
-    kept = lane < 0
-    for s in range(sh.subs):
-        kept = kept | ((lane >= s * sh.modes) & (lane < s * sh.modes + count_ref[s]))
-    load = jnp.where(kept, jnp.broadcast_to(load_ref[...], kept.shape), 0.0)
-    part = jnp.dot(
-        load, factor_ref[...], preferred_element_type=F32, precision=lax.Precision.HIGHEST
-    )
-    part = jnp.concatenate([part, jnp.zeros((8, sh.wide - sh.cols), F32)], axis=1)[:1]
-    payload = rows_of_lanes(part)
-    for i in range(sh.ndev):
-        t_out[i] = payload
-
 
 def setup_kernel(
     sh, place_ref, partner_ref, fields_ref, near_a, near_b, core_ref,
@@ -572,22 +599,19 @@
 
 
 def first_kernel(
-    sh, place_ref, tr_ref, pt_ref, ep_ref, ept_ref, t_in, w0, w1, ops_hbm,
-    lam_out, q_out, t_out, t_scr, ops_vmem, sems,
+    sh, place_ref, tr_ref, pt_ref, ep_ref, ept_ref, w0, w1, ops_ref,
+    lam_out, q_out, t_out, t_scr,
 ):
-    copies = ops_copies(ops_hbm, ops_vmem, sems, sh)
-    for copy in copies:
-        copy.start()
     me = place_ref[0]
     w_refs = (w0, w1)
-    for j in range(sh.crs):
-        acc = t_in[j]
-        for i in range(j + sh.crs, sh.ndev, sh.crs):
-            acc = acc + t_in[i]
-        t_scr[j * sh.halves : (j + 1) * sh.halves, :] = acc
+    for rel in range(sh.crs):
+        at = jnp.bitwise_xor(me, rel) * sh.halves
+        base = sh.crs // 2 * 3 * sh.factor_rows + rel // 2 * sh.sum_rows
+        for h in range(sh.halves):
+            t_scr[pl.ds(at + h, 1), :] = w_refs[rel % 2][base + h : base + h + 1, :]
     lam = lift(tr_ref, pt_ref, ep_ref, w_refs, t_scr, me, sh)
     lam_out[...] = lam
-    q = product(lanes_of(2.0 * lam, sh).astype(BF16), ops_vmem, sh, copies)
+    q = product(lanes_of(2.0 * lam, sh).astype(BF16), ops_ref, sh)
     q_out[...] = q
     at = pl.multiple_of(me * sh.piece, 16)
     value = tr_ref[sh.modes, pl.ds(at, sh.piece), :] - 2.0 * q
@@ -761,7 +785,7 @@
     rows = (sh.all_rows, LANES)
     t_shape = ("v", (sh.t_rows, LANES), F32)
     parcels = ("v", (sh.ndev, sh.t_rows, LANES), F32)
-    columns = ("v", (sh.ndev, sh.halves, LANES), F32)
+    columns = ("v", (sh.sum_rows, LANES), F32)
     q_shape = ("v", (sh.piece, LANES), F32)
     field_shape = ("v", (modes + 1,) + rows, F32)
     t_scratch = pltpu.VMEM((sh.t_rows, LANES), F32)
@@ -777,24 +801,46 @@
         return (count,) + rows
 
     parcel_shape = ("v", (sh.parcel + sh.factor_rows, LANES), F32)
-    raw = (rigid_traces, dual_rhs, send_list, rigid_load[None, :], coarse_factor)
-    fields, parcel_a, parcel_b, factor, t_part = call(
-        pack_kernel, "shhhhh",
-        [field_shape, parcel_shape, parcel_shape, ("v", (sh.factor_rows, LANES), F32), columns],
+    load = rigid_load[None, :]
+    (t_part,) = call(
+        start_kernel, "shh", [columns],
+        [pltpu.VMEM(load.shape, F32), pltpu.VMEM(coarse_factor.shape, F32)]
+        + [pltpu.SemaphoreType.DMA((2,))],
+        mode_count, load, coarse_factor, name="start", cost=100_000,
+    )
+    t_sum = t_part + permute(t_part, lambda i, j: (i ^ 1, j))
+    raw = (rigid_traces, dual_rhs, send_list, coarse_factor)
+    fields, parcel_a, parcel_b, factor = call(
+        pack_kernel, "shhhhv",
+        [field_shape, parcel_shape, parcel_shape, ("v", (sh.factor_rows, LANES), F32)],
         [pltpu.VMEM((sh.slot_lanes, LANES), F32)]
         + [pltpu.VMEM(x.shape, x.dtype) for x in raw]
         + [pltpu.SemaphoreType.DMA((len(raw),))],
-        mode_count, *raw, name="pack", cost=8_000_000,
+        mode_count, *raw, t_part, name="pack", cost=8_000_000,
+    )
+    parcel_a, parcel_b, factor, t_sum = lax.optimization_barrier(
+        (parcel_a, parcel_b, factor, t_sum)
     )
     near_a, near_b = swap_a(parcel_a), swap_b(parcel_b)
     factor_x = x_swaps(factor)
-    t_part, near_b = lax.optimization_barrier((t_part, near_b))
-    t_in = exchange(t_part)
+    sum_steps = [2**k for k in range(1, (lax.axis_size("sub") - 1).bit_length())]
+    for step in sum_steps[:-1]:
+        t_sum = t_sum + permute(t_sum, lambda i, j: (i ^ step, j))
+    ops_vmem, t_same = call(
+        load_kernel, "hv", [ops_kept, columns], [pltpu.SemaphoreType.DMA((ops_sems,))],
+        ops, t_sum, name="load", cost=long,
+    )
+    for step in sum_steps[-1:]:
+        t_same = t_same + permute(t_sum, lambda i, j: (i ^ step, j))
+    t_sum = t_same
+
     halves = core_swap(jnp.concatenate([near_a[: sh.names_at], near_b[: sh.names_at]], axis=0))
-    factor_ab = jnp.concatenate([near_a[sh.parcel :], near_b[sh.parcel :]], axis=0)
-    w0 = [factor, factor_ab]
+    factor_ab = jnp.concatenate([near_a[sh.parcel :], near_b[sh.parcel :], t_sum], axis=0)
+    pair_rows = 2 * sh.factor_rows
+    w0, sums = [factor, factor_ab[:pair_rows]], [t_sum]
     for own, pair in zip(factor_x, x_swaps(factor_ab)):
-        w0 += [own, pair]
+        w0 += [own, pair[:pair_rows]]
+        sums.append(pair[pair_rows:])
     traces, far_traces, jumper, far_pick, far_put = call(
         setup_kernel, "vvvvv",
         [
@@ -806,14 +852,13 @@
         [pltpu.VMEM(rows, F32)],
         partner, fields, near_a, near_b, halves, name="setup", cost=6_000_000,
     )
-    rider = jnp.concatenate([t_in[0, :1], far_traces[0, :7]], axis=0)
-    w0 = jnp.concatenate(w0 + [rider], axis=0)
+    w0 = jnp.concatenate(w0 + sums + [far_traces[0, :8]], axis=0)
     w1 = core_swap(w0)
     lam0, q, t_part = call(
-        first_kernel, "vvvvvvvh",
+        first_kernel, "vvvvvvv",
         [("v", rows, F32), q_shape, parcels],
-        [t_scratch, pltpu.VMEM(ops.shape, BF16), pltpu.SemaphoreType.DMA((ops_sems,))],
-        traces, far_traces, far_pick, far_put, t_in, w0, w1, ops, name="first", cost=long,
+        [t_scratch],
+        traces, far_traces, far_pick, far_put, w0, w1, ops_vmem, name="first", cost=long,
     )
     q0, q1 = spread_pieces(q)
     t_in = exchange(t_part)
@@ -860,6 +905,7 @@
         dual_ops.shape[2] // partner.shape[1] == LANES and dual_ops.shape[1] % LANES == 0
     )
     fits = whole_blocks and args[2].shape[1] % LANES + 8 <= LANES
+    fits = fits and sub_num & (sub_num - 1) == 0
     if fits and crs_num % 2 == 0 and crs_num & (crs_num - 1) == 0 and sub_num % 2 == 0:
         return local(*args)
     return plain(*args)

time: 115 us -> 110 us (0.957)
  starting transfers between devices: 39.7 us -> 37.5 us
  local copies, waits for them, and re-layouts: 2.3 us -> 0.78 us
  waiting for transfers between devices: 26.4 us -> 24.9 us
    all_to_all x3 -> x2, starting transfers between devices: 13.2 us -> 5.73 us  [exchange(): return lax.all_to_all(parcel, AXES, 0, 0)]
    all_to_all x3 -> x2, waiting for transfers between devices: 8.61 us -> 3.3 us  [exchange(): return lax.all_to_all(parcel, AXES, 0, 0)]
    ppermute x18 -> x21, starting transfers between devices: 26.5 us -> 31.8 us  [permute(): return lax.ppermute(value, AXES, pairs)]
    ppermute x18 -> x21, waiting for transfers between devices: 17.8 us -> 21.6 us  [permute(): return lax.ppermute(value, AXES, pairs)]
    pallas_call x7 -> x9, Pallas kernels: 32.5 us -> 32.9 us  [call(): pl.pallas_call(functools.partial(kernel, sh), out_shape=[pltpu.VMEM(s, t)...]
  transfers between devices with their start and end apart: 21 -> 23, of which waited for: 11 -> 12; matrix products, arithmetic and copies ran while one was open for 0% -> 0% of each run, Pallas kernels for 2% -> 8%
where the time goes in v3:
time: 110 us
  starting transfers between devices  37.5 us (34%)
  Pallas kernels  32.9 us (30%)
  waiting for transfers between devices  24.9 us (23%)
  blocking collectives  12.5 us (11%)
    pallas_call x9, Pallas kernels, call(): pl.pallas_call(functools.partial(kernel, sh), out_shape=[pltpu.VMEM(s, t)...  32.9 us
    ppermute x21, starting transfers between devices, permute(): return lax.ppermute(value, AXES, pairs)  31.8 us
    ppermute x21, waiting for transfers between devices, permute(): return lax.ppermute(value, AXES, pairs)  21.6 us
    all_to_all x1, blocking collectives, exchange(): return lax.all_to_all(parcel, AXES, 0, 0)  12.5 us
    all_to_all x2, starting transfers between devices, exchange(): return lax.all_to_all(parcel, AXES, 0, 0)  5.73 us
    all_to_all x2, waiting for transfers between devices, exchange(): return lax.all_to_all(parcel, AXES, 0, 0)  3.3 us
  transfers between devices with their start and end apart: 23, of which 12 were waited for; matrix products, arithmetic and copies ran while one was open for 0% of the time, Pallas kernels for 8%

profile of v3, /device:TPU:0, one launch (start us, length us, event | category | flops | bytes accessed | tf_op | source)
XLA Modules:
  0.0 109.6 jit_solution(5276444893846463321)
XLA Ops:
  1.4 1.6 %start.1.after_ref = f32[8,128]{1,0:T(8,128)S(1)} custom-call(s32[2]{0:T(128)S(1)} %pad_add_fusion.place_ref, s32[12]{0:T(128)S(1)} %copy-done.1, f32[1,72]{1,0:T(1,128)} %bitcast.8, f32[72,144]{1,0:T(8,128)} %factor_hbm.3), custom_call_target="tpu_custom_call" | custom-call | bytes 100000 | tf_op jit(solution)/shard_map/start/pallas_call | solution.py:771
  3.0 3.0 %collective-permute-start = (f32[8,128]{1,0:T(8,128)S(1)}, f32[8,128]{1,0:T(8,128)S(1)}, u32[]{:S(2)}, u32[]{:S(2)}) collective-permute-start(f32[8,128]{1,0:T(8,128)S(1)} %start.1.after_ref), channel_id=1, source_target_pairs={{0,4},{1,5},{2,6},{3,7},{4,0},{5,1},{6,2},{7,3},{8,12},{9,13},{10,... | collective-permute-start | bytes 12296 | tf_op jit(solution)/shard_map/ppermute | solution.py:725
  6.0 2.7 %pack.1 = (f32[7,192,128]{2,1,0:T(8,128)S(1)}, f32[400,128]{1,0:T(8,128)S(1)}, f32[400,128]{1,0:T(8,128)S(1)}, f32[112,128]{1,0:T(8,128)S(1)}) custom-call(s32[2]{0:T(128)S(1)} %pad_add_fusion.place_ref, s32[12]{0:T(128)S(1)} %copy-done.1, f32[12,6,1536]{2,1,0:T(8,128)} %traces_hbm.1, f32[12,1536]{1,0:T(8,128)} %rhs_hbm.1, s32[2,72]{1,0:T(2,128)} %send_hbm.1, ...), custom_call_target="tpu_custom_call" | custom-call | bytes 8000000 | tf_op jit(solution)/shard_map/pack/pallas_call | solution.py:771
  9.7 1.6 %collective-permute-start.5 = (f32[8,128]{1,0:T(8,128)S(1)}, f32[8,128]{1,0:T(8,128)S(1)}, u32[]{:S(2)}, u32[]{:S(2)}) collective-permute-start(f32[8,128]{1,0:T(8,128)S(1)} %add.14), channel_id=1, source_target_pairs={{0,8},{1,9},{2,10},{3,11},{4,12},{5,13},{6,14},{7,15},{8,0},{9,1},... | collective-permute-start | bytes 12296 | tf_op jit(solution)/shard_map/ppermute | solution.py:725
  11.2 1.5 %collective-permute-start.4 = (f32[112,128]{1,0:T(8,128)S(1)}, f32[112,128]{1,0:T(8,128)S(1)}, u32[]{:S(2)}, u32[]{:S(2)}) collective-permute-start(f32[112,128]{1,0:T(8,128)S(1)} %get-tuple-element.42), channel_id=1, source_target_pairs={{0,2},{1,3},{2,0},{3,1},{4,6},{5,7},{6,4},{7,5},{8,10},{9,11},{10,... | collective-permute-start | bytes 172040 | tf_op jit(solution)/shard_map/ppermute | solution.py:725
  13.3 2.6 %collective-permute-start.6 = (f32[8,128]{1,0:T(8,128)S(1)}, f32[8,128]{1,0:T(8,128)S(1)}, u32[]{:S(2)}, u32[]{:S(2)}) collective-permute-start(f32[8,128]{1,0:T(8,128)S(1)} %add.15.sum_ref), channel_id=1, source_target_pairs={{0,16},{1,17},{2,18},{3,19},{4,20},{5,21},{6,22},{7,23},{8,24},{9,... | collective-permute-start | bytes 12296 | tf_op jit(solution)/shard_map/ppermute | solution.py:725
  16.5 5.7 %load.1 = (bf16[4608,1536]{1,0:T(8,128)(2,1)S(1)}, f32[8,128]{1,0:T(8,128)S(1)}) custom-call(s32[2]{0:T(128)S(1)} %pad_add_fusion.place_ref, bf16[4608,1536]{1,0:T(8,128)(2,1)} %bitcast.6, f32[8,128]{1,0:T(8,128)S(1)} %add.15.sum_ref), custom_call_target="tpu_custom_call" | custom-call | bytes 14155776 | tf_op jit(solution)/shard_map/load/pallas_call | solution.py:771
  22.3 1.6 %collective-permute-start.7 = (f32[232,128]{1,0:T(8,128)S(1)}, f32[232,128]{1,0:T(8,128)S(1)}, u32[]{:S(2)}, u32[]{:S(2)}) collective-permute-start(f32[232,128]{1,0:T(8,128)S(1)} %pad_maximum_fusion.1), channel_id=1, source_target_pairs={{0,2},{1,3},{2,0},{3,1},{4,6},{5,7},{6,4},{7,5},{8,10},{9,11},{10,... | collective-permute-start | bytes 356360 | tf_op jit(solution)/shard_map/ppermute | solution.py:725
  24.1 3.2 %collective-permute-done.7 = f32[232,128]{1,0:T(8,128)S(1)} collective-permute-done((f32[232,128]{1,0:T(8,128)S(1)}, f32[232,128]{1,0:T(8,128)S(1)}, u32[]{:S(2)}, u32[]{:S(2)}) %collective-permute-start.7) | collective-permute-done | bytes 118816 | tf_op jit(solution)/shard_map/ppermute | solution.py:725
  27.3 2.2 %setup.1 = (f32[7,192,128]{2,1,0:T(8,128)S(1)}, f32[7,192,128]{2,1,0:T(8,128)S(1)}, bf16[192,576]{1,0:T(8,128)(2,1)S(1)}, bf16[192,48]{1,0:T(8,128)(2,1)S(1)}, bf16[48,48]{1,0:T(8,128)(2,1)S(1)}) custom-call(s32[2]{0:T(128)S(1)} %pad_add_fusion.place_ref, s32[12,12]{1,0:T(8,128)S(1)} %copy-done, f32[7,192,128]{2,1,0:T(8,128)S(1)} %get-tuple-element.31.fields_ref, ...), custom_call_target="tpu_custom_call" | custom-call | bytes 6000000 | tf_op jit(solution)/shard_map/setup/pallas_call | solution.py:771
  29.6 1.7 %collective-permute-done.8.w1 = f32[696,128]{1,0:T(8,128)S(1)} collective-permute-done((f32[696,128]{1,0:T(8,128)S(1)}, f32[696,128]{1,0:T(8,128)S(1)}, u32[]{:S(2)}, u32[]{:S(2)}) %collective-permute-start.8) | collective-permute-done | bytes 356384 | tf_op jit(solution)/shard_map/ppermute | solution.py:725
  31.2 5.1 %first.1 = (f32[192,128]{1,0:T(8,128)S(1)}, f32[48,128]{1,0:T(8,128)S(1)}, f32[32,8,128]{2,1,0:T(8,128)}) custom-call(s32[2]{0:T(128)S(1)} %pad_add_fusion.place_ref, f32[7,192,128]{2,1,0:T(8,128)S(1)} %get-tuple-element.37.tr_ref, f32[7,192,128]{2,1,0:T(8,128)S(1)} %get-tuple-element.38.pt_ref, bf16[192,48]{1,0:T(8,128)(2,1)S(1)} %get-tuple-element.40.ep_ref, ...), custom_call_target="tpu_custom_call" | custom-call | bytes 14155776 | tf_op jit(solution)/shard_map/first/pallas_call | solution.py:771
  37.0 6.7 %collective-permute-start.9 = (f32[48,128]{1,0:T(8,128)S(1)}, f32[48,128]{1,0:T(8,128)S(1)}, u32[]{:S(2)}, u32[]{:S(2)}) collective-permute-start(f32[48,128]{1,0:T(8,128)S(1)} %get-tuple-element.46), channel_id=1, source_target_pairs={{0,4},{1,5},{2,6},{3,7},{4,0},{5,1},{6,2},{7,3},{8,12},{9,13},{10,... | collective-permute-start | bytes 73736 | tf_op jit(solution)/shard_map/ppermute | solution.py:725
  43.7 3.2 %all-to-all-start = ((f32[32,8,128]{2,1,0:T(8,128)}), f32[32,8,128]{2,1,0:T(8,128)S(1)}, u32[]{:S(2)}, u32[]{:S(2)}) async-start(f32[32,8,128]{2,1,0:T(8,128)} %get-tuple-element.47), calls=%async_computation | async-start | bytes 262144 | tf_op jit(solution)/shard_map/all_to_all | solution.py:798
  46.9 1.8 %collective-permute-start.11 = (f32[144,128]{1,0:T(8,128)S(1)}, f32[144,128]{1,0:T(8,128)S(1)}, u32[]{:S(2)}, u32[]{:S(2)}) collective-permute-start(f32[144,128]{1,0:T(8,128)S(1)} %pad_maximum_fusion.2), channel_id=1, source_target_pairs={{0,2},{1,3},{2,0},{3,1},{4,6},{5,7},{6,4},{7,5},{8,10},{9,11},{10,... | collective-permute-start | bytes 221192 | tf_op jit(solution)/shard_map/ppermute | solution.py:725
  48.7 3.4 %collective-permute-done.11 = f32[144,128]{1,0:T(8,128)S(1)} collective-permute-done((f32[144,128]{1,0:T(8,128)S(1)}, f32[144,128]{1,0:T(8,128)S(1)}, u32[]{:S(2)}, u32[]{:S(2)}) %collective-permute-start.11) | collective-permute-done | bytes 73760 | tf_op jit(solution)/shard_map/ppermute | solution.py:725
  52.1 1.4 %collective-permute-done.12.q1 = f32[288,128]{1,0:T(8,128)S(1)} collective-permute-done((f32[288,128]{1,0:T(8,128)S(1)}, f32[288,128]{1,0:T(8,128)S(1)}, u32[]{:S(2)}, u32[]{:S(2)}) %collective-permute-start.12) | collective-permute-done | bytes 147488 | tf_op jit(solution)/shard_map/ppermute | solution.py:725
  53.5 1.6 %all-to-all-done.t_in = f32[32,8,128]{2,1,0:T(8,128)S(1)} async-done(((f32[32,8,128]{2,1,0:T(8,128)}), f32[32,8,128]{2,1,0:T(8,128)S(1)}, u32[]{:S(2)}, u32[]{:S(2)}) %all-to-all-start) | async-done | bytes 131104 | tf_op jit(solution)/shard_map/all_to_all | solution.py:798
  55.1 7.3 %second.1 = (f32[4,192,128]{2,1,0:T(8,128)S(1)}, f32[8,128]{1,0:T(8,128)S(1)}, f32[48,128]{1,0:T(8,128)S(1)}, f32[8,128]{1,0:T(8,128)S(1)}, bf16[4608,1536]{1,0:T(8,128)(2,1)S(1)}) custom-call(s32[2]{0:T(128)S(1)} %pad_add_fusion.place_ref, f32[7,192,128]{2,1,0:T(8,128)S(1)} %get-tuple-element.37.tr_ref, f32[7,192,128]{2,1,0:T(8,128)S(1)} %get-tuple-element.38.pt_ref, ...), custom_call_target="tpu_custom_call" | custom-call | bytes 14155776 | tf_op jit(solution)/shard_map/second/pallas_call | solution.py:771
  63.0 3.4 %collective-permute-start.13 = (f32[48,128]{1,0:T(8,128)S(1)}, f32[48,128]{1,0:T(8,128)S(1)}, u32[]{:S(2)}, u32[]{:S(2)}) collective-permute-start(f32[48,128]{1,0:T(8,128)S(1)} %get-tuple-element.48), channel_id=1, source_target_pairs={{0,4},{1,5},{2,6},{3,7},{4,0},{5,1},{6,2},{7,3},{8,12},{9,13},{10,... | collective-permute-start | bytes 73736 | tf_op jit(solution)/shard_map/ppermute | solution.py:725
  66.5 1.8 %collective-permute-done.13 = f32[48,128]{1,0:T(8,128)S(1)} collective-permute-done((f32[48,128]{1,0:T(8,128)S(1)}, f32[48,128]{1,0:T(8,128)S(1)}, u32[]{:S(2)}, u32[]{:S(2)}) %collective-permute-start.13) | collective-permute-done | bytes 24608 | tf_op jit(solution)/shard_map/ppermute | solution.py:725
  69.1 3.5 %collective-permute-done.15 = f32[144,128]{1,0:T(8,128)S(1)} collective-permute-done((f32[144,128]{1,0:T(8,128)S(1)}, f32[144,128]{1,0:T(8,128)S(1)}, u32[]{:S(2)}, u32[]{:S(2)}) %collective-permute-start.15) | collective-permute-done | bytes 73760 | tf_op jit(solution)/shard_map/ppermute | solution.py:725
  72.6 1.4 %collective-permute-done.16.q1 = f32[288,128]{1,0:T(8,128)S(1)} collective-permute-done((f32[288,128]{1,0:T(8,128)S(1)}, f32[288,128]{1,0:T(8,128)S(1)}, u32[]{:S(2)}, u32[]{:S(2)}) %collective-permute-start.16) | collective-permute-done | bytes 147488 | tf_op jit(solution)/shard_map/ppermute | solution.py:725
  75.0 12.5 %all_to_all.15.t_in = f32[32,8,128]{2,1,0:T(8,128)S(1)} all-to-all(f32[32,8,128]{2,1,0:T(8,128)S(1)} %get-tuple-element.51), channel_id=1, replica_groups=mesh['sub'=8,'crs'=4] {'sub','crs'}, dimensions={0} | all-to-all | bytes 262144 | tf_op jit(solution)/shard_map/all_to_all | solution.py:798
  87.4 5.4 %third.1 = (f32[3,192,128]{2,1,0:T(8,128)S(1)}, f32[8,128]{1,0:T(8,128)S(1)}, f32[48,128]{1,0:T(8,128)S(1)}, f32[32,8,128]{2,1,0:T(8,128)}) custom-call(s32[2]{0:T(128)S(1)} %pad_add_fusion.place_ref, f32[7,192,128]{2,1,0:T(8,128)S(1)} %get-tuple-element.37.tr_ref, f32[7,192,128]{2,1,0:T(8,128)S(1)} %get-tuple-element.38.pt_ref, ...), custom_call_target="tpu_custom_call" | custom-call | bytes 14155776 | tf_op jit(solution)/shard_map/third/pallas_call | solution.py:771
  93.4 3.4 %collective-permute-start.17 = (f32[48,128]{1,0:T(8,128)S(1)}, f32[48,128]{1,0:T(8,128)S(1)}, u32[]{:S(2)}, u32[]{:S(2)}) collective-permute-start(f32[48,128]{1,0:T(8,128)S(1)} %get-tuple-element.56), channel_id=1, source_target_pairs={{0,4},{1,5},{2,6},{3,7},{4,0},{5,1},{6,2},{7,3},{8,12},{9,13},{10,... | collective-permute-start | bytes 73736 | tf_op jit(solution)/shard_map/ppermute | solution.py:725
  96.9 2.6 %all-to-all-start.2 = ((f32[32,8,128]{2,1,0:T(8,128)}), f32[32,8,128]{2,1,0:T(8,128)S(1)}, u32[]{:S(2)}, u32[]{:S(2)}) async-start(f32[32,8,128]{2,1,0:T(8,128)} %get-tuple-element.57), calls=%async_computation.2 | async-start | bytes 262144 | tf_op jit(solution)/shard_map/all_to_all | solution.py:798
  99.5 1.7 %collective-permute-start.19 = (f32[144,128]{1,0:T(8,128)S(1)}, f32[144,128]{1,0:T(8,128)S(1)}, u32[]{:S(2)}, u32[]{:S(2)}) collective-permute-start(f32[144,128]{1,0:T(8,128)S(1)} %pad_maximum_fusion.4), channel_id=1, source_target_pairs={{0,2},{1,3},{2,0},{3,1},{4,6},{5,7},{6,4},{7,5},{8,10},{9,11},{10,... | collective-permute-start | bytes 221192 | tf_op jit(solution)/shard_map/ppermute | solution.py:725
  101.2 3.4 %collective-permute-done.19 = f32[144,128]{1,0:T(8,128)S(1)} collective-permute-done((f32[144,128]{1,0:T(8,128)S(1)}, f32[144,128]{1,0:T(8,128)S(1)}, u32[]{:S(2)}, u32[]{:S(2)}) %collective-permute-start.19) | collective-permute-done | bytes 73760 | tf_op jit(solution)/shard_map/ppermute | solution.py:725
  104.6 1.4 %collective-permute-done.20.q1 = f32[288,128]{1,0:T(8,128)S(1)} collective-permute-done((f32[288,128]{1,0:T(8,128)S(1)}, f32[288,128]{1,0:T(8,128)S(1)}, u32[]{:S(2)}, u32[]{:S(2)}) %collective-permute-start.20) | collective-permute-done | bytes 147488 | tf_op jit(solution)/shard_map/ppermute | solution.py:725
  105.9 1.8 %all-to-all-done.2.t_in = f32[32,8,128]{2,1,0:T(8,128)S(1)} async-done(((f32[32,8,128]{2,1,0:T(8,128)}), f32[32,8,128]{2,1,0:T(8,128)S(1)}, u32[]{:S(2)}, u32[]{:S(2)}) %all-to-all-start.2) | async-done | bytes 131104 | tf_op jit(solution)/shard_map/all_to_all | solution.py:798
  107.7 2.0 %last.1 = (f32[12,1536]{1,0:T(8,128)}, f32[12,1536]{1,0:T(8,128)}) custom-call(s32[2]{0:T(128)S(1)} %pad_add_fusion.place_ref, f32[7,192,128]{2,1,0:T(8,128)S(1)} %get-tuple-element.37.tr_ref, f32[7,192,128]{2,1,0:T(8,128)S(1)} %get-tuple-element.38.pt_ref, bf16[192,576]{1,0:T(8,128)(2,1)S(1)} %get-tuple-element.39.jump_ref, ...), custom_call_target="tpu_custom_call" | custom-call | bytes 4000000 | tf_op jit(solution)/shard_map/last/pallas_call | solution.py:771
  (59 shorter events, 6.9 us)
Async XLA Ops:
  0.6 26.7 %copy-start = (s32[12,12]{1,0:T(8,128)S(1)}, s32[12,12]{1,0:T(8,128)}, u32[]{:S(2)}) copy-start(s32[12,12]{1,0:T(8,128)} %partner_ref.1) | copy-start | bytes 1732
  0.7 0.7 copy-start.1
  3.0 5.8 %collective-permute-start = (f32[8,128]{1,0:T(8,128)S(1)}, f32[8,128]{1,0:T(8,128)S(1)}, u32[]{:S(2)}, u32[]{:S(2)}) collective-permute-start(f32[8,128]{1,0:T(8,128)S(1)} %start.1.after_ref), channel_id=1, source_target_pairs={{0,4},{1,5},{2,6},{3,7},{4,0},{5,1},{6,2},{7,3},{8,12},{9,13},{10,... | collective-permute-start | bytes 12296 | tf_op jit(solution)/shard_map/ppermute | solution.py:725
  8.8 13.5 %collective-permute-start.1 = (f32[400,128]{1,0:T(8,128)S(1)}, f32[400,128]{1,0:T(8,128)S(1)}, u32[]{:S(2)}, u32[]{:S(2)}) collective-permute-start(f32[400,128]{1,0:T(8,128)S(1)} %get-tuple-element.35), channel_id=1, source_target_pairs={{0,4},{1,5},{2,6},{3,7},{4,0},{5,1},{6,2},{7,3},{8,12},{9,13},{10,... | collective-permute-start | bytes 614408 | tf_op jit(solution)/shard_map/ppermute | solution.py:725
  9.7 3.6 %collective-permute-start.5 = (f32[8,128]{1,0:T(8,128)S(1)}, f32[8,128]{1,0:T(8,128)S(1)}, u32[]{:S(2)}, u32[]{:S(2)}) collective-permute-start(f32[8,128]{1,0:T(8,128)S(1)} %add.14), channel_id=1, source_target_pairs={{0,8},{1,9},{2,10},{3,11},{4,12},{5,13},{6,14},{7,15},{8,0},{9,1},... | collective-permute-start | bytes 12296 | tf_op jit(solution)/shard_map/ppermute | solution.py:725
  11.2 12.8 %collective-permute-start.4 = (f32[112,128]{1,0:T(8,128)S(1)}, f32[112,128]{1,0:T(8,128)S(1)}, u32[]{:S(2)}, u32[]{:S(2)}) collective-permute-start(f32[112,128]{1,0:T(8,128)S(1)} %get-tuple-element.42), channel_id=1, source_target_pairs={{0,2},{1,3},{2,0},{3,1},{4,6},{5,7},{6,4},{7,5},{8,10},{9,11},{10,... | collective-permute-start | bytes 172040 | tf_op jit(solution)/shard_map/ppermute | solution.py:725
  13.3 9.0 %collective-permute-start.6 = (f32[8,128]{1,0:T(8,128)S(1)}, f32[8,128]{1,0:T(8,128)S(1)}, u32[]{:S(2)}, u32[]{:S(2)}) collective-permute-start(f32[8,128]{1,0:T(8,128)S(1)} %add.15.sum_ref), channel_id=1, source_target_pairs={{0,16},{1,17},{2,18},{3,19},{4,20},{5,21},{6,22},{7,23},{8,24},{9,... | collective-permute-start | bytes 12296 | tf_op jit(solution)/shard_map/ppermute | solution.py:725
  15.9 6.4 %collective-permute-start.2 = (f32[400,128]{1,0:T(8,128)S(1)}, f32[400,128]{1,0:T(8,128)S(1)}, u32[]{:S(2)}, u32[]{:S(2)}) collective-permute-start(f32[400,128]{1,0:T(8,128)S(1)} %get-tuple-element.36), channel_id=1, source_target_pairs={{4,8},{5,9},{6,10},{7,11},{8,4},{9,5},{10,6},{11,7},{12,16},{13,17... | collective-permute-start | bytes 614408 | tf_op jit(solution)/shard_map/ppermute | solution.py:725
  22.3 4.9 %collective-permute-start.7 = (f32[232,128]{1,0:T(8,128)S(1)}, f32[232,128]{1,0:T(8,128)S(1)}, u32[]{:S(2)}, u32[]{:S(2)}) collective-permute-start(f32[232,128]{1,0:T(8,128)S(1)} %pad_maximum_fusion.1), channel_id=1, source_target_pairs={{0,2},{1,3},{2,0},{3,1},{4,6},{5,7},{6,4},{7,5},{8,10},{9,11},{10,... | collective-permute-start | bytes 356360 | tf_op jit(solution)/shard_map/ppermute | solution.py:725
  24.0 3.3 %collective-permute-start.3 = (f32[560,128]{1,0:T(8,128)S(1)}, f32[560,128]{1,0:T(8,128)S(1)}, u32[]{:S(2)}, u32[]{:S(2)}) collective-permute-start(f32[560,128]{1,0:T(8,128)S(1)} %pad_maximum_fusion), channel_id=1, source_target_pairs={{0,1},{1,0},{2,3},{3,2},{4,5},{5,4},{6,7},{7,6},{8,9},{9,8},{10,11... | collective-permute-start | bytes 860168 | tf_op jit(solution)/shard_map/ppermute | solution.py:725
  29.5 1.7 %collective-permute-start.8 = (f32[696,128]{1,0:T(8,128)S(1)}, f32[696,128]{1,0:T(8,128)S(1)}, u32[]{:S(2)}, u32[]{:S(2)}) collective-permute-start(f32[696,128]{1,0:T(8,128)S(1)} %constant_dynamic-update-slice_fusion.w0), channel_id=1, source_target_pairs={{0,1},{1,0},{2,3},{3,2},{4,5},{5,4},{6,7},{7,6},{8,9},{9,8},{10,11... | collective-permute-start | bytes 1069064 | tf_op jit(solution)/shard_map/ppermute | solution.py:725
  36.3 10.5 %collective-permute-start.10 = (f32[48,128]{1,0:T(8,128)S(1)}, f32[48,128]{1,0:T(8,128)S(1)}, u32[]{:S(2)}, u32[]{:S(2)}) collective-permute-start(f32[48,128]{1,0:T(8,128)S(1)} %get-tuple-element.46), channel_id=1, source_target_pairs={{4,8},{5,9},{6,10},{7,11},{8,4},{9,5},{10,6},{11,7},{12,16},{13,17... | collective-permute-start | bytes 73736 | tf_op jit(solution)/shard_map/ppermute | solution.py:725
  37.0 9.9 %collective-permute-start.9 = (f32[48,128]{1,0:T(8,128)S(1)}, f32[48,128]{1,0:T(8,128)S(1)}, u32[]{:S(2)}, u32[]{:S(2)}) collective-permute-start(f32[48,128]{1,0:T(8,128)S(1)} %get-tuple-element.46), channel_id=1, source_target_pairs={{0,4},{1,5},{2,6},{3,7},{4,0},{5,1},{6,2},{7,3},{8,12},{9,13},{10,... | collective-permute-start | bytes 73736 | tf_op jit(solution)/shard_map/ppermute | solution.py:725
  43.7 11.4 %all-to-all-start = ((f32[32,8,128]{2,1,0:T(8,128)}), f32[32,8,128]{2,1,0:T(8,128)S(1)}, u32[]{:S(2)}, u32[]{:S(2)}) async-start(f32[32,8,128]{2,1,0:T(8,128)} %get-tuple-element.47), calls=%async_computation | async-start | bytes 262144 | tf_op jit(solution)/shard_map/all_to_all | solution.py:798
  46.9 5.3 %collective-permute-start.11 = (f32[144,128]{1,0:T(8,128)S(1)}, f32[144,128]{1,0:T(8,128)S(1)}, u32[]{:S(2)}, u32[]{:S(2)}) collective-permute-start(f32[144,128]{1,0:T(8,128)S(1)} %pad_maximum_fusion.2), channel_id=1, source_target_pairs={{0,2},{1,3},{2,0},{3,1},{4,6},{5,7},{6,4},{7,5},{8,10},{9,11},{10,... | collective-permute-start | bytes 221192 | tf_op jit(solution)/shard_map/ppermute | solution.py:725
  52.1 1.4 %collective-permute-start.12 = (f32[288,128]{1,0:T(8,128)S(1)}, f32[288,128]{1,0:T(8,128)S(1)}, u32[]{:S(2)}, u32[]{:S(2)}) collective-permute-start(f32[288,128]{1,0:T(8,128)S(1)} %constant_dynamic-update-slice_fusion.7.q0), channel_id=1, source_target_pairs={{0,1},{1,0},{2,3},{3,2},{4,5},{5,4},{6,7},{7,6},{8,9},{9,8},{10,11... | collective-permute-start | bytes 442376 | tf_op jit(solution)/shard_map/ppermute | solution.py:725
  62.4 4.1 %collective-permute-start.14 = (f32[48,128]{1,0:T(8,128)S(1)}, f32[48,128]{1,0:T(8,128)S(1)}, u32[]{:S(2)}, u32[]{:S(2)}) collective-permute-start(f32[48,128]{1,0:T(8,128)S(1)} %get-tuple-element.48), channel_id=1, source_target_pairs={{4,8},{5,9},{6,10},{7,11},{8,4},{9,5},{10,6},{11,7},{12,16},{13,17... | collective-permute-start | bytes 73736 | tf_op jit(solution)/shard_map/ppermute | solution.py:725
  63.0 5.2 %collective-permute-start.13 = (f32[48,128]{1,0:T(8,128)S(1)}, f32[48,128]{1,0:T(8,128)S(1)}, u32[]{:S(2)}, u32[]{:S(2)}) collective-permute-start(f32[48,128]{1,0:T(8,128)S(1)} %get-tuple-element.48), channel_id=1, source_target_pairs={{0,4},{1,5},{2,6},{3,7},{4,0},{5,1},{6,2},{7,3},{8,12},{9,13},{10,... | collective-permute-start | bytes 73736 | tf_op jit(solution)/shard_map/ppermute | solution.py:725
  68.3 4.4 %collective-permute-start.15 = (f32[144,128]{1,0:T(8,128)S(1)}, f32[144,128]{1,0:T(8,128)S(1)}, u32[]{:S(2)}, u32[]{:S(2)}) collective-permute-start(f32[144,128]{1,0:T(8,128)S(1)} %pad_maximum_fusion.3), channel_id=1, source_target_pairs={{0,2},{1,3},{2,0},{3,1},{4,6},{5,7},{6,4},{7,5},{8,10},{9,11},{10,... | collective-permute-start | bytes 221192 | tf_op jit(solution)/shard_map/ppermute | solution.py:725
  72.6 1.4 %collective-permute-start.16 = (f32[288,128]{1,0:T(8,128)S(1)}, f32[288,128]{1,0:T(8,128)S(1)}, u32[]{:S(2)}, u32[]{:S(2)}) collective-permute-start(f32[288,128]{1,0:T(8,128)S(1)} %constant_dynamic-update-slice_fusion.11.q0), channel_id=1, source_target_pairs={{0,1},{1,0},{2,3},{3,2},{4,5},{5,4},{6,7},{7,6},{8,9},{9,8},{10,11... | collective-permute-start | bytes 442376 | tf_op jit(solution)/shard_map/ppermute | solution.py:725
  92.8 6.7 %collective-permute-start.18 = (f32[48,128]{1,0:T(8,128)S(1)}, f32[48,128]{1,0:T(8,128)S(1)}, u32[]{:S(2)}, u32[]{:S(2)}) collective-permute-start(f32[48,128]{1,0:T(8,128)S(1)} %get-tuple-element.56), channel_id=1, source_target_pairs={{4,8},{5,9},{6,10},{7,11},{8,4},{9,5},{10,6},{11,7},{12,16},{13,17... | collective-permute-start | bytes 73736 | tf_op jit(solution)/shard_map/ppermute | solution.py:725
  93.4 6.0 %collective-permute-start.17 = (f32[48,128]{1,0:T(8,128)S(1)}, f32[48,128]{1,0:T(8,128)S(1)}, u32[]{:S(2)}, u32[]{:S(2)}) collective-permute-start(f32[48,128]{1,0:T(8,128)S(1)} %get-tuple-element.56), channel_id=1, source_target_pairs={{0,4},{1,5},{2,6},{3,7},{4,0},{5,1},{6,2},{7,3},{8,12},{9,13},{10,... | collective-permute-start | bytes 73736 | tf_op jit(solution)/shard_map/ppermute | solution.py:725
  96.9 10.8 %all-to-all-start.2 = ((f32[32,8,128]{2,1,0:T(8,128)}), f32[32,8,128]{2,1,0:T(8,128)S(1)}, u32[]{:S(2)}, u32[]{:S(2)}) async-start(f32[32,8,128]{2,1,0:T(8,128)} %get-tuple-element.57), calls=%async_computation.2 | async-start | bytes 262144 | tf_op jit(solution)/shard_map/all_to_all | solution.py:798
  99.5 5.1 %collective-permute-start.19 = (f32[144,128]{1,0:T(8,128)S(1)}, f32[144,128]{1,0:T(8,128)S(1)}, u32[]{:S(2)}, u32[]{:S(2)}) collective-permute-start(f32[144,128]{1,0:T(8,128)S(1)} %pad_maximum_fusion.4), channel_id=1, source_target_pairs={{0,2},{1,3},{2,0},{3,1},{4,6},{5,7},{6,4},{7,5},{8,10},{9,11},{10,... | collective-permute-start | bytes 221192 | tf_op jit(solution)/shard_map/ppermute | solution.py:725
  104.5 1.4 %collective-permute-start.20 = (f32[288,128]{1,0:T(8,128)S(1)}, f32[288,128]{1,0:T(8,128)S(1)}, u32[]{:S(2)}, u32[]{:S(2)}) collective-permute-start(f32[288,128]{1,0:T(8,128)S(1)} %constant_dynamic-update-slice_fusion.15.q0), channel_id=1, source_target_pairs={{0,1},{1,0},{2,3},{3,2},{4,5},{5,4},{6,7},{7,6},{8,9},{9,8},{10,11... | collective-permute-start | bytes 442376 | tf_op jit(solution)/shard_map/ppermute | solution.py:725

commit v4 on v3

--- a/solution.py
+++ b/solution.py
@@ -159,6 +159,7 @@
         self.halves = self.full + 1
         self.wide = self.halves * LANES
         self.t_rows = self.crs * self.halves
+        self.row_sums = -(-self.t_rows // 8) * 8
         self.sum_rows = -(-self.halves // 8) * 8
         self.tile_rows = self.modes * self.pad
         self.beside = LANES // max(self.spot, 1)
@@ -239,9 +240,9 @@
                 acc += rest_tile(w_refs, sh, rel, where, tile) * t_rest[rel]
             rests[where, tile] = acc
     group = lane_group(sh, (sh.pad, LANES)) if sh.spot else None
-    columns = []
+    lanes = lax.broadcasted_iota(jnp.int32, (sh.pad, LANES), 1)
+    parts = [jnp.zeros((sh.pad, LANES), F32)] * 3
     for mode in range(sh.modes):
-        parts = []
         for where in range(3):
             acc = jnp.zeros((sh.pad, LANES), F32)
             if sh.spot:
@@ -250,35 +251,36 @@
             for rel in range(sh.crs):
                 for h in range(sh.full):
                     acc += full_tile(w_refs, sh, rel, where, mode, h) * t_row[rel, h]
-            parts.append(
-                jnp.broadcast_to(jnp.sum(acc, axis=1, keepdims=True), (sh.pad, LANES))
+            parts[where] = jnp.where(
+                lanes == mode, jnp.sum(acc, axis=1, keepdims=True), parts[where]
             )
-        columns.append(jnp.concatenate(parts, axis=0))
-    return jnp.concatenate(columns, axis=1)
+    return jnp.concatenate(parts, axis=0)
 
 
 def lift(tr_ref, pt_ref, ep_ref, w_refs, t_ref, me, sh):
-    spread = coarse_back(w_refs, t_ref, me, sh)
-    far = select_dot(ep_ref[...], spread)
+    found = coarse_back(w_refs, t_ref, me, sh)
+    far = select_dot(ep_ref[...], found)
     out = jnp.zeros((sh.all_rows, LANES), F32)
     for mode in range(sh.modes):
-        own = spread[: sh.pad, mode * LANES : (mode + 1) * LANES]
+        own = jnp.broadcast_to(found[: sh.pad, mode : mode + 1], (sh.pad, LANES))
         own = jnp.concatenate([own] * sh.blocks, axis=0)
-        out += tr_ref[mode] * own - pt_ref[mode] * far[:, mode * LANES : (mode + 1) * LANES]
+        out += tr_ref[mode] * own - pt_ref[mode] * far[:, mode : mode + 1]
     return out
 
 
 def coarse_part(value, tr_ref, pt_ref, ept_ref, w_refs, me, sh, t_out):
     at = pl.multiple_of(me * sh.piece, 16)
-    own, far = [], []
+    lanes = lax.broadcasted_iota(jnp.int32, (sh.piece, LANES), 1)
+    own, far = [], jnp.zeros((sh.piece, LANES), F32)
     for mode in range(sh.modes):
         mine = tr_ref[mode, pl.ds(at, sh.piece), :] * value
         acc = mine[: sh.pad]
         for b in range(1, sh.piece_blocks):
             acc = acc + mine[b * sh.pad : (b + 1) * sh.pad]
-        own.append(acc)
-        far.append(pt_ref[mode, pl.ds(at, sh.piece), :] * value)
-    moved = select_dot(ept_ref[...], jnp.concatenate(far, axis=1))
+        own.append(jnp.sum(acc, axis=1, keepdims=True))
+        theirs = pt_ref[mode, pl.ds(at, sh.piece), :] * value
+        far = jnp.where(lanes == mode, jnp.sum(theirs, axis=1, keepdims=True), far)
+    moved = select_dot(ept_ref[...], far)
     sums, rests = {}, {}
     group = lane_group(sh, (sh.pad, LANES)) if sh.spot else None
     side = {}
@@ -287,12 +289,11 @@
         table[key] = table[key] + term if key in table else term
 
     for mode in range(sh.modes):
-        moved_k = moved[:, mode * LANES : (mode + 1) * LANES]
         for where in range(3):
-            part = -moved_k[where * sh.pad : (where + 1) * sh.pad]
+            weight = -moved[where * sh.pad : (where + 1) * sh.pad, mode : mode + 1]
             if where == 0:
-                part = part + own[mode]
-            weight = jnp.broadcast_to(jnp.sum(part, axis=1, keepdims=True), (sh.pad, LANES))
+                weight = weight + own[mode]
+            weight = jnp.broadcast_to(weight, (sh.pad, LANES))
             for rel in range(sh.crs):
                 for h in range(sh.full):
                     add(sums, (rel, h), full_tile(w_refs, sh, rel, where, mode, h) * weight)
@@ -354,9 +355,9 @@
     return rows_of(acc, sh)
 
 
-def sum_parcels(t_in_ref, sh):
+def sum_parcels(t_in_ref):
     acc = t_in_ref[0]
-    for i in range(1, sh.ndev):
+    for i in range(1, t_in_ref.shape[0]):
         acc = acc + t_in_ref[i]
     return acc
 
@@ -621,7 +622,7 @@
 
 def second_kernel(
     sh, place_ref, tr_ref, pt_ref, jump_ref, ep_ref, ept_ref, q0, q1, t_in, w0, w1, ops_hbm,
-    state_ref, tr0_out, q_out, t_out, ops_out, t_scr, sems,
+    state_ref, tr0_out, q_out, ops_out, t_scr, t_out, sems,
 ):
     copies = ops_copies(ops_hbm, ops_out, sems, sh)
     for copy in copies:
@@ -629,7 +630,7 @@
     me = place_ref[0]
     w_refs = (w0, w1)
     applied = select_dot(jump_ref[...], jnp.concatenate([q0[...], q1[...]], axis=0))
-    tr0_out[...] = sum_parcels(t_in, sh)
+    tr0_out[...] = sum_parcels(t_in)
     back = lift(tr_ref, pt_ref, ep_ref, w_refs, tr0_out, me, sh)
     residual = tr_ref[sh.modes] - applied
     jump_r = pt_ref[sh.modes] - 2.0 * applied
@@ -639,7 +640,7 @@
     state_ref[2] = residual - back
     state_ref[3] = jump_d
     q = product(lanes_of(jump_d, sh).astype(BF16), ops_out, sh, copies)
-    q_out[...] = q
+    q_out[: sh.piece, :] = q
     coarse_part(2.0 * q, tr_ref, pt_ref, ept_ref, w_refs, me, sh, t_scr)
     mine = pl.ds(pl.multiple_of(me * sh.piece, 16), sh.piece)
     own_r = state_ref[0, mine, :]
@@ -653,15 +654,24 @@
         sh,
         t_out,
     )
-
-
-def square_kernel(sh, place_ref, jump_ref, q0, q1, t_in, applied_out, t_out):
-    me = place_ref[0]
-    applied_out[...] = select_dot(jump_ref[...], jnp.concatenate([q0[...], q1[...]], axis=0))
-    at = pl.multiple_of(me * sh.piece, 16)
-    mine = applied_out[pl.ds(at, sh.piece), :]
-    payload = jnp.where(sh.scalar_at(3), total(mine * mine), t_in[...])
-    for i in range(sh.ndev):
+    filler = jnp.zeros((sh.row_sums - sh.t_rows, LANES), F32)
+    q_out[sh.piece :, :] = jnp.concatenate([t_out[...], filler], axis=0) if (
+        sh.row_sums > sh.t_rows
+    ) else t_out[...]
+
+
+def square_kernel(sh, place_ref, jump_ref, q0, q1, applied_out, t_out):
+    span = sh.piece + sh.row_sums
+    pieces, sums = [], jnp.zeros((sh.t_rows, LANES), F32)
+    for ref in (q0, q1):
+        for i in range(3 * sh.crs // 2):
+            pieces.append(ref[i * span : i * span + sh.piece, :])
+            if i % 3 == 0:
+                sums = sums + ref[i * span + sh.piece : i * span + sh.piece + sh.t_rows, :]
+    applied = select_dot(jump_ref[...], jnp.concatenate(pieces, axis=0))
+    applied_out[...] = applied
+    payload = jnp.where(sh.scalar_at(3), total(applied * applied), sums)
+    for i in range(t_out.shape[0]):
         t_out[i] = payload
 
 
@@ -672,7 +682,7 @@
 ):
     me = place_ref[0]
     w_refs = (w0, w1)
-    sums = sum_parcels(t_in, sh)
+    sums = sum_parcels(t_in)
     tr0 = tr0_ref[...]
     d_a, r_a, r_r, a_a = (pick(sums, sh, i) for i in range(4))
     rw0 = r_r - norm2(tr0, sh)
@@ -702,7 +712,7 @@
     lam_out, p_out, t_scr,
 ):
     me = place_ref[0]
-    sums = sum_parcels(t_in, sh)
+    sums = sum_parcels(t_in)
     tr1 = tr1_ref[...]
     alpha = pick(tr1, sh, 0) / pick(sums, sh, 0)
     t_scr[...] = tr1 - alpha * sums
@@ -863,19 +873,20 @@
     q0, q1 = spread_pieces(q)
     t_in = exchange(t_part)
 
-    state0, tr0, q, t_part, ops_vmem = call(
+    state0, tr0, q, ops_vmem = call(
         second_kernel, "vvvvvvvvvvh",
-        [("v", stack(4), F32), t_shape, q_shape, t_shape, ops_kept],
-        [t_scratch, pltpu.SemaphoreType.DMA((ops_sems,))],
+        [("v", stack(4), F32), t_shape, ("v", (sh.piece + sh.row_sums, LANES), F32), ops_kept],
+        [t_scratch, t_scratch, pltpu.SemaphoreType.DMA((ops_sems,))],
         traces, far_traces, jumper, far_pick, far_put, q0, q1, t_in, w0, w1, ops,
         name="second", cost=long,
     )
     q0, q1 = spread_pieces(q)
+    sub_parcels = ("v", (lax.axis_size("sub"), sh.t_rows, LANES), F32)
     applied, t_part = call(
-        square_kernel, "vvvv", [("v", rows, F32), parcels], [],
-        jumper, q0, q1, t_part, name="square", cost=2_000_000,
-    )
-    t_in = exchange(t_part)
+        square_kernel, "vvv", [("v", rows, F32), sub_parcels], [],
+        jumper, q0, q1, name="square", cost=2_000_000,
+    )
+    t_in = lax.all_to_all(t_part, "sub", 0, 0)
 
     state1, tr1, q, t_part = call(
         third_kernel, "vvvvvvvvvvvv",
@@ -906,6 +917,7 @@
     )
     fits = whole_blocks and args[2].shape[1] % LANES + 8 <= LANES
     fits = fits and sub_num & (sub_num - 1) == 0
+    fits = fits and args[1].shape[1] <= LANES
     if fits and crs_num % 2 == 0 and crs_num & (crs_num - 1) == 0 and sub_num % 2 == 0:
         return local(*args)
     return plain(*args)

time: 110 us -> 108 us (0.982)
  no operation moved by 1% of the time
where the time goes in v4:
time: 108 us
  starting transfers between devices  37.4 us (35%)
  Pallas kernels  32.3 us (30%)
  waiting for transfers between devices  25.1 us (23%)
  blocking collectives  11.4 us (11%)
    pallas_call x9, Pallas kernels, call(): pl.pallas_call(functools.partial(kernel, sh), out_shape=[pltpu.VMEM(s, t)...  32.3 us
    ppermute x21, starting transfers between devices, permute(): return lax.ppermute(value, AXES, pairs)  31.6 us
    ppermute x21, waiting for transfers between devices, permute(): return lax.ppermute(value, AXES, pairs)  21.8 us
    all_to_all x1, blocking collectives, local(): t_in = lax.all_to_all(t_part, 'sub', 0, 0)  11.4 us
    all_to_all x2, starting transfers between devices, exchange(): return lax.all_to_all(parcel, AXES, 0, 0)  5.73 us
    all_to_all x2, waiting for transfers between devices, exchange(): return lax.all_to_all(parcel, AXES, 0, 0)  3.3 us
  transfers between devices with their start and end apart: 23, of which 12 were waited for; matrix products, arithmetic and copies ran while one was open for 0% of the time, Pallas kernels for 8%

profile of v4, /device:TPU:0, one launch (start us, length us, event | category | flops | bytes accessed | tf_op | source)
XLA Modules:
  0.0 108.1 jit_solution(4766626639313285371)
XLA Ops:
  1.4 1.6 %start.1.after_ref = f32[8,128]{1,0:T(8,128)S(1)} custom-call(s32[2]{0:T(128)S(1)} %pad_add_fusion.place_ref, s32[12]{0:T(128)S(1)} %copy-done.1, f32[1,72]{1,0:T(1,128)} %bitcast.8, f32[72,144]{1,0:T(8,128)} %factor_hbm.3), custom_call_target="tpu_custom_call" | custom-call | bytes 100000 | tf_op jit(solution)/shard_map/start/pallas_call | solution.py:781
  3.0 3.0 %collective-permute-start = (f32[8,128]{1,0:T(8,128)S(1)}, f32[8,128]{1,0:T(8,128)S(1)}, u32[]{:S(2)}, u32[]{:S(2)}) collective-permute-start(f32[8,128]{1,0:T(8,128)S(1)} %start.1.after_ref), channel_id=1, source_target_pairs={{0,4},{1,5},{2,6},{3,7},{4,0},{5,1},{6,2},{7,3},{8,12},{9,13},{10,... | collective-permute-start | bytes 12296 | tf_op jit(solution)/shard_map/ppermute | solution.py:735
  6.0 2.7 %pack.1 = (f32[7,192,128]{2,1,0:T(8,128)S(1)}, f32[400,128]{1,0:T(8,128)S(1)}, f32[400,128]{1,0:T(8,128)S(1)}, f32[112,128]{1,0:T(8,128)S(1)}) custom-call(s32[2]{0:T(128)S(1)} %pad_add_fusion.place_ref, s32[12]{0:T(128)S(1)} %copy-done.1, f32[12,6,1536]{2,1,0:T(8,128)} %traces_hbm.1, f32[12,1536]{1,0:T(8,128)} %rhs_hbm.1, s32[2,72]{1,0:T(2,128)} %send_hbm.1, ...), custom_call_target="tpu_custom_call" | custom-call | bytes 8000000 | tf_op jit(solution)/shard_map/pack/pallas_call | solution.py:781
  9.7 1.6 %collective-permute-start.5 = (f32[8,128]{1,0:T(8,128)S(1)}, f32[8,128]{1,0:T(8,128)S(1)}, u32[]{:S(2)}, u32[]{:S(2)}) collective-permute-start(f32[8,128]{1,0:T(8,128)S(1)} %add.14), channel_id=1, source_target_pairs={{0,8},{1,9},{2,10},{3,11},{4,12},{5,13},{6,14},{7,15},{8,0},{9,1},... | collective-permute-start | bytes 12296 | tf_op jit(solution)/shard_map/ppermute | solution.py:735
  11.2 1.5 %collective-permute-start.4 = (f32[112,128]{1,0:T(8,128)S(1)}, f32[112,128]{1,0:T(8,128)S(1)}, u32[]{:S(2)}, u32[]{:S(2)}) collective-permute-start(f32[112,128]{1,0:T(8,128)S(1)} %get-tuple-element.41), channel_id=1, source_target_pairs={{0,2},{1,3},{2,0},{3,1},{4,6},{5,7},{6,4},{7,5},{8,10},{9,11},{10,... | collective-permute-start | bytes 172040 | tf_op jit(solution)/shard_map/ppermute | solution.py:735
  13.3 2.6 %collective-permute-start.6 = (f32[8,128]{1,0:T(8,128)S(1)}, f32[8,128]{1,0:T(8,128)S(1)}, u32[]{:S(2)}, u32[]{:S(2)}) collective-permute-start(f32[8,128]{1,0:T(8,128)S(1)} %add.15.sum_ref), channel_id=1, source_target_pairs={{0,16},{1,17},{2,18},{3,19},{4,20},{5,21},{6,22},{7,23},{8,24},{9,... | collective-permute-start | bytes 12296 | tf_op jit(solution)/shard_map/ppermute | solution.py:735
  16.5 5.7 %load.1 = (bf16[4608,1536]{1,0:T(8,128)(2,1)S(1)}, f32[8,128]{1,0:T(8,128)S(1)}) custom-call(s32[2]{0:T(128)S(1)} %pad_add_fusion.place_ref, bf16[4608,1536]{1,0:T(8,128)(2,1)} %bitcast.6, f32[8,128]{1,0:T(8,128)S(1)} %add.15.sum_ref), custom_call_target="tpu_custom_call" | custom-call | bytes 14155776 | tf_op jit(solution)/shard_map/load/pallas_call | solution.py:781
  22.3 1.6 %collective-permute-start.7 = (f32[232,128]{1,0:T(8,128)S(1)}, f32[232,128]{1,0:T(8,128)S(1)}, u32[]{:S(2)}, u32[]{:S(2)}) collective-permute-start(f32[232,128]{1,0:T(8,128)S(1)} %pad_maximum_fusion.1), channel_id=1, source_target_pairs={{0,2},{1,3},{2,0},{3,1},{4,6},{5,7},{6,4},{7,5},{8,10},{9,11},{10,... | collective-permute-start | bytes 356360 | tf_op jit(solution)/shard_map/ppermute | solution.py:735
  24.1 3.2 %collective-permute-done.7 = f32[232,128]{1,0:T(8,128)S(1)} collective-permute-done((f32[232,128]{1,0:T(8,128)S(1)}, f32[232,128]{1,0:T(8,128)S(1)}, u32[]{:S(2)}, u32[]{:S(2)}) %collective-permute-start.7) | collective-permute-done | bytes 118816 | tf_op jit(solution)/shard_map/ppermute | solution.py:735
  27.3 2.2 %setup.1 = (f32[7,192,128]{2,1,0:T(8,128)S(1)}, f32[7,192,128]{2,1,0:T(8,128)S(1)}, bf16[192,576]{1,0:T(8,128)(2,1)S(1)}, bf16[192,48]{1,0:T(8,128)(2,1)S(1)}, bf16[48,48]{1,0:T(8,128)(2,1)S(1)}) custom-call(s32[2]{0:T(128)S(1)} %pad_add_fusion.place_ref, s32[12,12]{1,0:T(8,128)S(1)} %copy-done, f32[7,192,128]{2,1,0:T(8,128)S(1)} %get-tuple-element.30.fields_ref, ...), custom_call_target="tpu_custom_call" | custom-call | bytes 6000000 | tf_op jit(solution)/shard_map/setup/pallas_call | solution.py:781
  29.6 1.7 %collective-permute-done.8.w1 = f32[696,128]{1,0:T(8,128)S(1)} collective-permute-done((f32[696,128]{1,0:T(8,128)S(1)}, f32[696,128]{1,0:T(8,128)S(1)}, u32[]{:S(2)}, u32[]{:S(2)}) %collective-permute-start.8) | collective-permute-done | bytes 356384 | tf_op jit(solution)/shard_map/ppermute | solution.py:735
  31.2 5.0 %first.1 = (f32[192,128]{1,0:T(8,128)S(1)}, f32[48,128]{1,0:T(8,128)S(1)}, f32[32,8,128]{2,1,0:T(8,128)}) custom-call(s32[2]{0:T(128)S(1)} %pad_add_fusion.place_ref, f32[7,192,128]{2,1,0:T(8,128)S(1)} %get-tuple-element.36.tr_ref, f32[7,192,128]{2,1,0:T(8,128)S(1)} %get-tuple-element.37.pt_ref, bf16[192,48]{1,0:T(8,128)(2,1)S(1)} %get-tuple-element.39.ep_ref, ...), custom_call_target="tpu_custom_call" | custom-call | bytes 14155776 | tf_op jit(solution)/shard_map/first/pallas_call | solution.py:781
  36.9 6.7 %collective-permute-start.9 = (f32[48,128]{1,0:T(8,128)S(1)}, f32[48,128]{1,0:T(8,128)S(1)}, u32[]{:S(2)}, u32[]{:S(2)}) collective-permute-start(f32[48,128]{1,0:T(8,128)S(1)} %get-tuple-element.45), channel_id=1, source_target_pairs={{0,4},{1,5},{2,6},{3,7},{4,0},{5,1},{6,2},{7,3},{8,12},{9,13},{10,... | collective-permute-start | bytes 73736 | tf_op jit(solution)/shard_map/ppermute | solution.py:735
  43.5 3.2 %all-to-all-start = ((f32[32,8,128]{2,1,0:T(8,128)}), f32[32,8,128]{2,1,0:T(8,128)S(1)}, u32[]{:S(2)}, u32[]{:S(2)}) async-start(f32[32,8,128]{2,1,0:T(8,128)} %get-tuple-element.46), calls=%async_computation | async-start | bytes 262144 | tf_op jit(solution)/shard_map/all_to_all | solution.py:808
  46.7 1.8 %collective-permute-start.11 = (f32[144,128]{1,0:T(8,128)S(1)}, f32[144,128]{1,0:T(8,128)S(1)}, u32[]{:S(2)}, u32[]{:S(2)}) collective-permute-start(f32[144,128]{1,0:T(8,128)S(1)} %pad_maximum_fusion.3), channel_id=1, source_target_pairs={{0,2},{1,3},{2,0},{3,1},{4,6},{5,7},{6,4},{7,5},{8,10},{9,11},{10,... | collective-permute-start | bytes 221192 | tf_op jit(solution)/shard_map/ppermute | solution.py:735
  48.6 3.4 %collective-permute-done.11 = f32[144,128]{1,0:T(8,128)S(1)} collective-permute-done((f32[144,128]{1,0:T(8,128)S(1)}, f32[144,128]{1,0:T(8,128)S(1)}, u32[]{:S(2)}, u32[]{:S(2)}) %collective-permute-start.11) | collective-permute-done | bytes 73760 | tf_op jit(solution)/shard_map/ppermute | solution.py:735
  52.0 1.4 %collective-permute-done.12.q1 = f32[288,128]{1,0:T(8,128)S(1)} collective-permute-done((f32[288,128]{1,0:T(8,128)S(1)}, f32[288,128]{1,0:T(8,128)S(1)}, u32[]{:S(2)}, u32[]{:S(2)}) %collective-permute-start.12) | collective-permute-done | bytes 147488 | tf_op jit(solution)/shard_map/ppermute | solution.py:735
  53.4 1.6 %all-to-all-done.t_in = f32[32,8,128]{2,1,0:T(8,128)S(1)} async-done(((f32[32,8,128]{2,1,0:T(8,128)}), f32[32,8,128]{2,1,0:T(8,128)S(1)}, u32[]{:S(2)}, u32[]{:S(2)}) %all-to-all-start) | async-done | bytes 131104 | tf_op jit(solution)/shard_map/all_to_all | solution.py:808
  54.9 6.9 %second.1 = (f32[4,192,128]{2,1,0:T(8,128)S(1)}, f32[8,128]{1,0:T(8,128)S(1)}, f32[56,128]{1,0:T(8,128)S(1)}, bf16[4608,1536]{1,0:T(8,128)(2,1)S(1)}) custom-call(s32[2]{0:T(128)S(1)} %pad_add_fusion.place_ref, f32[7,192,128]{2,1,0:T(8,128)S(1)} %get-tuple-element.36.tr_ref, f32[7,192,128]{2,1,0:T(8,128)S(1)} %get-tuple-element.37.pt_ref, ...), custom_call_target="tpu_custom_call" | custom-call | bytes 14155776 | tf_op jit(solution)/shard_map/second/pallas_call | solution.py:781
  62.5 3.4 %collective-permute-start.13 = (f32[56,128]{1,0:T(8,128)S(1)}, f32[56,128]{1,0:T(8,128)S(1)}, u32[]{:S(2)}, u32[]{:S(2)}) collective-permute-start(f32[56,128]{1,0:T(8,128)S(1)} %get-tuple-element.47), channel_id=1, source_target_pairs={{0,4},{1,5},{2,6},{3,7},{4,0},{5,1},{6,2},{7,3},{8,12},{9,13},{10,... | collective-permute-start | bytes 86024 | tf_op jit(solution)/shard_map/ppermute | solution.py:735
  66.0 1.8 %collective-permute-done.13 = f32[56,128]{1,0:T(8,128)S(1)} collective-permute-done((f32[56,128]{1,0:T(8,128)S(1)}, f32[56,128]{1,0:T(8,128)S(1)}, u32[]{:S(2)}, u32[]{:S(2)}) %collective-permute-start.13) | collective-permute-done | bytes 28704 | tf_op jit(solution)/shard_map/ppermute | solution.py:735
  68.7 3.6 %collective-permute-done.15 = f32[168,128]{1,0:T(8,128)S(1)} collective-permute-done((f32[168,128]{1,0:T(8,128)S(1)}, f32[168,128]{1,0:T(8,128)S(1)}, u32[]{:S(2)}, u32[]{:S(2)}) %collective-permute-start.15) | collective-permute-done | bytes 86048 | tf_op jit(solution)/shard_map/ppermute | solution.py:735
  72.4 1.4 %collective-permute-done.16.q1 = f32[336,128]{1,0:T(8,128)S(1)} collective-permute-done((f32[336,128]{1,0:T(8,128)S(1)}, f32[336,128]{1,0:T(8,128)S(1)}, u32[]{:S(2)}, u32[]{:S(2)}) %collective-permute-start.16) | collective-permute-done | bytes 172064 | tf_op jit(solution)/shard_map/ppermute | solution.py:735
  74.8 11.4 %all_to_all.15.t_in = f32[8,8,128]{2,1,0:T(8,128)S(1)} all-to-all(f32[8,8,128]{2,1,0:T(8,128)S(1)} %get-tuple-element.49), channel_id=1, replica_groups=mesh['sub'=8,'crs'=4] {'sub'}, dimensions={0} | all-to-all | bytes 65536 | tf_op jit(solution)/shard_map/all_to_all | solution.py:889
  86.2 5.2 %third.1 = (f32[3,192,128]{2,1,0:T(8,128)S(1)}, f32[8,128]{1,0:T(8,128)S(1)}, f32[48,128]{1,0:T(8,128)S(1)}, f32[32,8,128]{2,1,0:T(8,128)}) custom-call(s32[2]{0:T(128)S(1)} %pad_add_fusion.place_ref, f32[7,192,128]{2,1,0:T(8,128)S(1)} %get-tuple-element.36.tr_ref, f32[7,192,128]{2,1,0:T(8,128)S(1)} %get-tuple-element.37.pt_ref, ...), custom_call_target="tpu_custom_call" | custom-call | bytes 14155776 | tf_op jit(solution)/shard_map/third/pallas_call | solution.py:781
  92.1 3.2 %collective-permute-start.17 = (f32[48,128]{1,0:T(8,128)S(1)}, f32[48,128]{1,0:T(8,128)S(1)}, u32[]{:S(2)}, u32[]{:S(2)}) collective-permute-start(f32[48,128]{1,0:T(8,128)S(1)} %get-tuple-element.54), channel_id=1, source_target_pairs={{0,4},{1,5},{2,6},{3,7},{4,0},{5,1},{6,2},{7,3},{8,12},{9,13},{10,... | collective-permute-start | bytes 73736 | tf_op jit(solution)/shard_map/ppermute | solution.py:735
  95.3 2.6 %all-to-all-start.2 = ((f32[32,8,128]{2,1,0:T(8,128)}), f32[32,8,128]{2,1,0:T(8,128)S(1)}, u32[]{:S(2)}, u32[]{:S(2)}) async-start(f32[32,8,128]{2,1,0:T(8,128)} %get-tuple-element.55), calls=%async_computation.2 | async-start | bytes 262144 | tf_op jit(solution)/shard_map/all_to_all | solution.py:808
  97.9 1.7 %collective-permute-start.19 = (f32[144,128]{1,0:T(8,128)S(1)}, f32[144,128]{1,0:T(8,128)S(1)}, u32[]{:S(2)}, u32[]{:S(2)}) collective-permute-start(f32[144,128]{1,0:T(8,128)S(1)} %pad_maximum_fusion.4), channel_id=1, source_target_pairs={{0,2},{1,3},{2,0},{3,1},{4,6},{5,7},{6,4},{7,5},{8,10},{9,11},{10,... | collective-permute-start | bytes 221192 | tf_op jit(solution)/shard_map/ppermute | solution.py:735
  99.6 3.4 %collective-permute-done.19 = f32[144,128]{1,0:T(8,128)S(1)} collective-permute-done((f32[144,128]{1,0:T(8,128)S(1)}, f32[144,128]{1,0:T(8,128)S(1)}, u32[]{:S(2)}, u32[]{:S(2)}) %collective-permute-start.19) | collective-permute-done | bytes 73760 | tf_op jit(solution)/shard_map/ppermute | solution.py:735
  102.9 1.4 %collective-permute-done.20.q1 = f32[288,128]{1,0:T(8,128)S(1)} collective-permute-done((f32[288,128]{1,0:T(8,128)S(1)}, f32[288,128]{1,0:T(8,128)S(1)}, u32[]{:S(2)}, u32[]{:S(2)}) %collective-permute-start.20) | collective-permute-done | bytes 147488 | tf_op jit(solution)/shard_map/ppermute | solution.py:735
  104.3 1.8 %all-to-all-done.2.t_in = f32[32,8,128]{2,1,0:T(8,128)S(1)} async-done(((f32[32,8,128]{2,1,0:T(8,128)}), f32[32,8,128]{2,1,0:T(8,128)S(1)}, u32[]{:S(2)}, u32[]{:S(2)}) %all-to-all-start.2) | async-done | bytes 131104 | tf_op jit(solution)/shard_map/all_to_all | solution.py:808
  106.1 2.0 %last.1 = (f32[12,1536]{1,0:T(8,128)}, f32[12,1536]{1,0:T(8,128)}) custom-call(s32[2]{0:T(128)S(1)} %pad_add_fusion.place_ref, f32[7,192,128]{2,1,0:T(8,128)S(1)} %get-tuple-element.36.tr_ref, f32[7,192,128]{2,1,0:T(8,128)S(1)} %get-tuple-element.37.pt_ref, bf16[192,576]{1,0:T(8,128)(2,1)S(1)} %get-tuple-element.38.jump_ref, ...), custom_call_target="tpu_custom_call" | custom-call | bytes 4000000 | tf_op jit(solution)/shard_map/last/pallas_call | solution.py:781
  (59 shorter events, 7.0 us)
Async XLA Ops:
  0.6 26.7 %copy-start = (s32[12,12]{1,0:T(8,128)S(1)}, s32[12,12]{1,0:T(8,128)}, u32[]{:S(2)}) copy-start(s32[12,12]{1,0:T(8,128)} %partner_ref.1) | copy-start | bytes 1732
  0.7 0.7 copy-start.1
  3.0 5.8 %collective-permute-start = (f32[8,128]{1,0:T(8,128)S(1)}, f32[8,128]{1,0:T(8,128)S(1)}, u32[]{:S(2)}, u32[]{:S(2)}) collective-permute-start(f32[8,128]{1,0:T(8,128)S(1)} %start.1.after_ref), channel_id=1, source_target_pairs={{0,4},{1,5},{2,6},{3,7},{4,0},{5,1},{6,2},{7,3},{8,12},{9,13},{10,... | collective-permute-start | bytes 12296 | tf_op jit(solution)/shard_map/ppermute | solution.py:735
  8.8 13.5 %collective-permute-start.1 = (f32[400,128]{1,0:T(8,128)S(1)}, f32[400,128]{1,0:T(8,128)S(1)}, u32[]{:S(2)}, u32[]{:S(2)}) collective-permute-start(f32[400,128]{1,0:T(8,128)S(1)} %get-tuple-element.34), channel_id=1, source_target_pairs={{0,4},{1,5},{2,6},{3,7},{4,0},{5,1},{6,2},{7,3},{8,12},{9,13},{10,... | collective-permute-start | bytes 614408 | tf_op jit(solution)/shard_map/ppermute | solution.py:735
  9.7 3.6 %collective-permute-start.5 = (f32[8,128]{1,0:T(8,128)S(1)}, f32[8,128]{1,0:T(8,128)S(1)}, u32[]{:S(2)}, u32[]{:S(2)}) collective-permute-start(f32[8,128]{1,0:T(8,128)S(1)} %add.14), channel_id=1, source_target_pairs={{0,8},{1,9},{2,10},{3,11},{4,12},{5,13},{6,14},{7,15},{8,0},{9,1},... | collective-permute-start | bytes 12296 | tf_op jit(solution)/shard_map/ppermute | solution.py:735
  11.2 12.8 %collective-permute-start.4 = (f32[112,128]{1,0:T(8,128)S(1)}, f32[112,128]{1,0:T(8,128)S(1)}, u32[]{:S(2)}, u32[]{:S(2)}) collective-permute-start(f32[112,128]{1,0:T(8,128)S(1)} %get-tuple-element.41), channel_id=1, source_target_pairs={{0,2},{1,3},{2,0},{3,1},{4,6},{5,7},{6,4},{7,5},{8,10},{9,11},{10,... | collective-permute-start | bytes 172040 | tf_op jit(solution)/shard_map/ppermute | solution.py:735
  13.3 9.0 %collective-permute-start.6 = (f32[8,128]{1,0:T(8,128)S(1)}, f32[8,128]{1,0:T(8,128)S(1)}, u32[]{:S(2)}, u32[]{:S(2)}) collective-permute-start(f32[8,128]{1,0:T(8,128)S(1)} %add.15.sum_ref), channel_id=1, source_target_pairs={{0,16},{1,17},{2,18},{3,19},{4,20},{5,21},{6,22},{7,23},{8,24},{9,... | collective-permute-start | bytes 12296 | tf_op jit(solution)/shard_map/ppermute | solution.py:735
  15.9 6.4 %collective-permute-start.2 = (f32[400,128]{1,0:T(8,128)S(1)}, f32[400,128]{1,0:T(8,128)S(1)}, u32[]{:S(2)}, u32[]{:S(2)}) collective-permute-start(f32[400,128]{1,0:T(8,128)S(1)} %get-tuple-element.35), channel_id=1, source_target_pairs={{4,8},{5,9},{6,10},{7,11},{8,4},{9,5},{10,6},{11,7},{12,16},{13,17... | collective-permute-start | bytes 614408 | tf_op jit(solution)/shard_map/ppermute | solution.py:735
  22.3 4.9 %collective-permute-start.7 = (f32[232,128]{1,0:T(8,128)S(1)}, f32[232,128]{1,0:T(8,128)S(1)}, u32[]{:S(2)}, u32[]{:S(2)}) collective-permute-start(f32[232,128]{1,0:T(8,128)S(1)} %pad_maximum_fusion.1), channel_id=1, source_target_pairs={{0,2},{1,3},{2,0},{3,1},{4,6},{5,7},{6,4},{7,5},{8,10},{9,11},{10,... | collective-permute-start | bytes 356360 | tf_op jit(solution)/shard_map/ppermute | solution.py:735
  24.0 3.3 %collective-permute-start.3 = (f32[560,128]{1,0:T(8,128)S(1)}, f32[560,128]{1,0:T(8,128)S(1)}, u32[]{:S(2)}, u32[]{:S(2)}) collective-permute-start(f32[560,128]{1,0:T(8,128)S(1)} %pad_maximum_fusion), channel_id=1, source_target_pairs={{0,1},{1,0},{2,3},{3,2},{4,5},{5,4},{6,7},{7,6},{8,9},{9,8},{10,11... | collective-permute-start | bytes 860168 | tf_op jit(solution)/shard_map/ppermute | solution.py:735
  29.5 1.7 %collective-permute-start.8 = (f32[696,128]{1,0:T(8,128)S(1)}, f32[696,128]{1,0:T(8,128)S(1)}, u32[]{:S(2)}, u32[]{:S(2)}) collective-permute-start(f32[696,128]{1,0:T(8,128)S(1)} %constant_dynamic-update-slice_fusion.w0), channel_id=1, source_target_pairs={{0,1},{1,0},{2,3},{3,2},{4,5},{5,4},{6,7},{7,6},{8,9},{9,8},{10,11... | collective-permute-start | bytes 1069064 | tf_op jit(solution)/shard_map/ppermute | solution.py:735
  36.2 10.5 %collective-permute-start.10 = (f32[48,128]{1,0:T(8,128)S(1)}, f32[48,128]{1,0:T(8,128)S(1)}, u32[]{:S(2)}, u32[]{:S(2)}) collective-permute-start(f32[48,128]{1,0:T(8,128)S(1)} %get-tuple-element.45), channel_id=1, source_target_pairs={{4,8},{5,9},{6,10},{7,11},{8,4},{9,5},{10,6},{11,7},{12,16},{13,17... | collective-permute-start | bytes 73736 | tf_op jit(solution)/shard_map/ppermute | solution.py:735
  36.9 9.9 %collective-permute-start.9 = (f32[48,128]{1,0:T(8,128)S(1)}, f32[48,128]{1,0:T(8,128)S(1)}, u32[]{:S(2)}, u32[]{:S(2)}) collective-permute-start(f32[48,128]{1,0:T(8,128)S(1)} %get-tuple-element.45), channel_id=1, source_target_pairs={{0,4},{1,5},{2,6},{3,7},{4,0},{5,1},{6,2},{7,3},{8,12},{9,13},{10,... | collective-permute-start | bytes 73736 | tf_op jit(solution)/shard_map/ppermute | solution.py:735
  43.5 11.4 %all-to-all-start = ((f32[32,8,128]{2,1,0:T(8,128)}), f32[32,8,128]{2,1,0:T(8,128)S(1)}, u32[]{:S(2)}, u32[]{:S(2)}) async-start(f32[32,8,128]{2,1,0:T(8,128)} %get-tuple-element.46), calls=%async_computation | async-start | bytes 262144 | tf_op jit(solution)/shard_map/all_to_all | solution.py:808
  46.7 5.3 %collective-permute-start.11 = (f32[144,128]{1,0:T(8,128)S(1)}, f32[144,128]{1,0:T(8,128)S(1)}, u32[]{:S(2)}, u32[]{:S(2)}) collective-permute-start(f32[144,128]{1,0:T(8,128)S(1)} %pad_maximum_fusion.3), channel_id=1, source_target_pairs={{0,2},{1,3},{2,0},{3,1},{4,6},{5,7},{6,4},{7,5},{8,10},{9,11},{10,... | collective-permute-start | bytes 221192 | tf_op jit(solution)/shard_map/ppermute | solution.py:735
  52.0 1.4 %collective-permute-start.12 = (f32[288,128]{1,0:T(8,128)S(1)}, f32[288,128]{1,0:T(8,128)S(1)}, u32[]{:S(2)}, u32[]{:S(2)}) collective-permute-start(f32[288,128]{1,0:T(8,128)S(1)} %constant_dynamic-update-slice_fusion.7.q0), channel_id=1, source_target_pairs={{0,1},{1,0},{2,3},{3,2},{4,5},{5,4},{6,7},{7,6},{8,9},{9,8},{10,11... | collective-permute-start | bytes 442376 | tf_op jit(solution)/shard_map/ppermute | solution.py:735
  61.8 4.1 %collective-permute-start.14 = (f32[56,128]{1,0:T(8,128)S(1)}, f32[56,128]{1,0:T(8,128)S(1)}, u32[]{:S(2)}, u32[]{:S(2)}) collective-permute-start(f32[56,128]{1,0:T(8,128)S(1)} %get-tuple-element.47), channel_id=1, source_target_pairs={{4,8},{5,9},{6,10},{7,11},{8,4},{9,5},{10,6},{11,7},{12,16},{13,17... | collective-permute-start | bytes 86024 | tf_op jit(solution)/shard_map/ppermute | solution.py:735
  62.5 5.3 %collective-permute-start.13 = (f32[56,128]{1,0:T(8,128)S(1)}, f32[56,128]{1,0:T(8,128)S(1)}, u32[]{:S(2)}, u32[]{:S(2)}) collective-permute-start(f32[56,128]{1,0:T(8,128)S(1)} %get-tuple-element.47), channel_id=1, source_target_pairs={{0,4},{1,5},{2,6},{3,7},{4,0},{5,1},{6,2},{7,3},{8,12},{9,13},{10,... | collective-permute-start | bytes 86024 | tf_op jit(solution)/shard_map/ppermute | solution.py:735
  67.8 4.5 %collective-permute-start.15 = (f32[168,128]{1,0:T(8,128)S(1)}, f32[168,128]{1,0:T(8,128)S(1)}, u32[]{:S(2)}, u32[]{:S(2)}) collective-permute-start(f32[168,128]{1,0:T(8,128)S(1)} %pad_maximum_fusion.2), channel_id=1, source_target_pairs={{0,2},{1,3},{2,0},{3,1},{4,6},{5,7},{6,4},{7,5},{8,10},{9,11},{10,... | collective-permute-start | bytes 258056 | tf_op jit(solution)/shard_map/ppermute | solution.py:735
  72.4 1.5 %collective-permute-start.16 = (f32[336,128]{1,0:T(8,128)S(1)}, f32[336,128]{1,0:T(8,128)S(1)}, u32[]{:S(2)}, u32[]{:S(2)}) collective-permute-start(f32[336,128]{1,0:T(8,128)S(1)} %constant_dynamic-update-slice_fusion.11.q0), channel_id=1, source_target_pairs={{0,1},{1,0},{2,3},{3,2},{4,5},{5,4},{6,7},{7,6},{8,9},{9,8},{10,11... | collective-permute-start | bytes 516104 | tf_op jit(solution)/shard_map/ppermute | solution.py:735
  91.4 6.4 %collective-permute-start.18 = (f32[48,128]{1,0:T(8,128)S(1)}, f32[48,128]{1,0:T(8,128)S(1)}, u32[]{:S(2)}, u32[]{:S(2)}) collective-permute-start(f32[48,128]{1,0:T(8,128)S(1)} %get-tuple-element.54), channel_id=1, source_target_pairs={{4,8},{5,9},{6,10},{7,11},{8,4},{9,5},{10,6},{11,7},{12,16},{13,17... | collective-permute-start | bytes 73736 | tf_op jit(solution)/shard_map/ppermute | solution.py:735
  92.1 5.8 %collective-permute-start.17 = (f32[48,128]{1,0:T(8,128)S(1)}, f32[48,128]{1,0:T(8,128)S(1)}, u32[]{:S(2)}, u32[]{:S(2)}) collective-permute-start(f32[48,128]{1,0:T(8,128)S(1)} %get-tuple-element.54), channel_id=1, source_target_pairs={{0,4},{1,5},{2,6},{3,7},{4,0},{5,1},{6,2},{7,3},{8,12},{9,13},{10,... | collective-permute-start | bytes 73736 | tf_op jit(solution)/shard_map/ppermute | solution.py:735
  95.3 10.8 %all-to-all-start.2 = ((f32[32,8,128]{2,1,0:T(8,128)}), f32[32,8,128]{2,1,0:T(8,128)S(1)}, u32[]{:S(2)}, u32[]{:S(2)}) async-start(f32[32,8,128]{2,1,0:T(8,128)} %get-tuple-element.55), calls=%async_computation.2 | async-start | bytes 262144 | tf_op jit(solution)/shard_map/all_to_all | solution.py:808
  97.9 5.1 %collective-permute-start.19 = (f32[144,128]{1,0:T(8,128)S(1)}, f32[144,128]{1,0:T(8,128)S(1)}, u32[]{:S(2)}, u32[]{:S(2)}) collective-permute-start(f32[144,128]{1,0:T(8,128)S(1)} %pad_maximum_fusion.4), channel_id=1, source_target_pairs={{0,2},{1,3},{2,0},{3,1},{4,6},{5,7},{6,4},{7,5},{8,10},{9,11},{10,... | collective-permute-start | bytes 221192 | tf_op jit(solution)/shard_map/ppermute | solution.py:735
  102.9 1.4 %collective-permute-start.20 = (f32[288,128]{1,0:T(8,128)S(1)}, f32[288,128]{1,0:T(8,128)S(1)}, u32[]{:S(2)}, u32[]{:S(2)}) collective-permute-start(f32[288,128]{1,0:T(8,128)S(1)} %constant_dynamic-update-slice_fusion.15.q0), channel_id=1, source_target_pairs={{0,1},{1,0},{2,3},{3,2},{4,5},{5,4},{6,7},{7,6},{8,9},{9,8},{10,11... | collective-permute-start | bytes 442376 | tf_op jit(solution)/shard_map/ppermute | solution.py:735
